TPU v7x, 128 devices: a whole 4x4x4 slice. The times are simulated.
128 devices in a mesh: dp: 2 (over core), ctx: 64 (over y, z, x).
Axes of the slice: x: 4, y: 4, z: 4, core: 2. Of those that a mesh axis runs over, the one named last changes fastest.
Arguments:
- queries: bfloat16 [16384, 1024], P(('dp', 'ctx')), may hold values from -5 to 5
- keys_values: bfloat16 [16384, 256], P(('dp', 'ctx')), may hold values from -4 to 4
- grad_out: bfloat16 [16384, 1024], P(('dp', 'ctx')), may hold values from -6 to 6
- placement: int32 [16384], P(('dp', 'ctx')), may hold values from 0 to 16383, as said below
- doc_lengths: int32 [2, 16], P('dp'), may hold values from 1 to 4224, 8192 in all within a row
Outputs:
- attn_out: bfloat16 [16384, 1024], P(('dp', 'ctx'))
- grad_queries: bfloat16 [16384, 1024], P(('dp', 'ctx'))
- grad_keys_values: bfloat16 [16384, 256], P(('dp', 'ctx'))
Inputs may be any that keep to these rules, and one draw needn't show every extreme that they name: `placement`: A permutation. Group position p lies on device p // 128 in dp+ctx order; the 128 loader rows of each device go exactly 1 to every device. `doc_lengths`: each row sums to 8192; its longest document has exactly 4224 tokens.
All inputs are finite; a program needn't handle non-finite values.
Results may differ from a plain program's by a relative error of at most 0.03.
Values may be sent and summed in bfloat16 or wider, within the bound.
No kernel may reach another device: no remote copies, remote signals or barrier semaphores. Data moves between devices by JAX's collectives and lax.ppermute only.
A program may use at most 192 MiB of HBM per device.

v0:
```python
import jax
import jax.numpy as jnp
from jax import lax
from jax.sharding import PartitionSpec as P

key_block = 512
masked_score = -1e30


def document_starts(positions, lengths):
    doc_ends = jnp.cumsum(lengths)
    earlier = jnp.where(doc_ends[None, :] <= positions[:, None], lengths[None, :], 0)
    return jnp.sum(earlier, axis=1)


def block_allowed(key_pos, query_pos, query_start):
    allowed = (key_pos[None, :] <= query_pos[:, None]) & (key_pos[None, :] >= query_start[:, None])
    return allowed[:, None, :]


def sweep(visit, carried, block_inputs, block_starts, query_low, query_high, nothing):

    def step(state, inputs):
        block_begin = inputs[0]
        rest = inputs[1:]
        key_pos = block_begin + jnp.arange(key_block, dtype=jnp.int32)
        needed = (block_begin <= query_high) & (block_begin + key_block - 1 >= query_low)

        def visit_block(inner):
            return visit(inner, rest, key_pos)

        def skip_block(inner):
            return (inner, nothing)

        return lax.cond(needed, visit_block, skip_block, state)

    return lax.scan(step, carried, (block_starts,) + tuple(block_inputs))


def on_device(queries, keys_values, grad_out, placement, doc_lengths):
    local_rows = queries.shape[0]
    query_width = queries.shape[1]
    pair_width = keys_values.shape[1]
    head_size = pair_width // 2
    head_count = query_width // head_size
    score_scale = head_size ** (-0.5)
    send_order = jnp.argsort(placement)
    slot_ids = placement[send_order] % local_rows
    sent_q = queries[send_order]
    sent_kv = keys_values[send_order]
    sent_g = grad_out[send_order]
    arrived_slots = lax.all_to_all(slot_ids, ("dp", "ctx"), split_axis=0, concat_axis=0, tiled=True)
    arrival = jnp.argsort(arrived_slots)
    got_q, got_kv, got_g = (
        lax.all_to_all(sent_q, ("dp", "ctx"), split_axis=0, concat_axis=0, tiled=True),
        lax.all_to_all(sent_kv, ("dp", "ctx"), split_axis=0, concat_axis=0, tiled=True),
        lax.all_to_all(sent_g, ("dp", "ctx"), split_axis=0, concat_axis=0, tiled=True),
    )
    group_q = got_q[arrival]
    group_kv = got_kv[arrival]
    group_g = got_g[arrival]
    position = lax.axis_index("ctx")
    query_pos = position * local_rows + jnp.arange(local_rows, dtype=jnp.int32)
    query_start = document_starts(query_pos, doc_lengths[0])
    query_low = query_start[0]
    query_high = query_pos[local_rows - 1]
    query_heads = group_q.reshape(local_rows, head_count, head_size)
    grad_heads = group_g.reshape(local_rows, head_count, head_size)
    key_window = lax.all_gather(group_kv, "ctx", axis=0, tiled=True)
    block_count = key_window.shape[0] // key_block
    key_blocks = key_window.reshape(block_count, key_block, pair_width)
    block_starts = key_block * jnp.arange(block_count, dtype=jnp.int32)
    no_scores = jnp.zeros((local_rows, head_count, key_block), jnp.float32)

    def row_stats(state, rest, key_pos):
        row_top, row_total = state
        key_rows = rest[0]
        scores = (
            jnp.einsum(
                "thd,kd->thk",
                query_heads,
                key_rows[:, :head_size],
                preferred_element_type=jnp.float32,
            )
            * score_scale
        )
        allowed = block_allowed(key_pos, query_pos, query_start)
        masked = jnp.where(allowed, scores, masked_score)
        new_top = jnp.maximum(row_top, jnp.max(masked, axis=2))
        kept = jnp.where(allowed, jnp.exp(masked - new_top[..., None]), 0.0)
        new_total = row_total * jnp.exp(row_top - new_top) + jnp.sum(kept, axis=2)
        return ((new_top, new_total), scores)

    start_top = jnp.full((local_rows, head_count), masked_score, jnp.float32)
    start_total = jnp.zeros((local_rows, head_count), jnp.float32)
    stats, score_blocks = sweep(
        row_stats,
        (start_top, start_total),
        (key_blocks,),
        block_starts,
        query_low,
        query_high,
        no_scores,
    )
    log_total = stats[0] + jnp.log(stats[1])

    def output_sum(out_sum, rest, key_pos):
        key_rows, scores = rest
        allowed = block_allowed(key_pos, query_pos, query_start)
        weights_full = jnp.where(allowed, jnp.exp(scores - log_total[..., None]), 0.0)
        weights_half = weights_full.astype(jnp.bfloat16)
        added = jnp.einsum(
            "thk,kd->thd", weights_half, key_rows[:, head_size:], preferred_element_type=jnp.float32
        )
        return (out_sum + added, weights_full)

    start_out = jnp.zeros((local_rows, head_count, head_size), jnp.float32)
    out_sum, weight_blocks = sweep(
        output_sum,
        start_out,
        (key_blocks, score_blocks),
        block_starts,
        query_low,
        query_high,
        no_scores,
    )
    attended = out_sum.astype(jnp.bfloat16)
    out_dot = jnp.sum(grad_heads.astype(jnp.float32) * attended.astype(jnp.float32), axis=2)

    def backward_block(grad_query_sum, rest, key_pos):
        key_rows, weights_full = rest
        weights_half = weights_full.astype(jnp.bfloat16)
        grad_weights = jnp.einsum(
            "thd,kd->thk", grad_heads, key_rows[:, head_size:], preferred_element_type=jnp.float32
        )
        grad_half = (weights_full * (grad_weights - out_dot[..., None]) * score_scale).astype(
            jnp.bfloat16
        )
        grad_query_sum = grad_query_sum + jnp.einsum(
            "thk,kd->thd", grad_half, key_rows[:, :head_size], preferred_element_type=jnp.float32
        )
        grad_keys = jnp.einsum(
            "thk,thd->kd", grad_half, query_heads, preferred_element_type=jnp.float32
        )
        grad_values = jnp.einsum(
            "thk,thd->kd", weights_half, grad_heads, preferred_element_type=jnp.float32
        )
        return (grad_query_sum, jnp.concatenate([grad_keys, grad_values], axis=1))

    no_terms = jnp.zeros((key_block, pair_width), jnp.float32)
    grad_query_sum, grad_pairs = sweep(
        backward_block,
        start_out,
        (key_blocks, weight_blocks),
        block_starts,
        query_low,
        query_high,
        no_terms,
    )
    grad_terms = grad_pairs.reshape(-1, pair_width)
    owned = lax.psum_scatter(grad_terms, "ctx", scatter_dimension=0, tiled=True)
    attended_rows = attended.reshape(local_rows, query_width)[arrived_slots]
    grad_query_rows = grad_query_sum.astype(jnp.bfloat16).reshape(local_rows, query_width)[
        arrived_slots
    ]
    grad_pair_rows = owned.astype(jnp.bfloat16)[arrived_slots]
    back_a, back_q, back_kv = (
        lax.all_to_all(attended_rows, ("dp", "ctx"), split_axis=0, concat_axis=0, tiled=True),
        lax.all_to_all(grad_query_rows, ("dp", "ctx"), split_axis=0, concat_axis=0, tiled=True),
        lax.all_to_all(grad_pair_rows, ("dp", "ctx"), split_axis=0, concat_axis=0, tiled=True),
    )
    sorted_rank = jnp.argsort(send_order)
    return (back_a[sorted_rank], back_q[sorted_rank], back_kv[sorted_rank])


def solution(mesh):
    in_specs = (
        P(("dp", "ctx"), None),
        P(("dp", "ctx"), None),
        P(("dp", "ctx"), None),
        P(("dp", "ctx")),
        P("dp", None),
    )
    out_specs = (P(("dp", "ctx"), None), P(("dp", "ctx"), None), P(("dp", "ctx"), None))
    return jax.shard_map(
        on_device, mesh=mesh, in_specs=in_specs, out_specs=out_specs, check_vma=False
    )
```

profile of v0, /device:TPU:1, one launch (start us, length us, event | category | flops | bytes accessed | tf_op | source)
XLA Modules:
  0.0 966.8 jit_solution(16851084107211700633)
XLA Ops:
  7.2 3.2 sort.45
  12.8 11.5 %all-to-all-start.1 = ((s32[128,1,1]{2,1,0:T(1,128)}), s32[128,1,1]{2,1,0:T(1,128)S(1)}, u32[]{:S(2)}, u32[]{:S(2)}) async-start(s32[128,1,1]{2,1,0:T(1,128)} %copy.88), calls=%async_computation.1 | async-start | bytes 131072 | tf_op jit(solution)/shard_map/all_to_all | solution.py:52
  27.8 6.0 all-to-all-done.1
  33.7 4.4 all-to-all-start
  40.5 2.5 sort.46
  43.1 4.5 all-to-all-done
  51.6 5.3 all-to-all-start.2
  59.5 8.7 all-to-all-done.2
  68.1 4.3 all-to-all-start.4
  74.9 8.5 all-to-all-done.4
  85.2 30.1 %all-gather.3.cloned.1.call-done = bf16[8192,256]{1,0:T(8,128)(2,1)} async-done(((bf16[128,256]{1,0:T(8,128)(2,1)}), bf16[8192,256]{1,0:T(8,128)(2,1)}) %all-gather.3.cloned.1.call-update) | async-done | bytes 4194320 | tf_op jit(solution)/shard_map/all_gather | solution.py:69
  115.3 125.3 %while.59 = (s32[]{:T(128)}, f32[128,8]{0,1:T(8,128)S(1)}, f32[128,8]{0,1:T(8,128)S(1)}, f32[16,128,8,512]{3,1,2,0:T(8,128)}, s32[16]{0:T(128)S(1)}, /*index=5*/...) while((s32[]{:T(128)}, f32[128,8]{0,1:T(8,128)S(1)}, ...), condition=%wide.region_9.10_spmd.clone, body=%wide.region_4.9_spmd.clone.sunk | while | flops 139135616 | bytes 26344784 | solution.py:37
  117.9 3.0 conditional.9
  241.5 128.6 %while.60 = (s32[]{:T(128)}, f32[128,8,128]{2,0,1:T(8,128)}, f32[16,128,8,512]{1,3,2,0:T(8,128)}, s32[16]{0:T(128)S(1)}, s32[]{:T(128)}, /*index=5*/s32[]{:T(128...) while((s32[]{:T(128)}, f32[128,8,128]{2,0,1:T(8,128)}, ...), condition=%wide.region_13.14_spmd.clone, body=%wide.region_10.13_spmd.clone.sunk | while | flops 137167488 | bytes 24989500 | solution.py:37
  244.0 6.8 conditional.10
  245.8 3.0 convolution_add_fusion
  371.4 64.9 %while.58 = (s32[]{:T(128)}, f32[128,8,128]{2,0,1:T(8,128)S(1)}, f32[16,512,256]{2,1,0:T(8,128)}, s32[16]{0:T(128)S(1)}, s32[]{:T(128)}, /*index=5*/s32[]{:T(128...) while((s32[]{:T(128)}, f32[128,8,128]{2,0,1:T(8,128)S(1)}, ...), condition=%wide.region_19.20_spmd, body=%wide.region_16.19_spmd.sunk | while | flops 539230208 | bytes 12588287 | solution.py:37
  373.9 6.2 conditional.8
  438.9 144.2 %all-to-all-start.5 = ((bf16[128,2,512]{2,1,0:T(2,128)(2,1)}), bf16[128,2,512]{2,1,0:T(2,128)(2,1)S(1)}, u32[]{:S(2)}, u32[]{:S(2)}) async-start(bf16[128,2,512]{2,1,0:T(2,128)(2,1)} %reshape.364), calls=%async_computation.5 | async-start | bytes 524288 | tf_op jit(solution)/shard_map/all_to_all | solution.py:169
  585.6 9.9 %all-to-all-done.5 = bf16[128,2,512]{2,1,0:T(2,128)(2,1)S(1)} async-done(((bf16[128,2,512]{2,1,0:T(2,128)(2,1)}), bf16[128,2,512]{2,1,0:T(2,128)(2,1)S(1)}, u32[]{:S(2)}, u32[]{:S(2)}) %all-to-all-start.5) | async-done | bytes 262176 | tf_op jit(solution)/shard_map/all_to_all | solution.py:169
  595.5 4.2 all-to-all-start.3
  602.3 292.0 %reduce-scatter.2.cloned.1.call-done = f32[128,256]{1,0:T(8,128)} async-done(((f32[8192,256]{1,0:T(8,128)}), f32[128,256]{1,0:T(8,128)}) %reduce-scatter.2.cloned.1.call-update) | async-done | bytes 131088 | tf_op jit(solution)/shard_map/reduce_scatter | solution.py:161
  897.4 51.5 %all-to-all-start.6 = ((bf16[128,2,128]{2,1,0:T(2,128)(2,1)}), bf16[128,2,128]{2,1,0:T(2,128)(2,1)S(1)}, u32[]{:S(2)}, u32[]{:S(2)}) async-start(bf16[128,2,128]{2,1,0:T(2,128)(2,1)} %reshape.366), calls=%async_computation.7 | async-start | bytes 131072 | tf_op jit(solution)/shard_map/all_to_all | solution.py:170
  952.7 5.7 all-to-all-done.6
  (473 shorter events, 264.2 us)
Async XLA Ops:
  7.2 41.9 %copy-start = (bf16[128,1024]{1,0:T(8,128)(2,1)S(1)}, bf16[128,1024]{1,0:T(8,128)(2,1)}, u32[]{:S(2)}) copy-start(bf16[128,1024]{1,0:T(8,128)(2,1)} %param.17) | copy-start | bytes 786436
  12.8 20.9 %all-to-all-start.1 = ((s32[128,1,1]{2,1,0:T(1,128)}), s32[128,1,1]{2,1,0:T(1,128)S(1)}, u32[]{:S(2)}, u32[]{:S(2)}) async-start(s32[128,1,1]{2,1,0:T(1,128)} %copy.88), calls=%async_computation.1 | async-start | bytes 131072 | tf_op jit(solution)/shard_map/all_to_all | solution.py:52
  33.7 13.8 %all-to-all-start = ((bf16[128,2,128]{2,1,0:T(2,128)(2,1)}), bf16[128,2,128]{2,1,0:T(2,128)(2,1)S(1)}, u32[]{:S(2)}, u32[]{:S(2)}) async-start(bf16[128,2,128]{2,1,0:T(2,128)(2,1)} %reshape.356), calls=%async_computation | async-start | bytes 131072 | tf_op jit(solution)/shard_map/all_to_all | solution.py:56
  38.1 77.2 %all-gather.3.cloned.1.call-start = ((), (), s32[]{:S(2)}) async-start(), calls=%async_computation.9 | async-start | bytes 4259840 | tf_op jit(solution)/shard_map/all_gather | solution.py:69
  49.1 7.9 copy-start.4
  51.6 16.5 %all-to-all-start.2 = ((bf16[128,2,512]{2,1,0:T(2,128)(2,1)}), bf16[128,2,512]{2,1,0:T(2,128)(2,1)S(1)}, u32[]{:S(2)}, u32[]{:S(2)}) async-start(bf16[128,2,512]{2,1,0:T(2,128)(2,1)} %reshape.358), calls=%async_computation.2 | async-start | bytes 524288 | tf_op jit(solution)/shard_map/all_to_all | solution.py:55
  56.9 15.8 %copy-start.5 = (s32[1,16]{1,0:T(1,128)S(1)}, s32[1,16]{1,0:T(1,128)}, u32[]{:S(2)}) copy-start(s32[1,16]{1,0:T(1,128)} %param.21) | copy-start | bytes 196
  68.1 15.2 %all-to-all-start.4 = ((bf16[128,2,512]{2,1,0:T(2,128)(2,1)}), bf16[128,2,512]{2,1,0:T(2,128)(2,1)S(1)}, u32[]{:S(2)}, u32[]{:S(2)}) async-start(bf16[128,2,512]{2,1,0:T(2,128)(2,1)} %reshape.362), calls=%async_computation.4 | async-start | bytes 524288 | tf_op jit(solution)/shard_map/all_to_all | solution.py:57
  72.5 821.8 %reduce-scatter.2.cloned.1.call-start = ((), (), s32[]{:S(2)}) async-start(), calls=%async_computation.8 | async-start | bytes 8519680 | tf_op jit(solution)/shard_map/reduce_scatter | solution.py:161
  128.5 1.4 copy-start.2
  143.9 1.4 copy-start.2
  166.8 1.4 copy-start.2
  189.8 1.4 copy-start.2
  212.7 1.4 copy-start.2
  220.4 1.4 copy-start.2
  228.0 1.4 copy-start.2
  258.5 1.4 copy-start.3
  304.3 1.4 copy-start.3
  311.9 1.4 copy-start.3
  319.5 1.4 copy-start.3
  438.9 156.7 %all-to-all-start.5 = ((bf16[128,2,512]{2,1,0:T(2,128)(2,1)}), bf16[128,2,512]{2,1,0:T(2,128)(2,1)S(1)}, u32[]{:S(2)}, u32[]{:S(2)}) async-start(bf16[128,2,512]{2,1,0:T(2,128)(2,1)} %reshape.364), calls=%async_computation.5 | async-start | bytes 524288 | tf_op jit(solution)/shard_map/all_to_all | solution.py:169
  595.5 301.8 %all-to-all-start.3 = ((bf16[128,2,512]{2,1,0:T(2,128)(2,1)}), bf16[128,2,512]{2,1,0:T(2,128)(2,1)S(1)}, u32[]{:S(2)}, u32[]{:S(2)}) async-start(bf16[128,2,512]{2,1,0:T(2,128)(2,1)} %reshape.360), calls=%async_computation.3 | async-start | bytes 524288 | tf_op jit(solution)/shard_map/all_to_all | solution.py:168
  897.4 61.1 %all-to-all-start.6 = ((bf16[128,2,128]{2,1,0:T(2,128)(2,1)}), bf16[128,2,128]{2,1,0:T(2,128)(2,1)S(1)}, u32[]{:S(2)}, u32[]{:S(2)}) async-start(bf16[128,2,128]{2,1,0:T(2,128)(2,1)} %reshape.366), calls=%async_computation.7 | async-start | bytes 131072 | tf_op jit(solution)/shard_map/all_to_all | solution.py:170
  949.5 10.4 %copy-start.1 = (bf16[128,1024]{1,0:T(8,128)(2,1)S(1)}, bf16[128,1024]{1,0:T(8,128)(2,1)}, u32[]{:S(2)}) copy-start(bf16[128,1024]{1,0:T(8,128)(2,1)} %param.17) | copy-start | bytes 786436
  (21 other events, 29.3 us)
Sparse Core Ops, SparseCore 0:
  49.2 66.0 all-gather.2
  436.4 457.8 reduce-scatter.1
where the time goes:
time: 972 us; the launch traced here: 967 us
  waiting for transfers between devices  365 us (38%)
  local copies, waits for them, and re-layouts  235 us (24%)
  starting transfers between devices  226 us (23%)
  loops' own time  96.4 us (10%)
  other arithmetic  21.8 us (2%)
  between operations  14.4 us (1%)
    reduce_scatter x1, waiting for transfers between devices, on_device(): owned = lax.psum_scatter(grad_terms, 'ctx', scatter_dimension=0, tiled=True)  292 us
    all_to_all x1, starting transfers between devices, on_device(): lax.all_to_all(grad_query_rows, ('dp', 'ctx'), split_axis=0, concat_axis=...  144 us
    dynamic_update_slice x96, local copies, waits for them, and re-layouts, sweep(): return lax.scan(step, carried, (block_starts,) + tuple(block_inputs))  128 us
    another operation x3, loops' own time, sweep(): return lax.scan(step, carried, (block_starts,) + tuple(block_inputs))  95 us
    all_to_all x1, starting transfers between devices, on_device(): lax.all_to_all(grad_pair_rows, ('dp', 'ctx'), split_axis=0, concat_axis=0...  51.5 us
    while x64, local copies, waits for them, and re-layouts  44.3 us
    all_gather x1, waiting for transfers between devices, on_device(): key_window = lax.all_gather(group_kv, 'ctx', axis=0, tiled=True)  30.1 us
    dynamic_slice x48, local copies, waits for them, and re-layouts, sweep(): return lax.scan(step, carried, (block_starts,) + tuple(block_inputs))  27.9 us
  transfers between devices with their start and end apart: 9, of which 8 were waited for; matrix products, arithmetic and copies ran while one was open for 3% of the time, Pallas kernels for 0%

commit v1 on v0

v1 whole, which is shorter than its diff:
```python
import functools

import jax
import jax.numpy as jnp
import numpy as np
from jax import lax
from jax.experimental import pallas as pl
from jax.experimental.pallas import tpu as pltpu
from jax.sharding import PartitionSpec as P

block = 128
head = 128
window = 18
kv_rows = 2 * window
slot_row = kv_rows
end_rows = kv_rows + 1
head_rows = 40
send_rows = 56
group = 16
other_half = 1000
nothing = -100000
masked_score = -1e30
vmem_bytes = 60 * 1024 * 1024


def kv_code():
    i = lax.broadcasted_iota(jnp.int32, (group, head_rows, block), 0)
    r = lax.broadcasted_iota(jnp.int32, (group, head_rows, block), 1)
    code = 2 * i + (r >> 1) * 2 + (r & 1) * other_half
    return jnp.where(r < kv_rows, code, nothing).reshape(group * head_rows, block)


def kv_offset(t):
    chip = t % 64
    return 2 * (chip - (window - 1)) + t // 64, chip // 32


def one_hot(mask):
    return jnp.where(mask, 1.0, 0.0).astype(jnp.bfloat16)


def pack_kernel(place_ref, ends_ref, q_ref, kv_ref, g_ref, out_ref):
    place = place_ref[...]
    rows = place >> 7
    slots = place & (block - 1)
    lane = lax.broadcasted_iota(jnp.int32, (block, block), 1)
    rows_down = jnp.broadcast_to(rows.astype(jnp.float32), (block, block)).T.astype(jnp.int32)
    slots_down = jnp.broadcast_to(slots.astype(jnp.float32), (block, block)).T
    slot_line = jnp.sum(jnp.where(rows_down == lane, slots_down, 0.0), axis=0, keepdims=True)
    lane8 = lax.broadcasted_iota(jnp.int32, (8, block), 1)
    row8 = lax.broadcasted_iota(jnp.int32, (8, block), 0)
    extra = jnp.where(row8 == slot_row % 8, jnp.broadcast_to(slot_line, (8, block)), 0.0)
    end = jnp.int32(0)
    for i in range(16):
        end = end + ends_ref[0, i]
        extra = jnp.where((lane8 == i) & (row8 == end_rows % 8), (end >> 6).astype(jnp.float32), extra)
        extra = jnp.where((lane8 == i) & (row8 == end_rows % 8 + 1), (end & 63).astype(jnp.float32), extra)
    code = kv_code()
    kv = jnp.concatenate([kv_ref[:, :head], kv_ref[:, head:]], axis=0)
    for t in range(0, 128, group):
        offset, stream = kv_offset(t)
        line = jnp.where((rows >> 6) == stream, rows - offset, 2 * nothing)
        pick = jnp.concatenate([one_hot(code == line), one_hot(code == line + other_half)], axis=1)
        got = jnp.dot(pick, kv, preferred_element_type=jnp.float32).reshape(group, head_rows, head)
        tail = got[:, head_rows - 8 :, :] + extra[None]
        got = jnp.concatenate([got[:, : head_rows - 8, :], tail], axis=1)
        out_ref[t : t + group, :head_rows, :] = got.astype(jnp.bfloat16)
    i = lax.broadcasted_iota(jnp.int32, (group * 8, block), 0)
    codes = [
        jnp.where(((i & 7) >> 1) == h, 2 * (i >> 3) + (i & 1), nothing) for h in range(4)
    ]
    for core in range(2):
        both = jnp.concatenate(
            [
                jnp.concatenate(
                    [
                        q_ref[:, (4 * core + h) * head : (4 * core + h + 1) * head],
                        g_ref[:, (4 * core + h) * head : (4 * core + h + 1) * head],
                    ],
                    axis=1,
                )
                for h in range(4)
            ],
            axis=0,
        )
        for c in range(0, 64, group):
            line = rows - 2 * c
            pick = jnp.concatenate([one_hot(codes[h] == line) for h in range(4)], axis=1)
            got = jnp.dot(pick, both, preferred_element_type=jnp.float32).astype(jnp.bfloat16)
            t = core * 64 + c
            out_ref[t : t + group, head_rows : head_rows + 8, :] = got[:, :head].reshape(group, 8, head)
            out_ref[t : t + group, head_rows + 8 :, :] = got[:, head:].reshape(group, 8, head)


def unpack_kernel(place_ref, code_ref, got_ref, out_ref, dq_ref, dkv_ref):
    rows_down = jnp.broadcast_to((place_ref[...] >> 7).astype(jnp.float32), (block, block)).T.astype(jnp.int32)
    wide = jnp.concatenate([rows_down] * (group * head_rows // block), axis=1)
    code = code_ref[0:1, :]
    sums = [jnp.zeros((block, head), jnp.float32), jnp.zeros((block, head), jnp.float32)]
    for t in range(0, 128, group):
        offset, stream = kv_offset(t)
        down = jnp.where((wide >> 6) == stream, wide - offset, 2 * nothing)
        terms = got_ref[t : t + group, :head_rows, :].reshape(group * head_rows, head)
        for half in range(2):
            pick = one_hot(code == down + half * other_half)
            sums[half] = sums[half] + jnp.dot(pick, terms, preferred_element_type=jnp.float32)
    dkv_ref[...] = jnp.concatenate(sums, axis=1).astype(jnp.bfloat16)
    lane = lax.broadcasted_iota(jnp.int32, (block, 512), 1)
    wide = jnp.concatenate([rows_down] * 4, axis=1)
    chip_code = 2 * (lane >> 3) + (lane & 1)
    for core in range(2):
        both = jnp.concatenate(
            [
                got_ref[core * 64 : core * 64 + 64, head_rows : head_rows + 8, :].reshape(512, head),
                got_ref[core * 64 : core * 64 + 64, head_rows + 8 :, :].reshape(512, head),
            ],
            axis=1,
        )
        for h in range(4):
            pick = one_hot((chip_code == wide) & (((lane & 7) >> 1) == h))
            got = jnp.dot(pick, both, preferred_element_type=jnp.float32).astype(jnp.bfloat16)
            at = (4 * core + h) * head
            out_ref[:, at : at + head] = got[:, :head]
            dq_ref[:, at : at + head] = got[:, head:]


def nt(a, b):
    return lax.dot_general(a, b, (((1,), (1,)), ((), ())), preferred_element_type=jnp.float32)


def tn(a, b):
    return lax.dot_general(a, b, (((0,), (0,)), ((), ())), preferred_element_type=jnp.float32)


def attention_kernel(
    where_ref, mine_ref, other_ref, info_ref, qg_ref,
    dmine_ref, dother_ref, out_ref, dq_ref,
    scores, weights, top, total, acc, dot, qs, gs, key_pos, bound,
):
    core = where_ref[0]
    chip = where_ref[1]
    first = 2 * (chip - (window - 1))
    scale = head ** (-0.5)
    to_exp2 = scale * 1.4426950408889634
    slots = info_ref[0].astype(jnp.float32)
    by_block = slots.T
    ends = info_ref[1, pl.ds(64 * (chip // 32), 16), :].astype(jnp.float32)[0:1] * 64.0
    ends = ends + info_ref[2, pl.ds(64 * (chip // 32), 16), :].astype(jnp.float32)[0:1]
    stream_base = (64 * (chip // 32)).astype(jnp.float32)
    block_row = lax.broadcasted_iota(jnp.int32, (block, block), 0).astype(jnp.float32)
    key_pos[...] = by_block + 128.0 * (block_row - stream_base)
    lane = lax.broadcasted_iota(jnp.int32, (block, block), 1)
    starts = []
    for par in range(2):
        slot = jnp.sum(jnp.where(lane == 2 * chip + par, slots, 0.0), axis=1, keepdims=True)
        pos = slot + 128.0 * ((2 * chip + par).astype(jnp.float32) - stream_base)
        start = jnp.max(jnp.where(ends <= pos, ends, 0.0), axis=1, keepdims=True)
        starts.append(start)
        bound[0, par * block : (par + 1) * block, :] = jnp.broadcast_to(pos, (block, block))
        bound[1, par * block : (par + 1) * block, :] = jnp.broadcast_to(start, (block, block))
    low = jnp.min(starts[0]).astype(jnp.int32) >> 8
    low = low - (chip % 32 - (window - 1))
    top[...] = jnp.full(top.shape, masked_score, jnp.float32)
    total[...] = jnp.zeros(total.shape, jnp.float32)
    acc[...] = jnp.zeros(acc.shape, jnp.float32)

    @pl.loop(0, low)
    def _(m):
        dmine_ref[2 * m] = jnp.zeros((block, head), jnp.float32)
        dmine_ref[2 * m + 1] = jnp.zeros((block, head), jnp.float32)
        dother_ref[2 * m] = jnp.zeros((block, head), jnp.bfloat16)
        dother_ref[2 * m + 1] = jnp.zeros((block, head), jnp.bfloat16)

    def pair(m, half):
        return jnp.concatenate([mine_ref[2 * m + half], other_ref[2 * m + half]], axis=0)

    @pl.loop(low, window)
    def _(m):
        keys = pair(m, 0)
        bias = []
        for par in (core, 1 - core):
            kp = key_pos[pl.ds(first + 2 * m + par, 1), :]
            bias.append(jnp.where((kp <= bound[0]) & (kp >= bound[1]), 0.0, masked_score))
        bias = jnp.concatenate(bias, axis=1)
        for h in range(4):
            s = nt(qg_ref[h * 256 : (h + 1) * 256, :], keys) + bias
            scores[m, h] = s
            top[h] = jnp.maximum(top[h], jnp.maximum(s[:, :block], s[:, block:]))

    for h in range(4):
        peak = jnp.max(top[h], axis=1, keepdims=True)
        top[h] = jnp.broadcast_to(peak * to_exp2, (256, block))

    @pl.loop(low, window)
    def _(m):
        values = pair(m, 1)
        for h in range(4):
            peak = top[h]
            p = jnp.exp2(scores[m, h] * to_exp2 - jnp.concatenate([peak, peak], axis=1))
            total[h] = total[h] + (p[:, :block] + p[:, block:])
            half = p.astype(jnp.bfloat16)
            weights[m, h] = half
            acc[h] = acc[h] + jnp.dot(half, values, preferred_element_type=jnp.float32)

    for h in range(4):
        inv = 1.0 / jnp.sum(total[h], axis=1, keepdims=True)
        o = (acc[h] * inv).astype(jnp.bfloat16)
        out_ref[h * 256 : (h + 1) * 256, :] = o
        g = qg_ref[1024 + h * 256 : 1024 + (h + 1) * 256, :].astype(jnp.float32)
        q = qg_ref[h * 256 : (h + 1) * 256, :].astype(jnp.float32)
        d = jnp.sum(g * o.astype(jnp.float32), axis=1, keepdims=True)
        dot[h] = jnp.broadcast_to(d, (256, block))
        gs[h] = (g * inv).astype(jnp.bfloat16)
        qs[h] = (q * (inv * scale)).astype(jnp.bfloat16)
        total[h] = jnp.broadcast_to(inv * scale, (256, block))
        acc[h] = jnp.zeros((256, head), jnp.float32)

    @pl.loop(low, window)
    def _(m):
        keys = pair(m, 0)
        values = pair(m, 1)
        dk = jnp.zeros((256, head), jnp.float32)
        dv = jnp.zeros((256, head), jnp.float32)
        for h in range(4):
            gw = nt(qg_ref[1024 + h * 256 : 1024 + (h + 1) * 256, :], values)
            d = dot[h]
            p = weights[m, h]
            ds = (p.astype(jnp.float32) * (gw - jnp.concatenate([d, d], axis=1))).astype(jnp.bfloat16)
            acc[h] = acc[h] + jnp.dot(ds, keys, preferred_element_type=jnp.float32)
            dk = dk + tn(ds, qs[h])
            dv = dv + tn(p, gs[h])
        dmine_ref[2 * m] = dk[:block]
        dmine_ref[2 * m + 1] = dv[:block]
        dother_ref[2 * m] = dk[block:].astype(jnp.bfloat16)
        dother_ref[2 * m + 1] = dv[block:].astype(jnp.bfloat16)

    for h in range(4):
        dq_ref[h * 256 : (h + 1) * 256, :] = (acc[h] * total[h]).astype(jnp.bfloat16)


def vmem(n):
    return [pl.BlockSpec(memory_space=pltpu.VMEM)] * n


def smem():
    return pl.BlockSpec(memory_space=pltpu.SMEM)


params = pltpu.CompilerParams(vmem_limit_bytes=vmem_bytes)


def swap(x):
    return lax.ppermute(x, "dp", [(0, 1), (1, 0)])


def exchange(x):
    return lax.all_to_all(x, ("dp", "ctx"), split_axis=0, concat_axis=0, tiled=True)


def on_device(queries, keys_values, grad_out, placement, doc_lengths):
    bf16, f32 = jnp.bfloat16, jnp.float32
    place = placement.reshape(1, block)
    sent = pl.pallas_call(
        pack_kernel,
        out_shape=jax.ShapeDtypeStruct((128, send_rows, head), bf16),
        in_specs=vmem(1) + [smem()] + vmem(3),
        out_specs=vmem(1)[0],
        compiler_params=params,
        name="pack",
    )(place, doc_lengths, queries, keys_values, grad_out)
    got = exchange(sent).transpose(1, 0, 2)
    mine = got[:kv_rows]
    info = got[kv_rows:head_rows]
    qg = got[head_rows:].reshape(2, 4, 2, block, head).reshape(2048, head)
    other = swap(mine)
    where = jnp.stack([lax.axis_index("dp"), lax.axis_index("ctx")]).astype(jnp.int32)
    dmine, dother, out, dq = pl.pallas_call(
        attention_kernel,
        out_shape=(
            jax.ShapeDtypeStruct((kv_rows, block, head), f32),
            jax.ShapeDtypeStruct((kv_rows, block, head), bf16),
            jax.ShapeDtypeStruct((1024, head), bf16),
            jax.ShapeDtypeStruct((1024, head), bf16),
        ),
        in_specs=[smem()] + vmem(4),
        out_specs=tuple(vmem(4)),
        scratch_shapes=[
            pltpu.VMEM((window, 4, 256, 256), f32),
            pltpu.VMEM((window, 4, 256, 256), bf16),
            pltpu.VMEM((4, 256, block), f32),
            pltpu.VMEM((4, 256, block), f32),
            pltpu.VMEM((4, 256, head), f32),
            pltpu.VMEM((4, 256, block), f32),
            pltpu.VMEM((4, 256, head), bf16),
            pltpu.VMEM((4, 256, head), bf16),
            pltpu.VMEM((block, block), f32),
            pltpu.VMEM((2, 256, block), f32),
        ],
        compiler_params=params,
        name="attention",
    )(where, mine, other, info, qg)
    terms = (dmine + swap(dother).astype(f32)).astype(bf16)
    back = jnp.concatenate(
        [
            terms,
            jnp.zeros((head_rows - kv_rows, block, head), bf16),
            out.reshape(8, block, head),
            dq.reshape(8, block, head),
        ],
        axis=0,
    ).transpose(1, 0, 2)
    returned = exchange(back)
    r = np.arange(group * head_rows)
    i, r = r // head_rows, r % head_rows
    code = np.where(r < kv_rows, 2 * i + (r // 2) * 2 + (r % 2) * other_half, nothing)
    code = jnp.asarray(np.tile(code[None], (8, 1)).astype(np.int32))
    return pl.pallas_call(
        unpack_kernel,
        out_shape=(
            jax.ShapeDtypeStruct((block, 8 * head), bf16),
            jax.ShapeDtypeStruct((block, 8 * head), bf16),
            jax.ShapeDtypeStruct((block, 2 * head), bf16),
        ),
        in_specs=vmem(3),
        out_specs=tuple(vmem(3)),
        compiler_params=params,
        name="unpack",
    )(place, code, returned)


def solution(mesh):
    rows = P(("dp", "ctx"), None)
    return jax.shard_map(
        on_device,
        mesh=mesh,
        in_specs=(rows, rows, rows, P(("dp", "ctx")), P("dp", None)),
        out_specs=(rows, rows, rows),
        check_vma=False,
    )
```

time: 972 us -> 129 us (0.13)
  waiting for transfers between devices: 365 us -> 0.84 us
  local copies, waits for them, and re-layouts: 235 us -> 5.42 us
  starting transfers between devices: 226 us -> 1.44 us
  blocking collectives: 0 us -> 102 us
  loops' own time: 96.4 us -> 0 us
  other arithmetic: 21.8 us -> 3.93 us
  Pallas kernels: 0 us -> 14.3 us
  between operations: 14.4 us -> 0.69 us
    reduce_scatter x1 -> x0, waiting for transfers between devices: 292 us -> none  [on_device(): owned = lax.psum_scatter(grad_terms, 'ctx', scatter_dimension=0, tiled=True)]
    all_to_all x7 -> x0, starting transfers between devices: 225 us -> none  [the longest x1 144 us: on_device(): lax.all_to_all(grad_query_rows, ('dp', 'ctx'), split_axis=0, concat_axis=...]
    dynamic_update_slice x96 -> x0, local copies, waits for them, and re-layouts: 128 us -> none  [sweep(): return lax.scan(step, carried, (block_starts,) + tuple(block_inputs))]
    all_to_all x0 -> x2, blocking collectives: none -> 102 us  [exchange(): lax.all_to_all(x, ('dp', 'ctx'), split_axis=0, concat_axis=0, tiled=True)]
    another operation x51 -> x0, loops' own time: 96.4 us -> none  [the longest x3 95 us: sweep(): return lax.scan(step, carried, (block_starts,) + tuple(block_inputs))]
    while x66 -> x0, local copies, waits for them, and re-layouts: 44.8 us -> none
    all_to_all x7 -> x0, waiting for transfers between devices: 43.2 us -> none  [the longest x1 9.88 us: on_device(): lax.all_to_all(grad_query_rows, ('dp', 'ctx'), split_axis=0, concat_axis=...]
    all_gather x1 -> x0, waiting for transfers between devices: 30.1 us -> none  [on_device(): key_window = lax.all_gather(group_kv, 'ctx', axis=0, tiled=True)]
  transfers between devices with their start and end apart: 9 -> 2, of which waited for: 8 -> 2; matrix products, arithmetic and copies ran while one was open for 3% -> 3% of each run, Pallas kernels for 0% -> 0%
where the time goes in v1:
time: 129 us
  blocking collectives  102 us (79%)
  Pallas kernels  14.3 us (11%)
  local copies, waits for them, and re-layouts  5.42 us (4%)
  other arithmetic  3.93 us (3%)
  starting transfers between devices  1.44 us (1%)
    all_to_all x2, blocking collectives, exchange(): lax.all_to_all(x, ('dp', 'ctx'), split_axis=0, concat_axis=0, tiled=True)  102 us
    pallas_call x1, Pallas kernels, on_device(): pl.pallas_call(attention_kernel, out_shape=(jax.ShapeDtypeStruct((kv_rows...  7.05 us
    pallas_call x1, Pallas kernels, on_device(): pl.pallas_call(unpack_kernel, out_shape=(jax.ShapeDtypeStruct((block, 8 *...  3.76 us
    pallas_call x1, Pallas kernels, on_device(): pl.pallas_call(pack_kernel, out_shape=jax.ShapeDtypeStruct((128, send_row...  3.48 us
    convert_element_type x2, other arithmetic, on_device(): terms = (dmine + swap(dother).astype(f32)).astype(bf16)  2.87 us
  transfers between devices with their start and end apart: 2, of which 2 were waited for; matrix products, arithmetic and copies ran while one was open for 3% of the time, Pallas kernels for 0%

profile of v1, /device:TPU:1, one launch (start us, length us, event | category | flops | bytes accessed | tf_op | source)
XLA Modules:
  0.0 128.8 jit_solution(3119078409917537003)
XLA Ops:
  0.6 3.5 %pack.1 = bf16[128,56,128]{2,1,0:T(8,128)(2,1)} custom-call(s32[1,128]{1,0:T(1,128)} %bitcast.17, s32[1,16]{1,0:T(1,128)} %ends_ref.1, bf16[128,1024]{1,0:T(8,128)(2,1)} %q_ref.1, bf16[128,256]{1,0:T(8,128)(2,1)} %kv_ref.1, bf16[128,1024]{1,0:T(8,128)(2,1)} %g_ref.1), custom_call_target="tpu_custom_call" | custom-call | tf_op jit(solution)/shard_map/pack/pallas_call | solution.py:263
  4.1 38.4 %all_to_all.10 = bf16[128,56,128]{2,1,0:T(8,128)(2,1)S(1)} all-to-all(bf16[128,56,128]{2,1,0:T(8,128)(2,1)} %pack.1), channel_id=1, replica_groups=mesh['dp'=2,'ctx'=64] {'dp','ctx'}, dimensions={0} | all-to-all | bytes 3670016 | tf_op jit(solution)/shard_map/all_to_all | solution.py:257
  42.5 0.4 copy.32
  43.0 0.1 slice.12.mine_ref
  43.1 0.0 copy-start
  43.1 1.1 collective-permute-start
  44.2 0.6 pad_add_fusion.where_ref
  44.8 0.8 slice.14
  45.6 0.7 slice.13.info_ref
  46.3 0.5 collective-permute-done.other_ref
  46.8 0.0 copy-done
  46.8 7.0 %attention.1 = (f32[36,128,128]{2,1,0:T(8,128)}, bf16[36,128,128]{2,1,0:T(8,128)(2,1)}, bf16[1024,128]{1,0:T(8,128)(2,1)}, bf16[1024,128]{1,0:T(8,128)(2,1)}) custom-call(s32[2]{0:T(128)} %pad_add_fusion.where_ref, bf16[36,128,128]{2,1,0:T(8,128)(2,1)} %copy-done, bf16[36,128,128]{2,1,0:T(8,128)(2,1)} %collective-permute-done.other_ref, ...), custom_call_target="tpu_custom_call" | custom-call | tf_op jit(solution)/shard_map/attention/pallas_call | solution.py:277
  53.8 0.4 collective-permute-start.1
  54.2 0.1 pad.1.clone
  54.3 1.1 copy.25
  55.4 1.1 copy.26
  56.5 0.0 copy-start.1
  56.5 0.3 collective-permute-done.1
  56.9 0.3 convert_element_type.6
  57.2 1.0 copy-done.1
  58.2 2.6 %fusion = bf16[36,128,128]{2,0,1:T(8,128)(2,1)S(1)} fusion(f32[36,128,128]{2,1,0:T(8,128)S(1)} %convert_element_type.6, f32[36,128,128]{2,1,0:T(8,128)S(1)} %copy-done.1), kind=kLoop, calls=%fused_computation.1 | loop fusion | flops 1179648 | bytes 5898240 | tf_op jit(solution)/shard_map/convert_element_type | solution.py:302
  60.8 0.4 maximum_bitcast_fusion
  61.2 63.8 %all_to_all.11.got_ref = bf16[128,56,128]{2,1,0:T(8,128)(2,1)} all-to-all(bf16[128,56,128]{2,1,0:T(8,128)(2,1)S(1)} %maximum_bitcast_fusion), channel_id=1, replica_groups=mesh['dp'=2,'ctx'=64] {'dp','ctx'}, dimensions={0} | all-to-all | bytes 3670016 | tf_op jit(solution)/shard_map/all_to_all | solution.py:257
  125.0 3.8 %unpack.1 = (bf16[128,1024]{1,0:T(8,128)(2,1)}, bf16[128,1024]{1,0:T(8,128)(2,1)}, bf16[128,256]{1,0:T(8,128)(2,1)}) custom-call(s32[1,128]{1,0:T(1,128)} %bitcast.18, s32[8,640]{1,0:T(8,128)} %constant.13.clone.code_ref, bf16[128,56,128]{2,1,0:T(8,128)(2,1)} %all_to_all.11.got_ref), custom_call_target="tpu_custom_call" | custom-call | tf_op jit(solution)/shard_map/unpack/pallas_call | solution.py:317
  (1 shorter events, 0.0 us)
Async XLA Ops:
  43.1 3.7 %copy-start = (bf16[36,128,128]{2,1,0:T(8,128)(2,1)}, bf16[36,128,128]{2,1,0:T(8,128)(2,1)S(1)}, u32[]{:S(2)}) copy-start(bf16[36,128,128]{2,1,0:T(8,128)(2,1)S(1)} %slice.12.mine_ref) | copy-start | bytes 3538948
  43.1 3.7 %collective-permute-start = (bf16[36,128,128]{2,1,0:T(8,128)(2,1)S(1)}, bf16[36,128,128]{2,1,0:T(8,128)(2,1)}, u32[]{:S(2)}, u32[]{:S(2)}) collective-permute-start(bf16[36,128,128]{2,1,0:T(8,128)(2,1)S(1)} %slice.12.mine_ref), channel_id=1, source_target_pairs={{0,64},{64,0},{1,65},{65,1},{2,66},{66,2},{3,67},{67,3},{4,68},{68... | collective-permute-start | bytes 3538952 | tf_op jit(solution)/shard_map/ppermute | solution.py:253
  53.8 3.1 %collective-permute-start.1 = (bf16[36,128,128]{2,1,0:T(8,128)(2,1)}, bf16[36,128,128]{2,1,0:T(8,128)(2,1)S(1)}, u32[]{:S(2)}, u32[]{:S(2)}) collective-permute-start(bf16[36,128,128]{2,1,0:T(8,128)(2,1)} %get-tuple-element.8), channel_id=1, source_target_pairs={{0,64},{64,0},{1,65},{65,1},{2,66},{66,2},{3,67},{67,3},{4,68},{68... | collective-permute-start | bytes 3538952 | tf_op jit(solution)/shard_map/ppermute | solution.py:253
  56.5 1.7 %copy-start.1 = (f32[36,128,128]{2,1,0:T(8,128)S(1)}, f32[36,128,128]{2,1,0:T(8,128)}, u32[]{:S(2)}) copy-start(f32[36,128,128]{2,1,0:T(8,128)} %get-tuple-element.7) | copy-start | bytes 7077892

commit v2 on v1

v2 whole, which is shorter than its diff:
```python
import jax
import jax.numpy as jnp
from jax import lax
from jax.experimental import pallas as pl
from jax.experimental.pallas import tpu as pltpu
from jax.sharding import PartitionSpec as P

block = 128
head = 128
entries = 36
pairs = entries // 2
kv_rows = 2 * pairs
head_rows = 40
send_rows = 56
group = 16
other_half = 1000
nothing = -100000
masked_score = -1e30
far = 1e9
vmem_bytes = 60 * 1024 * 1024


def one_hot(mask):
    return jnp.where(mask, 1.0, 0.0).astype(jnp.bfloat16)


def down(line):
    return jnp.broadcast_to(line.astype(jnp.float32), (block, block)).T


def stream_length(core, mine_ref, other_ref, stream, i):
    return jnp.where(core == stream, mine_ref[0, i], other_ref[0, i])


def make_plan(core, mine_ref, other_ref):
    lane = lax.broadcasted_iota(jnp.int32, (1, block), 1)
    pos = (lane & 63) * block
    start = jnp.zeros((1, block), jnp.int32)
    end0, end1 = jnp.int32(0), jnp.int32(0)
    for i in range(16):
        end0 = end0 + stream_length(core, mine_ref, other_ref, 0, i)
        end1 = end1 + stream_length(core, mine_ref, other_ref, 1, i)
        end = jnp.where(lane < 64, end0, end1)
        start = jnp.where(end <= pos, end, start)
    count = (lane & 63) - (start >> 7) + 1
    key = count * 64 + (lane & 63)
    row = lax.broadcasted_iota(jnp.int32, (block, block), 0)
    col = lax.broadcasted_iota(jnp.int32, (block, block), 1)
    above = (down(key) > key.astype(jnp.float32)) & ((row >> 6) == (col >> 6))
    rank = jnp.sum(jnp.where(above, 1.0, 0.0), axis=0, keepdims=True).astype(jnp.int32)
    seat = jnp.where(rank < 32, rank, 63 - rank) + 32 * (lane >> 6) + jnp.where(rank < 32, 0, 64)
    here = down(seat) == col.astype(jnp.float32)
    block_line = jnp.sum(jnp.where(here, row.astype(jnp.float32), 0.0), axis=0, keepdims=True)
    count_line = jnp.sum(jnp.where(here, down(count), 0.0), axis=0, keepdims=True)
    return block_line, count_line


def pack_kernel(core_ref, mine_ref, other_ref, place_ref, q_ref, kv_ref, g_ref, out_ref, plan_ref):
    block_line, count_line = make_plan(core_ref[0], mine_ref, other_ref)
    row8 = lax.broadcasted_iota(jnp.int32, (8, block), 0)
    plan_ref[...] = jnp.where(row8 == 0, block_line, jnp.where(row8 == 1, count_line, 0.0))
    block_down = down(block_line).astype(jnp.int32)
    count_down = down(count_line).astype(jnp.int32)
    rows = place_ref[...] >> 7
    lane = lax.broadcasted_iota(jnp.int32, (block, block), 1)
    slots_down = down(place_ref[...] & (block - 1))
    slot_line = jnp.sum(jnp.where(down(rows) == lane.astype(jnp.float32), slots_down, 0.0), axis=0, keepdims=True)
    extra = jnp.where(row8 == kv_rows % 8, slot_line, 0.0)
    kv = jnp.concatenate([kv_ref[:, :head], kv_ref[:, head:]], axis=0)
    r = lax.broadcasted_iota(jnp.int32, (group, head_rows, block), 1)
    half = (r & 1) * other_half
    for t in range(0, 128, group):
        core, chip = t // 64, t % 64

        def spread(x):
            return jnp.broadcast_to(x[:, None, :], (group, head_rows, block))

        first = block_down[chip : chip + group]
        first_count = count_down[chip : chip + group]
        second = block_down[64 + chip : 64 + chip + group]
        second_count = count_down[64 + chip : 64 + chip + group]
        entry = (r & -2) + core
        code = jnp.where(
            entry < spread(first_count),
            entry + spread(first - first_count + 1),
            jnp.where(entry >= spread(entries - second_count), entry + spread(second - (entries - 1)), nothing),
        )
        code = (jnp.where(r < kv_rows, code, nothing) + half).reshape(group * head_rows, block)
        pick = jnp.concatenate([one_hot(code == rows), one_hot(code == rows + other_half)], axis=1)
        got = jnp.dot(pick, kv, preferred_element_type=jnp.float32).reshape(group, head_rows, head)
        tail = got[:, head_rows - 8 :, :] + extra[None]
        got = jnp.concatenate([got[:, : head_rows - 8, :], tail], axis=1)
        out_ref[t : t + group, :head_rows, :] = got.astype(jnp.bfloat16)
    j = lax.broadcasted_iota(jnp.int32, (group, 8, block), 1)
    both = []
    for core in range(2):
        heads = [slice((4 * core + h) * head, (4 * core + h + 1) * head) for h in range(4)]
        both.append(jnp.concatenate([jnp.concatenate([q_ref[:, at], g_ref[:, at]], axis=1) for at in heads], axis=0))
    for c in range(0, 64, group):
        first = jnp.broadcast_to(block_down[c : c + group][:, None, :], (group, 8, block))
        second = jnp.broadcast_to(block_down[64 + c : 64 + c + group][:, None, :], (group, 8, block))
        mine = jnp.where(j < 4, first, second) == rows[None]
        pick = jnp.concatenate(
            [one_hot(mine & ((j & 3) == h)).reshape(group * 8, block) for h in range(4)], axis=1
        )
        for core in range(2):
            got = jnp.dot(pick, both[core], preferred_element_type=jnp.float32).astype(jnp.bfloat16)
            t = core * 64 + c
            out_ref[t : t + group, head_rows : head_rows + 8, :] = got[:, :head].reshape(group, 8, head)
            out_ref[t : t + group, head_rows + 8 :, :] = got[:, head:].reshape(group, 8, head)


def spread_lanes(plan, width):
    chip = lax.broadcasted_iota(jnp.int32, (block, 64 * width), 0) * width
    lane = lax.broadcasted_iota(jnp.int32, (block, 64 * width), 1)
    return jnp.dot(plan, one_hot((lane >= chip) & (lane < chip + width)), preferred_element_type=jnp.float32)


def unpack_kernel(place_ref, plan_ref, got_ref, out_ref, dq_ref, dkv_ref):
    rows_down = down(place_ref[...] >> 7)
    plan = plan_ref[...]
    lane = lax.broadcasted_iota(jnp.int32, (8, block), 1)
    lines = [plan[0:1], plan[1:2]]
    lines = lines + [pltpu.roll(plan, 64, 1)[i : i + 1] for i in range(2)]
    lines.append(lane[0:1].astype(jnp.float32))
    stacked = jnp.zeros((16, block), jnp.float32)
    row = lax.broadcasted_iota(jnp.int32, (16, block), 0)
    for i, line in enumerate(lines):
        stacked = jnp.where((row == i) & (lane[0:1] < 64), line, stacked)
    stacked = stacked.astype(jnp.bfloat16)
    wide = spread_lanes(stacked, head_rows)
    first, first_count, second, second_count, chip = [wide[i : i + 1] for i in range(5)]
    r = lax.broadcasted_iota(jnp.int32, (1, 64 * head_rows), 1) - head_rows * chip.astype(jnp.int32)
    sums = [jnp.zeros((block, head), jnp.float32), jnp.zeros((block, head), jnp.float32)]
    rows_wide = jnp.concatenate([rows_down] * (64 * head_rows // block), axis=1)
    for core in range(2):
        entry = ((r & -2) + core).astype(jnp.float32)
        code = jnp.where(
            entry < first_count,
            entry + (first - first_count + 1),
            jnp.where(entry >= entries - second_count, entry + (second - (entries - 1)), float(nothing)),
        )
        code = jnp.where(r < kv_rows, code, float(nothing))
        terms = got_ref[core * 64 : core * 64 + 64, :head_rows, :].reshape(64 * head_rows, head)
        for half in range(2):
            pick = one_hot(jnp.where((r & 1) == half, code, float(nothing)) == rows_wide)
            sums[half] = sums[half] + jnp.dot(pick, terms, preferred_element_type=jnp.float32)
    dkv_ref[...] = jnp.concatenate(sums, axis=1).astype(jnp.bfloat16)
    wide = spread_lanes(stacked, 8)
    j = lax.broadcasted_iota(jnp.int32, (1, 512), 1) & 7
    code = jnp.where(j < 4, wide[0:1], wide[2:3])
    rows_wide = jnp.concatenate([rows_down] * 4, axis=1)
    picks = [one_hot(jnp.where((j & 3) == h, code, float(nothing)) == rows_wide) for h in range(4)]
    for core in range(2):
        both = jnp.concatenate(
            [
                got_ref[core * 64 : core * 64 + 64, head_rows : head_rows + 8, :].reshape(512, head),
                got_ref[core * 64 : core * 64 + 64, head_rows + 8 :, :].reshape(512, head),
            ],
            axis=1,
        )
        for h in range(4):
            got = jnp.dot(picks[h], both, preferred_element_type=jnp.float32).astype(jnp.bfloat16)
            at = (4 * core + h) * head
            out_ref[:, at : at + head] = got[:, :head]
            dq_ref[:, at : at + head] = got[:, head:]


def nt(a, b):
    return lax.dot_general(a, b, (((1,), (1,)), ((), ())), preferred_element_type=jnp.float32)


def tn(a, b):
    return lax.dot_general(a, b, (((0,), (0,)), ((), ())), preferred_element_type=jnp.float32)


def attention_kernel(
    where_ref, mine_len, other_len, plan_ref, mine_ref, other_ref, info_ref, qg_ref,
    dmine_ref, dother_ref, out_ref, dq_ref,
    scores, weights, top, total, acc, dot, qs, gs, key_pos, bound,
):
    core = where_ref[0]
    chip = where_ref[1]
    stream = chip // 32
    scale = head ** (-0.5)
    to_exp2 = scale * 1.4426950408889634
    slots = info_ref[0].astype(jnp.float32)
    stream_base = (64 * stream).astype(jnp.float32)
    block_row = lax.broadcasted_iota(jnp.int32, (block, block), 0).astype(jnp.float32)
    key_pos[...] = slots.T + 128.0 * (block_row - stream_base)
    lane = lax.broadcasted_iota(jnp.int32, (block, block), 1)
    lane8 = lax.broadcasted_iota(jnp.int32, (8, block), 1)
    row8 = lax.broadcasted_iota(jnp.int32, (8, block), 0)
    plan = plan_ref[...]
    dmine_ref[...] = jnp.zeros(dmine_ref.shape, jnp.float32)
    dother_ref[...] = jnp.zeros(dother_ref.shape, jnp.float32)

    def planned(row, x):
        seat = (row8 == row) & (lane8 == chip + 64 * x)
        return jnp.sum(jnp.where(seat, plan, 0.0)).astype(jnp.int32)

    def pair(m, half):
        return jnp.concatenate([mine_ref[2 * m + half], other_ref[2 * m + half]], axis=0)

    for x in range(2):
        mine_block = planned(0, x)
        count = planned(1, x)
        if x == 0:
            begin, end = jnp.int32(0), (count + 1) >> 1
            entry_low, entry_high = jnp.int32(0), count
            base = mine_block - count + 1
        else:
            begin, end = (entries - count) >> 1, jnp.int32(pairs)
            entry_low, entry_high = entries - count, jnp.int32(entries)
            base = mine_block - (entries - 1)
        slot = jnp.sum(jnp.where(lane == mine_block, slots, 0.0), axis=1, keepdims=True)
        pos = jnp.broadcast_to(slot + 128.0 * (mine_block.astype(jnp.float32) - stream_base), (block, block))
        start = jnp.zeros((block, block), jnp.float32)
        doc_end = jnp.int32(0)
        for i in range(16):
            doc_end = doc_end + stream_length(core, mine_len, other_len, stream, i)
            f = doc_end.astype(jnp.float32)
            start = jnp.where(f <= pos, f, start)
        bound[0] = pos
        bound[1] = start
        top[...] = jnp.full(top.shape, masked_score, jnp.float32)
        total[...] = jnp.zeros(total.shape, jnp.float32)
        acc[...] = jnp.zeros(acc.shape, jnp.float32)
        q_at, g_at = x * 512, 1024 + x * 512

        @pl.loop(begin, end)
        def _(m):
            keys = pair(m, 0)
            bias = []
            for par in (core, 1 - core):
                entry = 2 * m + par
                valid = (entry >= entry_low) & (entry < entry_high)
                kp = key_pos[pl.ds(jnp.where(valid, base + entry, 0), 1), :]
                kp = jnp.where(valid, kp, far)
                bias.append(jnp.where((kp <= bound[0]) & (kp >= bound[1]), 0.0, masked_score))
            bias = jnp.concatenate(bias, axis=1)
            bias = jnp.concatenate([bias, bias], axis=0)
            for h in range(2):
                s = nt(qg_ref[q_at + h * 256 : q_at + (h + 1) * 256, :], keys) + bias
                scores[m, h] = s
                top[h] = jnp.maximum(top[h], jnp.maximum(s[:, :block], s[:, block:]))

        for h in range(2):
            peak = jnp.max(top[h], axis=1, keepdims=True)
            top[h] = jnp.broadcast_to(peak * to_exp2, (256, block))

        @pl.loop(begin, end)
        def _(m):
            values = pair(m, 1)
            for h in range(2):
                peak = top[h]
                p = jnp.exp2(scores[m, h] * to_exp2 - jnp.concatenate([peak, peak], axis=1))
                total[h] = total[h] + (p[:, :block] + p[:, block:])
                half = p.astype(jnp.bfloat16)
                weights[m, h] = half
                acc[h] = acc[h] + jnp.dot(half, values, preferred_element_type=jnp.float32)

        for h in range(2):
            inv = 1.0 / jnp.sum(total[h], axis=1, keepdims=True)
            o = (acc[h] * inv).astype(jnp.bfloat16)
            out_ref[q_at + h * 256 : q_at + (h + 1) * 256, :] = o
            g = qg_ref[g_at + h * 256 : g_at + (h + 1) * 256, :].astype(jnp.float32)
            q = qg_ref[q_at + h * 256 : q_at + (h + 1) * 256, :].astype(jnp.float32)
            d = jnp.sum(g * o.astype(jnp.float32), axis=1, keepdims=True)
            dot[h] = jnp.broadcast_to(d, (256, block))
            gs[h] = (g * inv).astype(jnp.bfloat16)
            qs[h] = (q * (inv * scale)).astype(jnp.bfloat16)
            total[h] = jnp.broadcast_to(inv * scale, (256, block))
            acc[h] = jnp.zeros((256, head), jnp.float32)

        @pl.loop(begin, end)
        def _(m):
            keys = pair(m, 0)
            values = pair(m, 1)
            dk = jnp.zeros((256, head), jnp.float32)
            dv = jnp.zeros((256, head), jnp.float32)
            for h in range(2):
                gw = nt(qg_ref[g_at + h * 256 : g_at + (h + 1) * 256, :], values)
                d = dot[h]
                p = weights[m, h]
                ds = (p.astype(jnp.float32) * (gw - jnp.concatenate([d, d], axis=1))).astype(jnp.bfloat16)
                acc[h] = acc[h] + jnp.dot(ds, keys, preferred_element_type=jnp.float32)
                dk = dk + tn(ds, qs[h])
                dv = dv + tn(p, gs[h])
            dmine_ref[2 * m] = dmine_ref[2 * m] + dk[:block]
            dmine_ref[2 * m + 1] = dmine_ref[2 * m + 1] + dv[:block]
            dother_ref[2 * m] = dother_ref[2 * m] + dk[block:]
            dother_ref[2 * m + 1] = dother_ref[2 * m + 1] + dv[block:]

        for h in range(2):
            dq_ref[q_at + h * 256 : q_at + (h + 1) * 256, :] = (acc[h] * total[h]).astype(jnp.bfloat16)


def vmem(n):
    return [pl.BlockSpec(memory_space=pltpu.VMEM)] * n


def smem():
    return pl.BlockSpec(memory_space=pltpu.SMEM)


params = pltpu.CompilerParams(vmem_limit_bytes=vmem_bytes)


def swap(x):
    return lax.ppermute(x, "dp", [(0, 1), (1, 0)])


def exchange(x):
    return lax.all_to_all(x, ("dp", "ctx"), split_axis=0, concat_axis=0, tiled=True)


def on_device(queries, keys_values, grad_out, placement, doc_lengths):
    bf16, f32 = jnp.bfloat16, jnp.float32
    place = placement.reshape(1, block)
    where = jnp.stack([lax.axis_index("dp"), lax.axis_index("ctx")]).astype(jnp.int32)
    other_lengths = swap(doc_lengths)
    sent, plan = pl.pallas_call(
        pack_kernel,
        out_shape=(
            jax.ShapeDtypeStruct((128, send_rows, head), bf16),
            jax.ShapeDtypeStruct((8, block), f32),
        ),
        in_specs=[smem()] * 3 + vmem(4),
        out_specs=tuple(vmem(2)),
        compiler_params=params,
        name="pack",
    )(where, doc_lengths, other_lengths, place, queries, keys_values, grad_out)
    got = exchange(sent).transpose(1, 0, 2)
    mine = got[:kv_rows]
    info = got[kv_rows:head_rows]
    qg = got[head_rows:].reshape(2048, head)
    other = swap(mine)
    dmine, dother, out, dq = pl.pallas_call(
        attention_kernel,
        out_shape=(
            jax.ShapeDtypeStruct((kv_rows, block, head), f32),
            jax.ShapeDtypeStruct((kv_rows, block, head), f32),
            jax.ShapeDtypeStruct((1024, head), bf16),
            jax.ShapeDtypeStruct((1024, head), bf16),
        ),
        in_specs=[smem()] * 3 + vmem(5),
        out_specs=tuple(vmem(4)),
        scratch_shapes=[
            pltpu.VMEM((pairs, 2, 256, 256), f32),
            pltpu.VMEM((pairs, 2, 256, 256), bf16),
            pltpu.VMEM((2, 256, block), f32),
            pltpu.VMEM((2, 256, block), f32),
            pltpu.VMEM((2, 256, head), f32),
            pltpu.VMEM((2, 256, block), f32),
            pltpu.VMEM((2, 256, head), bf16),
            pltpu.VMEM((2, 256, head), bf16),
            pltpu.VMEM((block, block), f32),
            pltpu.VMEM((2, block, block), f32),
        ],
        compiler_params=params,
        name="attention",
    )(where, doc_lengths, other_lengths, plan, mine, other, info, qg)
    terms = (dmine + swap(dother.astype(bf16)).astype(f32)).astype(bf16)
    back = jnp.concatenate(
        [
            terms,
            jnp.zeros((head_rows - kv_rows, block, head), bf16),
            out.reshape(8, block, head),
            dq.reshape(8, block, head),
        ],
        axis=0,
    ).transpose(1, 0, 2)
    returned = exchange(back)
    return pl.pallas_call(
        unpack_kernel,
        out_shape=(
            jax.ShapeDtypeStruct((block, 8 * head), bf16),
            jax.ShapeDtypeStruct((block, 8 * head), bf16),
            jax.ShapeDtypeStruct((block, 2 * head), bf16),
        ),
        in_specs=vmem(3),
        out_specs=tuple(vmem(3)),
        compiler_params=params,
        name="unpack",
    )(place, plan, returned)


def solution(mesh):
    rows = P(("dp", "ctx"), None)
    return jax.shard_map(
        on_device,
        mesh=mesh,
        in_specs=(rows, rows, rows, P(("dp", "ctx")), P("dp", None)),
        out_specs=(rows, rows, rows),
        check_vma=False,
    )
```

time: 129 us -> 121 us (0.938)
  blocking collectives: 102 us -> 68.2 us
  Pallas kernels: 14.3 us -> 35.7 us
  waiting for transfers between devices: 0.84 us -> 3.3 us
  other arithmetic: 3.93 us -> 5.87 us
  starting transfers between devices: 1.44 us -> 3.03 us
  local copies, waits for them, and re-layouts: 5.42 us -> 4.01 us
    all_to_all x2, blocking collectives: 102 us -> 68.2 us  [exchange(): lax.all_to_all(x, ('dp', 'ctx'), split_axis=0, concat_axis=0, tiled=True)]
    pallas_call x1, Pallas kernels: 7.05 us -> 27.3 us  [on_device(): pl.pallas_call(attention_kernel, out_shape=(jax.ShapeDtypeStruct((kv_rows...]
    ppermute x2 -> x3, waiting for transfers between devices: 0.84 us -> 3.3 us  [swap(): return lax.ppermute(x, 'dp', [(0, 1), (1, 0)])]
    convert_element_type x2 -> x3, other arithmetic: 2.87 us -> 4.77 us  [on_device(): terms = (dmine + swap(dother.astype(bf16)).astype(f32)).astype(bf16)]
    ppermute x2 -> x3, starting transfers between devices: 1.44 us -> 3.03 us  [swap(): return lax.ppermute(x, 'dp', [(0, 1), (1, 0)])]
  transfers between devices with their start and end apart: 2 -> 3, of which waited for: 2 -> 3; matrix products, arithmetic and copies ran while one was open for 3% -> 2% of each run, Pallas kernels for 0% -> 0%
where the time goes in v2:
time: 121 us
  blocking collectives  68.2 us (56%)
  Pallas kernels  35.7 us (30%)
  other arithmetic  5.87 us (5%)
  local copies, waits for them, and re-layouts  4.01 us (3%)
  waiting for transfers between devices  3.3 us (3%)
  starting transfers between devices  3.03 us (3%)
    all_to_all x2, blocking collectives, exchange(): lax.all_to_all(x, ('dp', 'ctx'), split_axis=0, concat_axis=0, tiled=True)  68.2 us
    pallas_call x1, Pallas kernels, on_device(): pl.pallas_call(attention_kernel, out_shape=(jax.ShapeDtypeStruct((kv_rows...  27.3 us
    convert_element_type x3, other arithmetic, on_device(): terms = (dmine + swap(dother.astype(bf16)).astype(f32)).astype(bf16)  4.77 us
    pallas_call x1, Pallas kernels, on_device(): pl.pallas_call(pack_kernel, out_shape=(jax.ShapeDtypeStruct((128, send_ro...  4.35 us
    pallas_call x1, Pallas kernels, on_device(): pl.pallas_call(unpack_kernel, out_shape=(jax.ShapeDtypeStruct((block, 8 *...  4.02 us
    ppermute x3, waiting for transfers between devices, swap(): return lax.ppermute(x, 'dp', [(0, 1), (1, 0)])  3.3 us
    ppermute x3, starting transfers between devices, swap(): return lax.ppermute(x, 'dp', [(0, 1), (1, 0)])  3.03 us
  transfers between devices with their start and end apart: 3, of which 3 were waited for; matrix products, arithmetic and copies ran while one was open for 2% of the time, Pallas kernels for 0%

profile of v2, /device:TPU:1, one launch (start us, length us, event | category | flops | bytes accessed | tf_op | source)
XLA Modules:
  0.0 120.8 jit_solution(6217922270763743083)
XLA Ops:
  0.6 1.5 %collective-permute-start = (s32[1,16]{1,0:T(1,128)}, s32[1,16]{1,0:T(1,128)S(1)}, u32[]{:S(2)}, u32[]{:S(2)}) collective-permute-start(s32[1,16]{1,0:T(1,128)} %mine_len.1), channel_id=1, source_target_pairs={{0,64},{64,0},{1,65},{65,1},{2,66},{66,2},{3,67},{67,3},{4,68},{68... | collective-permute-start | bytes 200 | tf_op jit(solution)/shard_map/ppermute | solution.py:311
  2.1 0.7 pad_add_fusion.core_ref.where_ref
  2.8 0.3 collective-permute-done.other_ref.other_len
  3.1 0.5 copy-done.5
  3.6 4.4 %pack.1 = (bf16[128,56,128]{2,1,0:T(8,128)(2,1)}, f32[8,128]{1,0:T(8,128)}) custom-call(s32[2]{0:T(128)} %pad_add_fusion.core_ref.where_ref, s32[1,16]{1,0:T(1,128)} %mine_len.1, s32[1,16]{1,0:T(1,128)} %copy-done.5, s32[1,128]{1,0:T(1,128)} %bitcast.17, bf16[128,1024]{1,0:T(8,128)(2,1)} %q_ref.1, bf16[128,256]{1,0:T(8,128)(2,1)} %kv_ref.1, ...), custom_call_target="tpu_custom_call" | custom-call | tf_op jit(solution)/shard_map/pack/pallas_call | solution.py:323
  7.9 37.3 %all_to_all.10 = bf16[128,56,128]{2,1,0:T(8,128)(2,1)S(1)} all-to-all(bf16[128,56,128]{2,1,0:T(8,128)(2,1)} %get-tuple-element.10), channel_id=1, replica_groups=mesh['dp'=2,'ctx'=64] {'dp','ctx'}, dimensions={0} | all-to-all | bytes 3670016 | tf_op jit(solution)/shard_map/all_to_all | solution.py:315
  45.2 0.4 copy.31
  45.7 0.1 slice.12.mine_ref
  45.8 1.1 collective-permute-start.1
  46.9 0.8 slice.14
  47.7 0.7 slice.13.info_ref
  48.3 1.0 collective-permute-done.1.other_ref
  49.3 1.0 copy-done.2
  50.4 27.3 %attention.1 = (f32[36,128,128]{2,1,0:T(8,128)}, f32[36,128,128]{2,1,0:T(8,128)}, bf16[1024,128]{1,0:T(8,128)(2,1)}, bf16[1024,128]{1,0:T(8,128)(2,1)}) custom-call(s32[2]{0:T(128)} %pad_add_fusion.core_ref.where_ref, s32[1,16]{1,0:T(1,128)} %mine_len.1, s32[1,16]{1,0:T(1,128)} %copy-done.5, f32[8,128]{1,0:T(8,128)} %get-tuple-element.9.plan_ref, ...), custom_call_target="tpu_custom_call" | custom-call | tf_op jit(solution)/shard_map/attention/pallas_call | solution.py:339
  77.7 1.9 %convert_element_type.9 = bf16[36,128,128]{2,1,0:T(8,128)(2,1)S(1)} convert(f32[36,128,128]{2,1,0:T(8,128)} %get-tuple-element.12) | non-fusion elementwise | flops 589824 | bytes 3538944 | tf_op jit(solution)/shard_map/convert_element_type | solution.py:364
  79.6 0.5 collective-permute-start.2
  80.2 0.2 copy.24
  80.3 0.2 copy.25
  80.5 2.0 %collective-permute-done.2 = bf16[36,128,128]{2,1,0:T(8,128)(2,1)S(1)} collective-permute-done((bf16[36,128,128]{2,1,0:T(8,128)(2,1)S(1)}, bf16[36,128,128]{2,1,0:T(8,128)(2,1)S(1)}, u32[]{:S(2)}, u32[]{:S(2)}) %collective-permute-start.2) | collective-permute-done | bytes 1179680 | tf_op jit(solution)/shard_map/ppermute | solution.py:311
  82.6 0.3 convert_element_type.10
  82.8 2.6 %fusion = bf16[36,128,128]{2,0,1:T(8,128)(2,1)S(1)} fusion(f32[36,128,128]{2,1,0:T(8,128)S(1)} %convert_element_type.10, f32[36,128,128]{2,1,0:T(8,128)S(1)} %copy-done.1), kind=kLoop, calls=%fused_computation.1 | loop fusion | flops 1179648 | bytes 5898240 | tf_op jit(solution)/shard_map/convert_element_type | solution.py:364
  85.4 0.4 maximum_bitcast_fusion
  85.9 30.9 %all_to_all.11.got_ref = bf16[128,56,128]{2,1,0:T(8,128)(2,1)} all-to-all(bf16[128,56,128]{2,1,0:T(8,128)(2,1)S(1)} %maximum_bitcast_fusion), channel_id=1, replica_groups=mesh['dp'=2,'ctx'=64] {'dp','ctx'}, dimensions={0} | all-to-all | bytes 3670016 | tf_op jit(solution)/shard_map/all_to_all | solution.py:315
  116.8 4.0 %unpack.1 = (bf16[128,1024]{1,0:T(8,128)(2,1)}, bf16[128,1024]{1,0:T(8,128)(2,1)}, bf16[128,256]{1,0:T(8,128)(2,1)}) custom-call(s32[1,128]{1,0:T(1,128)} %bitcast.18, f32[8,128]{1,0:T(8,128)} %get-tuple-element.9.plan_ref, bf16[128,56,128]{2,1,0:T(8,128)(2,1)} %all_to_all.11.got_ref), custom_call_target="tpu_custom_call" | custom-call | tf_op jit(solution)/shard_map/unpack/pallas_call | solution.py:375
  (12 shorter events, 0.1 us)
Async XLA Ops:
  0.6 2.5 %collective-permute-start = (s32[1,16]{1,0:T(1,128)}, s32[1,16]{1,0:T(1,128)S(1)}, u32[]{:S(2)}, u32[]{:S(2)}) collective-permute-start(s32[1,16]{1,0:T(1,128)} %mine_len.1), channel_id=1, source_target_pairs={{0,64},{64,0},{1,65},{65,1},{2,66},{66,2},{3,67},{67,3},{4,68},{68... | collective-permute-start | bytes 200 | tf_op jit(solution)/shard_map/ppermute | solution.py:311
  3.1 0.5 copy-start.5
  45.8 3.6 %copy-start = (bf16[36,128,128]{2,1,0:T(8,128)(2,1)}, bf16[36,128,128]{2,1,0:T(8,128)(2,1)S(1)}, u32[]{:S(2)}) copy-start(bf16[36,128,128]{2,1,0:T(8,128)(2,1)S(1)} %slice.12.mine_ref) | copy-start | bytes 3538948
  45.8 3.6 %collective-permute-start.1 = (bf16[36,128,128]{2,1,0:T(8,128)(2,1)S(1)}, bf16[36,128,128]{2,1,0:T(8,128)(2,1)S(1)}, u32[]{:S(2)}, u32[]{:S(2)}) collective-permute-start(bf16[36,128,128]{2,1,0:T(8,128)(2,1)S(1)} %slice.12.mine_ref), channel_id=1, source_target_pairs={{0,64},{64,0},{1,65},{65,1},{2,66},{66,2},{3,67},{67,3},{4,68},{68... | collective-permute-start | bytes 3538952 | tf_op jit(solution)/shard_map/ppermute | solution.py:311
  49.3 1.0 copy-start.2
  77.7 2.5 %copy-start.4 = (bf16[1024,128]{1,0:T(8,128)(2,1)S(1)}, bf16[1024,128]{1,0:T(8,128)(2,1)}, u32[]{:S(2)}) copy-start(bf16[1024,128]{1,0:T(8,128)(2,1)} %get-tuple-element.13) | copy-start | bytes 786436
  77.7 2.6 %copy-start.3 = (bf16[1024,128]{1,0:T(8,128)(2,1)S(1)}, bf16[1024,128]{1,0:T(8,128)(2,1)}, u32[]{:S(2)}) copy-start(bf16[1024,128]{1,0:T(8,128)(2,1)} %get-tuple-element.14) | copy-start | bytes 786436
  79.6 2.9 %collective-permute-start.2 = (bf16[36,128,128]{2,1,0:T(8,128)(2,1)S(1)}, bf16[36,128,128]{2,1,0:T(8,128)(2,1)S(1)}, u32[]{:S(2)}, u32[]{:S(2)}) collective-permute-start(bf16[36,128,128]{2,1,0:T(8,128)(2,1)S(1)} %convert_element_type.9), channel_id=1, source_target_pairs={{0,64},{64,0},{1,65},{65,1},{2,66},{66,2},{3,67},{67,3},{4,68},{68... | collective-permute-start | bytes 3538952 | tf_op jit(solution)/shard_map/ppermute | solution.py:311
  80.5 2.3 %copy-start.1 = (f32[36,128,128]{2,1,0:T(8,128)S(1)}, f32[36,128,128]{2,1,0:T(8,128)}, u32[]{:S(2)}) copy-start(f32[36,128,128]{2,1,0:T(8,128)} %get-tuple-element.11) | copy-start | bytes 7077892

commit v3 on v2

--- a/solution.py
+++ b/solution.py
@@ -17,7 +17,8 @@
 nothing = -100000
 masked_score = -1e30
 far = 1e9
-vmem_bytes = 60 * 1024 * 1024
+step = 3
+mib = 1024 * 1024
 
 
 def one_hot(mask):
@@ -55,8 +56,8 @@
     return block_line, count_line
 
 
-def pack_kernel(core_ref, mine_ref, other_ref, place_ref, q_ref, kv_ref, g_ref, out_ref, plan_ref):
-    block_line, count_line = make_plan(core_ref[0], mine_ref, other_ref)
+def pack_kernel(mine_ref, other_ref, place_ref, q_ref, kv_ref, g_ref, out_ref, plan_ref):
+    block_line, count_line = make_plan(lax.axis_index("dp"), mine_ref, other_ref)
     row8 = lax.broadcasted_iota(jnp.int32, (8, block), 0)
     plan_ref[...] = jnp.where(row8 == 0, block_line, jnp.where(row8 == 1, count_line, 0.0))
     block_down = down(block_line).astype(jnp.int32)
@@ -174,55 +175,73 @@
     return lax.dot_general(a, b, (((0,), (0,)), ((), ())), preferred_element_type=jnp.float32)
 
 
+def nn(a, b):
+    return jnp.dot(a, b, preferred_element_type=jnp.float32)
+
+
 def attention_kernel(
-    where_ref, mine_len, other_len, plan_ref, mine_ref, other_ref, info_ref, qg_ref,
+    mine_len, other_len, plan_ref, mine_ref, other_ref,
     dmine_ref, dother_ref, out_ref, dq_ref,
-    scores, weights, top, total, acc, dot, qs, gs, key_pos, bound,
+    kv, qg, scores, weights, top, total, acc, dot, qs, gs, key_pos, bound,
 ):
-    core = where_ref[0]
-    chip = where_ref[1]
+    core = lax.axis_index("dp")
+    chip = lax.axis_index("ctx")
     stream = chip // 32
     scale = head ** (-0.5)
     to_exp2 = scale * 1.4426950408889634
-    slots = info_ref[0].astype(jnp.float32)
     stream_base = (64 * stream).astype(jnp.float32)
     block_row = lax.broadcasted_iota(jnp.int32, (block, block), 0).astype(jnp.float32)
-    key_pos[...] = slots.T + 128.0 * (block_row - stream_base)
-    lane = lax.broadcasted_iota(jnp.int32, (block, block), 1)
     lane8 = lax.broadcasted_iota(jnp.int32, (8, block), 1)
     row8 = lax.broadcasted_iota(jnp.int32, (8, block), 0)
+    for side, ref in enumerate((mine_ref, other_ref)):
+        for r in range(0, send_rows if side == 0 else head_rows, 8):
+            rows = jnp.transpose(ref[:, r : r + 8, :], (1, 0, 2))
+            if r >= head_rows:
+                at = (r - head_rows) * block
+                qg[at : at + 8 * block, :] = rows.reshape(8 * block, head)
+                continue
+            for i in range(0, min(8, kv_rows - r), 2):
+                at = (r + i + side) * block
+                kv[0, at : at + block, :] = rows[i]
+                kv[1, at : at + block, :] = rows[i + 1]
+            if side == 0 and r + 8 == head_rows:
+                slots = rows[kv_rows - r].astype(jnp.float32)
+                key_pos[...] = slots.T + 128.0 * (block_row - stream_base)
     plan = plan_ref[...]
-    dmine_ref[...] = jnp.zeros(dmine_ref.shape, jnp.float32)
-    dother_ref[...] = jnp.zeros(dother_ref.shape, jnp.float32)
+    dmine_ref[...] = jnp.zeros(dmine_ref.shape, jnp.bfloat16)
+    dother_ref[...] = jnp.zeros(dother_ref.shape, jnp.bfloat16)
+    span = 256 * step
 
     def planned(row, x):
         seat = (row8 == row) & (lane8 == chip + 64 * x)
         return jnp.sum(jnp.where(seat, plan, 0.0)).astype(jnp.int32)
 
-    def pair(m, half):
-        return jnp.concatenate([mine_ref[2 * m + half], other_ref[2 * m + half]], axis=0)
+    def some(half, m):
+        return kv[half, pl.ds(pl.multiple_of(m * span, span), span), :]
+
+    def add(ref, i, x):
+        ref[i] = (ref[i].astype(jnp.float32) + x).astype(jnp.bfloat16)
 
     for x in range(2):
         mine_block = planned(0, x)
         count = planned(1, x)
         if x == 0:
-            begin, end = jnp.int32(0), (count + 1) >> 1
+            begin, end = jnp.int32(0), (count + 2 * step - 1) // (2 * step)
             entry_low, entry_high = jnp.int32(0), count
             base = mine_block - count + 1
         else:
-            begin, end = (entries - count) >> 1, jnp.int32(pairs)
+            begin, end = (entries - count) // (2 * step), jnp.int32(pairs // step)
             entry_low, entry_high = entries - count, jnp.int32(entries)
             base = mine_block - (entries - 1)
-        slot = jnp.sum(jnp.where(lane == mine_block, slots, 0.0), axis=1, keepdims=True)
-        pos = jnp.broadcast_to(slot + 128.0 * (mine_block.astype(jnp.float32) - stream_base), (block, block))
-        start = jnp.zeros((block, block), jnp.float32)
+        pos = key_pos[pl.ds(mine_block, 1), :]
+        start = jnp.zeros((1, block), jnp.float32)
         doc_end = jnp.int32(0)
         for i in range(16):
             doc_end = doc_end + stream_length(core, mine_len, other_len, stream, i)
             f = doc_end.astype(jnp.float32)
             start = jnp.where(f <= pos, f, start)
-        bound[0] = pos
-        bound[1] = start
+        bound[0:1] = pos
+        bound[1:2] = start
         top[...] = jnp.full(top.shape, masked_score, jnp.float32)
         total[...] = jnp.zeros(total.shape, jnp.float32)
         acc[...] = jnp.zeros(acc.shape, jnp.float32)
@@ -230,70 +249,79 @@
 
         @pl.loop(begin, end)
         def _(m):
-            keys = pair(m, 0)
+            keys = some(0, m)
             bias = []
-            for par in (core, 1 - core):
-                entry = 2 * m + par
+            for u, par in [(u, par) for u in range(step) for par in (core, 1 - core)]:
+                entry = 2 * (m * step + u) + par
                 valid = (entry >= entry_low) & (entry < entry_high)
                 kp = key_pos[pl.ds(jnp.where(valid, base + entry, 0), 1), :]
-                kp = jnp.where(valid, kp, far)
-                bias.append(jnp.where((kp <= bound[0]) & (kp >= bound[1]), 0.0, masked_score))
-            bias = jnp.concatenate(bias, axis=1)
-            bias = jnp.concatenate([bias, bias], axis=0)
-            for h in range(2):
-                s = nt(qg_ref[q_at + h * 256 : q_at + (h + 1) * 256, :], keys) + bias
-                scores[m, h] = s
-                top[h] = jnp.maximum(top[h], jnp.maximum(s[:, :block], s[:, block:]))
-
-        for h in range(2):
-            peak = jnp.max(top[h], axis=1, keepdims=True)
-            top[h] = jnp.broadcast_to(peak * to_exp2, (256, block))
+                kp = jnp.broadcast_to(jnp.where(valid, kp, far), (block, block)).T
+                bias.append(jnp.where((kp <= bound[0:1]) & (kp >= bound[1:2]), 0.0, masked_score))
+            bias = jnp.concatenate(bias, axis=0)
+            bias = jnp.concatenate([bias] * 4, axis=1)
+            s = nt(keys, qg[q_at : q_at + 512, :]) + bias
+            scores[m] = s
+            top[...] = jnp.maximum(top[...], jnp.max(s.reshape(span // 8, 8, 512), axis=0))
+
+        top[...] = jnp.broadcast_to(jnp.max(top[...], axis=0, keepdims=True) * to_exp2, top.shape)
 
         @pl.loop(begin, end)
         def _(m):
-            values = pair(m, 1)
-            for h in range(2):
-                peak = top[h]
-                p = jnp.exp2(scores[m, h] * to_exp2 - jnp.concatenate([peak, peak], axis=1))
-                total[h] = total[h] + (p[:, :block] + p[:, block:])
-                half = p.astype(jnp.bfloat16)
-                weights[m, h] = half
-                acc[h] = acc[h] + jnp.dot(half, values, preferred_element_type=jnp.float32)
-
-        for h in range(2):
-            inv = 1.0 / jnp.sum(total[h], axis=1, keepdims=True)
-            o = (acc[h] * inv).astype(jnp.bfloat16)
-            out_ref[q_at + h * 256 : q_at + (h + 1) * 256, :] = o
-            g = qg_ref[g_at + h * 256 : g_at + (h + 1) * 256, :].astype(jnp.float32)
-            q = qg_ref[q_at + h * 256 : q_at + (h + 1) * 256, :].astype(jnp.float32)
+            p = jnp.exp2(scores[m] * to_exp2 - top[0:1])
+            total[...] = total[...] + jnp.sum(p.reshape(span // 8, 8, 512), axis=0)
+            half = p.astype(jnp.bfloat16)
+            weights[m] = half
+            acc[...] = acc[...] + tn(some(1, m), half)
+
+        inv = 1.0 / jnp.sum(total[...], axis=0, keepdims=True)
+        for h in range(4):
+            at = slice(h * block, (h + 1) * block)
+            q_rows = slice(q_at + h * block, q_at + (h + 1) * block)
+            inv_down = jnp.broadcast_to(inv[:, at], (block, block)).T
+            o = (acc[:, at].T * inv_down).astype(jnp.bfloat16)
+            out_ref[q_rows, :] = o
+            g = qg[g_at + h * block : g_at + (h + 1) * block, :].astype(jnp.float32)
+            q = qg[q_rows, :].astype(jnp.float32)
             d = jnp.sum(g * o.astype(jnp.float32), axis=1, keepdims=True)
-            dot[h] = jnp.broadcast_to(d, (256, block))
-            gs[h] = (g * inv).astype(jnp.bfloat16)
-            qs[h] = (q * (inv * scale)).astype(jnp.bfloat16)
-            total[h] = jnp.broadcast_to(inv * scale, (256, block))
-            acc[h] = jnp.zeros((256, head), jnp.float32)
+            dot[:, at] = jnp.broadcast_to(d, (block, block)).T[:8]
+            gs[at] = (g * inv_down).astype(jnp.bfloat16)
+            qs[at] = (q * (inv_down * scale)).astype(jnp.bfloat16)
+        total[...] = jnp.broadcast_to(inv * scale, total.shape)
+        acc[...] = jnp.zeros(acc.shape, jnp.float32)
 
         @pl.loop(begin, end)
         def _(m):
-            keys = pair(m, 0)
-            values = pair(m, 1)
-            dk = jnp.zeros((256, head), jnp.float32)
-            dv = jnp.zeros((256, head), jnp.float32)
-            for h in range(2):
-                gw = nt(qg_ref[g_at + h * 256 : g_at + (h + 1) * 256, :], values)
-                d = dot[h]
-                p = weights[m, h]
-                ds = (p.astype(jnp.float32) * (gw - jnp.concatenate([d, d], axis=1))).astype(jnp.bfloat16)
-                acc[h] = acc[h] + jnp.dot(ds, keys, preferred_element_type=jnp.float32)
-                dk = dk + tn(ds, qs[h])
-                dv = dv + tn(p, gs[h])
-            dmine_ref[2 * m] = dmine_ref[2 * m] + dk[:block]
-            dmine_ref[2 * m + 1] = dmine_ref[2 * m + 1] + dv[:block]
-            dother_ref[2 * m] = dother_ref[2 * m] + dk[block:]
-            dother_ref[2 * m + 1] = dother_ref[2 * m + 1] + dv[block:]
-
-        for h in range(2):
-            dq_ref[q_at + h * 256 : q_at + (h + 1) * 256, :] = (acc[h] * total[h]).astype(jnp.bfloat16)
+            gw = nt(some(1, m), qg[g_at : g_at + 512, :])
+            p = weights[m]
+            ds = (p.astype(jnp.float32) * (gw - dot[0:1])).astype(jnp.bfloat16)
+            acc[...] = acc[...] + tn(some(0, m), ds)
+            dk = nn(ds, qs[...])
+            dv = nn(p, gs[...])
+            for u in range(step):
+                i = 2 * (m * step + u)
+                add(dmine_ref, i, dk[u * 256 : u * 256 + block])
+                add(dmine_ref, i + 1, dv[u * 256 : u * 256 + block])
+                add(dother_ref, i, dk[u * 256 + block : (u + 1) * 256])
+                add(dother_ref, i + 1, dv[u * 256 + block : (u + 1) * 256])
+
+        for h in range(4):
+            at = slice(h * block, (h + 1) * block)
+            dq_ref[q_at + h * block : q_at + (h + 1) * block, :] = (acc[:, at] * total[0:1, at]).T.astype(jnp.bfloat16)
+
+
+def join_kernel(mine_ref, other_ref, out_ref, dq_ref, back_ref):
+    def put(r, rows):
+        back_ref[:, r : r + 8, :] = jnp.transpose(rows, (1, 0, 2))
+
+    for r in range(0, head_rows, 8):
+        n = min(8, kv_rows - r)
+        rows = mine_ref[r : r + n].astype(jnp.float32) + other_ref[r : r + n].astype(jnp.float32)
+        rows = rows.astype(jnp.bfloat16)
+        if n < 8:
+            rows = jnp.concatenate([rows, jnp.zeros((8 - n, block, head), jnp.bfloat16)], axis=0)
+        put(r, rows)
+    put(head_rows, out_ref[...].reshape(8, block, head))
+    put(head_rows + 8, dq_ref[...].reshape(8, block, head))
 
 
 def vmem(n):
@@ -304,7 +332,8 @@
     return pl.BlockSpec(memory_space=pltpu.SMEM)
 
 
-params = pltpu.CompilerParams(vmem_limit_bytes=vmem_bytes)
+def params(size):
+    return pltpu.CompilerParams(vmem_limit_bytes=size * mib)
 
 
 def swap(x):
@@ -318,7 +347,6 @@
 def on_device(queries, keys_values, grad_out, placement, doc_lengths):
     bf16, f32 = jnp.bfloat16, jnp.float32
     place = placement.reshape(1, block)
-    where = jnp.stack([lax.axis_index("dp"), lax.axis_index("ctx")]).astype(jnp.int32)
     other_lengths = swap(doc_lengths)
     sent, plan = pl.pallas_call(
         pack_kernel,
@@ -326,51 +354,47 @@
             jax.ShapeDtypeStruct((128, send_rows, head), bf16),
             jax.ShapeDtypeStruct((8, block), f32),
         ),
-        in_specs=[smem()] * 3 + vmem(4),
+        in_specs=[smem()] * 2 + vmem(4),
         out_specs=tuple(vmem(2)),
-        compiler_params=params,
+        compiler_params=params(24),
         name="pack",
-    )(where, doc_lengths, other_lengths, place, queries, keys_values, grad_out)
-    got = exchange(sent).transpose(1, 0, 2)
-    mine = got[:kv_rows]
-    info = got[kv_rows:head_rows]
-    qg = got[head_rows:].reshape(2048, head)
-    other = swap(mine)
+    )(doc_lengths, other_lengths, place, queries, keys_values, grad_out)
+    got = exchange(sent)
     dmine, dother, out, dq = pl.pallas_call(
         attention_kernel,
         out_shape=(
-            jax.ShapeDtypeStruct((kv_rows, block, head), f32),
-            jax.ShapeDtypeStruct((kv_rows, block, head), f32),
+            jax.ShapeDtypeStruct((kv_rows, block, head), bf16),
+            jax.ShapeDtypeStruct((kv_rows, block, head), bf16),
             jax.ShapeDtypeStruct((1024, head), bf16),
             jax.ShapeDtypeStruct((1024, head), bf16),
         ),
-        in_specs=[smem()] * 3 + vmem(5),
+        in_specs=[smem()] * 2 + vmem(3),
         out_specs=tuple(vmem(4)),
         scratch_shapes=[
-            pltpu.VMEM((pairs, 2, 256, 256), f32),
-            pltpu.VMEM((pairs, 2, 256, 256), bf16),
-            pltpu.VMEM((2, 256, block), f32),
-            pltpu.VMEM((2, 256, block), f32),
-            pltpu.VMEM((2, 256, head), f32),
-            pltpu.VMEM((2, 256, block), f32),
-            pltpu.VMEM((2, 256, head), bf16),
-            pltpu.VMEM((2, 256, head), bf16),
+            pltpu.VMEM((2, entries * block, head), bf16),
+            pltpu.VMEM((2048, head), bf16),
+            pltpu.VMEM((pairs // step, 256 * step, 512), f32),
+            pltpu.VMEM((pairs // step, 256 * step, 512), bf16),
+            pltpu.VMEM((8, 512), f32),
+            pltpu.VMEM((8, 512), f32),
+            pltpu.VMEM((head, 512), f32),
+            pltpu.VMEM((8, 512), f32),
+            pltpu.VMEM((512, head), bf16),
+            pltpu.VMEM((512, head), bf16),
             pltpu.VMEM((block, block), f32),
-            pltpu.VMEM((2, block, block), f32),
+            pltpu.VMEM((8, block), f32),
         ],
-        compiler_params=params,
+        compiler_params=params(48),
         name="attention",
-    )(where, doc_lengths, other_lengths, plan, mine, other, info, qg)
-    terms = (dmine + swap(dother.astype(bf16)).astype(f32)).astype(bf16)
-    back = jnp.concatenate(
-        [
-            terms,
-            jnp.zeros((head_rows - kv_rows, block, head), bf16),
-            out.reshape(8, block, head),
-            dq.reshape(8, block, head),
-        ],
-        axis=0,
-    ).transpose(1, 0, 2)
+    )(doc_lengths, other_lengths, plan, got, swap(got))
+    back = pl.pallas_call(
+        join_kernel,
+        out_shape=jax.ShapeDtypeStruct((128, send_rows, head), bf16),
+        in_specs=vmem(4),
+        out_specs=vmem(1)[0],
+        compiler_params=params(24),
+        name="join",
+    )(dmine, swap(dother), out, dq)
     returned = exchange(back)
     return pl.pallas_call(
         unpack_kernel,
@@ -381,7 +405,7 @@
         ),
         in_specs=vmem(3),
         out_specs=tuple(vmem(3)),
-        compiler_params=params,
+        compiler_params=params(24),
         name="unpack",
     )(place, plan, returned)
 

time: 121 us -> 106 us (0.88)
  Pallas kernels: 35.7 us -> 22.8 us
  other arithmetic: 5.87 us -> 0 us
  waiting for transfers between devices: 3.3 us -> 6.84 us
  local copies, waits for them, and re-layouts: 4.01 us -> 5.31 us
    pallas_call x1, Pallas kernels: 27.3 us -> 17 us  [on_device(): pl.pallas_call(attention_kernel, out_shape=(jax.ShapeDtypeStruct((kv_rows...]
    convert_element_type x3 -> x0, other arithmetic: 4.77 us -> none  [on_device(): terms = (dmine + swap(dother.astype(bf16)).astype(f32)).astype(bf16)]
    unnamed x12 -> x16, local copies, waits for them, and re-layouts: 1.57 us -> 5.31 us
    ppermute x3, waiting for transfers between devices: 3.3 us -> 6.84 us  [swap(): return lax.ppermute(x, 'dp', [(0, 1), (1, 0)])]
    pallas_call x1, Pallas kernels: 4.35 us -> 2.56 us  [on_device(): pl.pallas_call(pack_kernel, out_shape=(jax.ShapeDtypeStruct((128, send_ro...]
    slice x3 -> x0, local copies, waits for them, and re-layouts: 1.57 us -> none  [the longest x1 0.83 us: on_device(): qg = got[head_rows:].reshape(2048, head)]
    pallas_call x1, Pallas kernels: 4.02 us -> 2.49 us  [on_device(): pl.pallas_call(unpack_kernel, out_shape=(jax.ShapeDtypeStruct((block, 8 *...]
  transfers between devices with their start and end apart: 3 -> 3, of which waited for: 3 -> 3; matrix products, arithmetic and copies ran while one was open for 2% -> 0% of each run, Pallas kernels for 0% -> 0%
where the time goes in v3:
time: 106 us
  blocking collectives  67.4 us (64%)
  Pallas kernels  22.8 us (22%)
  waiting for transfers between devices  6.84 us (6%)
  local copies, waits for them, and re-layouts  5.31 us (5%)
  starting transfers between devices  2.95 us (3%)
    all_to_all x2, blocking collectives, exchange(): lax.all_to_all(x, ('dp', 'ctx'), split_axis=0, concat_axis=0, tiled=True)  67.4 us
    pallas_call x1, Pallas kernels, on_device(): pl.pallas_call(attention_kernel, out_shape=(jax.ShapeDtypeStruct((kv_rows...  17 us
    ppermute x3, waiting for transfers between devices, swap(): return lax.ppermute(x, 'dp', [(0, 1), (1, 0)])  6.84 us
    unnamed x16, local copies, waits for them, and re-layouts  5.31 us
    ppermute x3, starting transfers between devices, swap(): return lax.ppermute(x, 'dp', [(0, 1), (1, 0)])  2.95 us
    pallas_call x1, Pallas kernels, on_device(): pl.pallas_call(pack_kernel, out_shape=(jax.ShapeDtypeStruct((128, send_ro...  2.56 us
    pallas_call x1, Pallas kernels, on_device(): pl.pallas_call(unpack_kernel, out_shape=(jax.ShapeDtypeStruct((block, 8 *...  2.49 us
  transfers between devices with their start and end apart: 3, of which 3 were waited for; matrix products, arithmetic and copies ran while one was open for 0% of the time, Pallas kernels for 0%

profile of v3, /device:TPU:1, one launch (start us, length us, event | category | flops | bytes accessed | tf_op | source)
XLA Modules:
  0.0 105.9 jit_solution(13340410879022991464)
XLA Ops:
  0.6 1.5 %collective-permute-start = (s32[1,16]{1,0:T(1,128)}, s32[1,16]{1,0:T(1,128)S(1)}, u32[]{:S(2)}, u32[]{:S(2)}) collective-permute-start(s32[1,16]{1,0:T(1,128)} %mine_len.1), channel_id=1, source_target_pairs={{0,64},{64,0},{1,65},{65,1},{2,66},{66,2},{3,67},{67,3},{4,68},{68... | collective-permute-start | bytes 200 | tf_op jit(solution)/shard_map/ppermute | solution.py:340
  2.1 1.0 collective-permute-done.other_ref.other_len
  3.1 0.0 copy-start
  3.1 0.9 copy-done
  4.0 0.0 copy-start.1
  4.0 0.9 copy-done.1
  5.0 0.8 copy-done.2
  5.8 0.7 copy-done.3
  6.5 0.7 copy-done.5
  7.1 2.6 %pack.1 = (bf16[128,56,128]{2,1,0:T(8,128)(2,1)S(1)}, f32[8,128]{1,0:T(8,128)S(1)}) custom-call(s32[1,16]{1,0:T(1,128)S(1)} %copy-done.3, s32[1,16]{1,0:T(1,128)S(1)} %collective-permute-done.other_ref.other_len, s32[1,128]{1,0:T(1,128)S(1)} %bitcast.1, bf16[128,1024]{1,0:T(8,128)(2,1)S(1)} %copy-done, bf16[128,256]{1,0:T(8,128)(2,1)S(1)} %copy-done.2, ...), custom_call_target="tpu_custom_call" | custom-call | tf_op jit(solution)/shard_map/pack/pallas_call | solution.py:351
  9.7 0.0 copy-start.4
  9.7 37.1 %all_to_all.10.mine_ref = bf16[128,56,128]{2,1,0:T(8,128)(2,1)S(1)} all-to-all(bf16[128,56,128]{2,1,0:T(8,128)(2,1)S(1)} %get-tuple-element.10), channel_id=1, replica_groups=mesh['dp'=2,'ctx'=64] {'dp','ctx'}, dimensions={0} | all-to-all | bytes 3670016 | tf_op jit(solution)/shard_map/all_to_all | solution.py:344
  46.8 1.0 collective-permute-start.1
  47.8 3.4 %collective-permute-done.1.other_ref = bf16[128,56,128]{2,1,0:T(8,128)(2,1)S(1)} collective-permute-done((bf16[128,56,128]{2,1,0:T(8,128)(2,1)S(1)}, bf16[128,56,128]{2,1,0:T(8,128)(2,1)S(1)}, u32[]{:S(2)}, u32[]{:S(2)}) %collective-permute-start.1) | collective-permute-done | bytes 1835040 | tf_op jit(solution)/shard_map/ppermute | solution.py:340
  51.2 1.2 %copy-done.7 = bf16[128,56,128]{2,1,0:T(8,128)(2,1)} copy-done((bf16[128,56,128]{2,1,0:T(8,128)(2,1)}, bf16[128,56,128]{2,1,0:T(8,128)(2,1)S(1)}, u32[]{:S(2)}) %copy-start.7) | copy-done | bytes 1835032
  52.5 0.0 copy-done.4
  52.5 17.0 %attention.1 = (bf16[36,128,128]{2,1,0:T(8,128)(2,1)S(1)}, bf16[36,128,128]{2,1,0:T(8,128)(2,1)S(1)}, bf16[1024,128]{1,0:T(8,128)(2,1)S(1)}, bf16[1024,128]{1,0:T(8,128)(2,1)S(1)}) custom-call(s32[1,16]{1,0:T(1,128)S(1)} %copy-done.4, s32[1,16]{1,0:T(1,128)S(1)} %collective-permute-done.other_ref.other_len, f32[8,128]{1,0:T(8,128)S(1)} %get-tuple-element.9.plan_ref, ...), custom_call_target="tpu_custom_call" | custom-call | tf_op jit(solution)/shard_map/attention/pallas_call | solution.py:363
  69.5 0.5 collective-permute-start.2
  69.9 2.5 %collective-permute-done.2.other_ref = bf16[36,128,128]{2,1,0:T(8,128)(2,1)S(1)} collective-permute-done((bf16[36,128,128]{2,1,0:T(8,128)(2,1)S(1)}, bf16[36,128,128]{2,1,0:T(8,128)(2,1)S(1)}, u32[]{:S(2)}, u32[]{:S(2)}) %collective-permute-start.2) | collective-permute-done | bytes 1179680 | tf_op jit(solution)/shard_map/ppermute | solution.py:340
  72.4 0.7 join.1
  73.1 0.0 copy-start.6
  73.1 30.3 %all_to_all.11.got_ref = bf16[128,56,128]{2,1,0:T(8,128)(2,1)S(1)} all-to-all(bf16[128,56,128]{2,1,0:T(8,128)(2,1)S(1)} %join.1), channel_id=1, replica_groups=mesh['dp'=2,'ctx'=64] {'dp','ctx'}, dimensions={0} | all-to-all | bytes 3670016 | tf_op jit(solution)/shard_map/all_to_all | solution.py:344
  103.4 0.0 copy-done.6
  103.4 2.5 %unpack.1 = (bf16[128,1024]{1,0:T(8,128)(2,1)}, bf16[128,1024]{1,0:T(8,128)(2,1)}, bf16[128,256]{1,0:T(8,128)(2,1)}) custom-call(s32[1,128]{1,0:T(1,128)S(1)} %bitcast.2, f32[8,128]{1,0:T(8,128)S(1)} %get-tuple-element.9.plan_ref, bf16[128,56,128]{2,1,0:T(8,128)(2,1)S(1)} %all_to_all.11.got_ref), custom_call_target="tpu_custom_call" | custom-call | tf_op jit(solution)/shard_map/unpack/pallas_call | solution.py:399
  (4 shorter events, 0.0 us)
Async XLA Ops:
  0.6 2.5 %collective-permute-start = (s32[1,16]{1,0:T(1,128)}, s32[1,16]{1,0:T(1,128)S(1)}, u32[]{:S(2)}, u32[]{:S(2)}) collective-permute-start(s32[1,16]{1,0:T(1,128)} %mine_len.1), channel_id=1, source_target_pairs={{0,64},{64,0},{1,65},{65,1},{2,66},{66,2},{3,67},{67,3},{4,68},{68... | collective-permute-start | bytes 200 | tf_op jit(solution)/shard_map/ppermute | solution.py:340
  3.1 0.9 copy-start
  4.0 0.9 copy-start.1
  5.0 0.8 copy-start.2
  5.8 0.7 copy-start.3
  6.5 0.7 copy-start.5
  9.7 42.8 %copy-start.4 = (s32[1,16]{1,0:T(1,128)S(1)}, s32[1,16]{1,0:T(1,128)}, u32[]{:S(2)}) copy-start(s32[1,16]{1,0:T(1,128)} %mine_len.1) | copy-start | bytes 196
  46.8 4.4 %collective-permute-start.1 = (bf16[128,56,128]{2,1,0:T(8,128)(2,1)S(1)}, bf16[128,56,128]{2,1,0:T(8,128)(2,1)S(1)}, u32[]{:S(2)}, u32[]{:S(2)}) collective-permute-start(bf16[128,56,128]{2,1,0:T(8,128)(2,1)S(1)} %all_to_all.10.mine_ref), channel_id=1, source_target_pairs={{0,64},{64,0},{1,65},{65,1},{2,66},{66,2},{3,67},{67,3},{4,68},{68... | collective-permute-start | bytes 5505032 | tf_op jit(solution)/shard_map/ppermute | solution.py:340
  51.2 1.3 %copy-start.7 = (bf16[128,56,128]{2,1,0:T(8,128)(2,1)}, bf16[128,56,128]{2,1,0:T(8,128)(2,1)S(1)}, u32[]{:S(2)}) copy-start(bf16[128,56,128]{2,1,0:T(8,128)(2,1)S(1)} %collective-permute-done.1.other_ref) | copy-start | bytes 5505028
  69.5 2.9 %collective-permute-start.2 = (bf16[36,128,128]{2,1,0:T(8,128)(2,1)S(1)}, bf16[36,128,128]{2,1,0:T(8,128)(2,1)S(1)}, u32[]{:S(2)}, u32[]{:S(2)}) collective-permute-start(bf16[36,128,128]{2,1,0:T(8,128)(2,1)S(1)} %get-tuple-element.12), channel_id=1, source_target_pairs={{0,64},{64,0},{1,65},{65,1},{2,66},{66,2},{3,67},{67,3},{4,68},{68... | collective-permute-start | bytes 3538952 | tf_op jit(solution)/shard_map/ppermute | solution.py:340
  73.1 30.3 %copy-start.6 = (s32[128]{0:T(128)S(1)}, s32[128]{0:T(128)}, u32[]{:S(2)}) copy-start(s32[128]{0:T(128)} %param.8) | copy-start | bytes 1540

commit v4 on v3

--- a/solution.py
+++ b/solution.py
@@ -56,7 +56,27 @@
     return block_line, count_line
 
 
-def pack_kernel(mine_ref, other_ref, place_ref, q_ref, kv_ref, g_ref, out_ref, plan_ref):
+def pack_kernel(
+    mine_hbm, other_hbm, place_hbm, q_hbm, kv_hbm, g_hbm, out_hbm, plan_ref,
+    mine_ref, other_ref, place_ref, q_ref, kv_ref, g_ref, out_ref, sems,
+):
+    moves = [
+        pltpu.make_async_copy(src, dst, sems.at[i])
+        for i, (src, dst) in enumerate(
+            [
+                (mine_hbm, mine_ref),
+                (other_hbm, other_ref),
+                (place_hbm, place_ref),
+                (kv_hbm, kv_ref),
+                (q_hbm, q_ref),
+                (g_hbm, g_ref),
+            ]
+        )
+    ]
+    for move in moves:
+        move.start()
+    for move in moves[:3]:
+        move.wait()
     block_line, count_line = make_plan(lax.axis_index("dp"), mine_ref, other_ref)
     row8 = lax.broadcasted_iota(jnp.int32, (8, block), 0)
     plan_ref[...] = jnp.where(row8 == 0, block_line, jnp.where(row8 == 1, count_line, 0.0))
@@ -67,48 +87,57 @@
     slots_down = down(place_ref[...] & (block - 1))
     slot_line = jnp.sum(jnp.where(down(rows) == lane.astype(jnp.float32), slots_down, 0.0), axis=0, keepdims=True)
     extra = jnp.where(row8 == kv_rows % 8, slot_line, 0.0)
+    moves[3].wait()
     kv = jnp.concatenate([kv_ref[:, :head], kv_ref[:, head:]], axis=0)
     r = lax.broadcasted_iota(jnp.int32, (group, head_rows, block), 1)
     half = (r & 1) * other_half
-    for t in range(0, 128, group):
-        core, chip = t // 64, t % 64
-
-        def spread(x):
-            return jnp.broadcast_to(x[:, None, :], (group, head_rows, block))
-
+    j = lax.broadcasted_iota(jnp.int32, (group, 8, block), 1)
+    moves[4].wait()
+    moves[5].wait()
+    both = []
+    for core in range(2):
+        heads = [slice((4 * core + h) * head, (4 * core + h + 1) * head) for h in range(4)]
+        both.append(jnp.concatenate([jnp.concatenate([q_ref[:, at], g_ref[:, at]], axis=1) for at in heads], axis=0))
+
+    def spread(x, n):
+        return jnp.broadcast_to(x[:, None, :], (group, n, block))
+
+    sends = []
+    for chip in range(0, 64, group):
         first = block_down[chip : chip + group]
         first_count = count_down[chip : chip + group]
         second = block_down[64 + chip : 64 + chip + group]
         second_count = count_down[64 + chip : 64 + chip + group]
-        entry = (r & -2) + core
-        code = jnp.where(
-            entry < spread(first_count),
-            entry + spread(first - first_count + 1),
-            jnp.where(entry >= spread(entries - second_count), entry + spread(second - (entries - 1)), nothing),
-        )
-        code = (jnp.where(r < kv_rows, code, nothing) + half).reshape(group * head_rows, block)
-        pick = jnp.concatenate([one_hot(code == rows), one_hot(code == rows + other_half)], axis=1)
-        got = jnp.dot(pick, kv, preferred_element_type=jnp.float32).reshape(group, head_rows, head)
-        tail = got[:, head_rows - 8 :, :] + extra[None]
-        got = jnp.concatenate([got[:, : head_rows - 8, :], tail], axis=1)
-        out_ref[t : t + group, :head_rows, :] = got.astype(jnp.bfloat16)
-    j = lax.broadcasted_iota(jnp.int32, (group, 8, block), 1)
-    both = []
-    for core in range(2):
-        heads = [slice((4 * core + h) * head, (4 * core + h + 1) * head) for h in range(4)]
-        both.append(jnp.concatenate([jnp.concatenate([q_ref[:, at], g_ref[:, at]], axis=1) for at in heads], axis=0))
-    for c in range(0, 64, group):
-        first = jnp.broadcast_to(block_down[c : c + group][:, None, :], (group, 8, block))
-        second = jnp.broadcast_to(block_down[64 + c : 64 + c + group][:, None, :], (group, 8, block))
-        mine = jnp.where(j < 4, first, second) == rows[None]
-        pick = jnp.concatenate(
-            [one_hot(mine & ((j & 3) == h)).reshape(group * 8, block) for h in range(4)], axis=1
+        wanted = jnp.where(j < 4, spread(first, 8), spread(second, 8)) == rows[None]
+        heads = jnp.concatenate(
+            [one_hot(wanted & ((j & 3) == h)).reshape(group * 8, block) for h in range(4)], axis=1
         )
         for core in range(2):
-            got = jnp.dot(pick, both[core], preferred_element_type=jnp.float32).astype(jnp.bfloat16)
-            t = core * 64 + c
+            t = core * 64 + chip
+            entry = (r & -2) + core
+            code = jnp.where(
+                entry < spread(first_count, head_rows),
+                entry + spread(first - first_count + 1, head_rows),
+                jnp.where(
+                    entry >= spread(entries - second_count, head_rows),
+                    entry + spread(second - (entries - 1), head_rows),
+                    nothing,
+                ),
+            )
+            code = (jnp.where(r < kv_rows, code, nothing) + half).reshape(group * head_rows, block)
+            pick = jnp.concatenate([one_hot(code == rows), one_hot(code == rows + other_half)], axis=1)
+            got = jnp.dot(pick, kv, preferred_element_type=jnp.float32).reshape(group, head_rows, head)
+            tail = got[:, head_rows - 8 :, :] + extra[None]
+            got = jnp.concatenate([got[:, : head_rows - 8, :], tail], axis=1)
+            out_ref[t : t + group, :head_rows, :] = got.astype(jnp.bfloat16)
+            got = jnp.dot(heads, both[core], preferred_element_type=jnp.float32).astype(jnp.bfloat16)
             out_ref[t : t + group, head_rows : head_rows + 8, :] = got[:, :head].reshape(group, 8, head)
             out_ref[t : t + group, head_rows + 8 :, :] = got[:, head:].reshape(group, 8, head)
+            at = pl.ds(t, group)
+            sends.append(pltpu.make_async_copy(out_ref.at[at], out_hbm.at[at], sems.at[6 + len(sends)]))
+            sends[-1].start()
+    for send in sends:
+        send.wait()
 
 
 def spread_lanes(plan, width):
@@ -117,7 +146,13 @@
     return jnp.dot(plan, one_hot((lane >= chip) & (lane < chip + width)), preferred_element_type=jnp.float32)
 
 
-def unpack_kernel(place_ref, plan_ref, got_ref, out_ref, dq_ref, dkv_ref):
+def unpack_kernel(
+    place_ref, plan_ref, got_ref, out_hbm, dq_hbm, dkv_hbm, out_ref, dq_ref, dkv_ref, sems
+):
+    moves = [
+        pltpu.make_async_copy(src, dst, sems.at[i])
+        for i, (src, dst) in enumerate([(out_ref, out_hbm), (dq_ref, dq_hbm), (dkv_ref, dkv_hbm)])
+    ]
     rows_down = down(place_ref[...] >> 7)
     plan = plan_ref[...]
     lane = lax.broadcasted_iota(jnp.int32, (8, block), 1)
@@ -129,6 +164,26 @@
     for i, line in enumerate(lines):
         stacked = jnp.where((row == i) & (lane[0:1] < 64), line, stacked)
     stacked = stacked.astype(jnp.bfloat16)
+    wide = spread_lanes(stacked, 8)
+    j = lax.broadcasted_iota(jnp.int32, (1, 512), 1) & 7
+    code = jnp.where(j < 4, wide[0:1], wide[2:3])
+    rows_wide = jnp.concatenate([rows_down] * 4, axis=1)
+    picks = [one_hot(jnp.where((j & 3) == h, code, float(nothing)) == rows_wide) for h in range(4)]
+    for core in range(2):
+        both = jnp.concatenate(
+            [
+                got_ref[core * 64 : core * 64 + 64, head_rows : head_rows + 8, :].reshape(512, head),
+                got_ref[core * 64 : core * 64 + 64, head_rows + 8 :, :].reshape(512, head),
+            ],
+            axis=1,
+        )
+        for h in range(4):
+            got = jnp.dot(picks[h], both, preferred_element_type=jnp.float32).astype(jnp.bfloat16)
+            at = (4 * core + h) * head
+            out_ref[:, at : at + head] = got[:, :head]
+            dq_ref[:, at : at + head] = got[:, head:]
+    moves[0].start()
+    moves[1].start()
     wide = spread_lanes(stacked, head_rows)
     first, first_count, second, second_count, chip = [wide[i : i + 1] for i in range(5)]
     r = lax.broadcasted_iota(jnp.int32, (1, 64 * head_rows), 1) - head_rows * chip.astype(jnp.int32)
@@ -147,24 +202,9 @@
             pick = one_hot(jnp.where((r & 1) == half, code, float(nothing)) == rows_wide)
             sums[half] = sums[half] + jnp.dot(pick, terms, preferred_element_type=jnp.float32)
     dkv_ref[...] = jnp.concatenate(sums, axis=1).astype(jnp.bfloat16)
-    wide = spread_lanes(stacked, 8)
-    j = lax.broadcasted_iota(jnp.int32, (1, 512), 1) & 7
-    code = jnp.where(j < 4, wide[0:1], wide[2:3])
-    rows_wide = jnp.concatenate([rows_down] * 4, axis=1)
-    picks = [one_hot(jnp.where((j & 3) == h, code, float(nothing)) == rows_wide) for h in range(4)]
-    for core in range(2):
-        both = jnp.concatenate(
-            [
-                got_ref[core * 64 : core * 64 + 64, head_rows : head_rows + 8, :].reshape(512, head),
-                got_ref[core * 64 : core * 64 + 64, head_rows + 8 :, :].reshape(512, head),
-            ],
-            axis=1,
-        )
-        for h in range(4):
-            got = jnp.dot(picks[h], both, preferred_element_type=jnp.float32).astype(jnp.bfloat16)
-            at = (4 * core + h) * head
-            out_ref[:, at : at + head] = got[:, :head]
-            dq_ref[:, at : at + head] = got[:, head:]
+    moves[2].start()
+    for move in moves:
+        move.wait()
 
 
 def nt(a, b):
@@ -179,10 +219,23 @@
     return jnp.dot(a, b, preferred_element_type=jnp.float32)
 
 
+def split_kernel(got_ref, kv_ref, info_ref, qg_ref):
+    for r in range(0, send_rows, 8):
+        rows = jnp.transpose(got_ref[:, r : r + 8, :], (1, 0, 2))
+        if r < kv_rows:
+            n = min(8, kv_rows - r)
+            kv_ref[r : r + n] = rows[:n]
+            if n < 8:
+                info_ref[...] = rows[n]
+        else:
+            at = (r - head_rows) * block
+            qg_ref[at : at + 8 * block, :] = rows.reshape(8 * block, head)
+
+
 def attention_kernel(
-    mine_len, other_len, plan_ref, mine_ref, other_ref,
+    mine_len, other_len, plan_ref, mine_ref, other_ref, info_ref, qg,
     dmine_ref, dother_ref, out_ref, dq_ref,
-    kv, qg, scores, weights, top, total, acc, dot, qs, gs, key_pos, bound,
+    kv, scores, weights, top, total, acc, dot, qs, gs, key_pos, bound,
 ):
     core = lax.axis_index("dp")
     chip = lax.axis_index("ctx")
@@ -193,20 +246,12 @@
     block_row = lax.broadcasted_iota(jnp.int32, (block, block), 0).astype(jnp.float32)
     lane8 = lax.broadcasted_iota(jnp.int32, (8, block), 1)
     row8 = lax.broadcasted_iota(jnp.int32, (8, block), 0)
-    for side, ref in enumerate((mine_ref, other_ref)):
-        for r in range(0, send_rows if side == 0 else head_rows, 8):
-            rows = jnp.transpose(ref[:, r : r + 8, :], (1, 0, 2))
-            if r >= head_rows:
-                at = (r - head_rows) * block
-                qg[at : at + 8 * block, :] = rows.reshape(8 * block, head)
-                continue
-            for i in range(0, min(8, kv_rows - r), 2):
-                at = (r + i + side) * block
-                kv[0, at : at + block, :] = rows[i]
-                kv[1, at : at + block, :] = rows[i + 1]
-            if side == 0 and r + 8 == head_rows:
-                slots = rows[kv_rows - r].astype(jnp.float32)
-                key_pos[...] = slots.T + 128.0 * (block_row - stream_base)
+    slots = info_ref[...].astype(jnp.float32)
+    key_pos[...] = slots.T + 128.0 * (block_row - stream_base)
+    for i in range(pairs):
+        for half in range(2):
+            kv[half, 2 * i * block : (2 * i + 1) * block, :] = mine_ref[2 * i + half]
+            kv[half, (2 * i + 1) * block : (2 * i + 2) * block, :] = other_ref[2 * i + half]
     plan = plan_ref[...]
     dmine_ref[...] = jnp.zeros(dmine_ref.shape, jnp.bfloat16)
     dother_ref[...] = jnp.zeros(dother_ref.shape, jnp.bfloat16)
@@ -354,12 +399,33 @@
             jax.ShapeDtypeStruct((128, send_rows, head), bf16),
             jax.ShapeDtypeStruct((8, block), f32),
         ),
-        in_specs=[smem()] * 2 + vmem(4),
-        out_specs=tuple(vmem(2)),
-        compiler_params=params(24),
+        in_specs=[pl.BlockSpec(memory_space=pl.ANY)] * 6,
+        out_specs=(pl.BlockSpec(memory_space=pl.ANY), vmem(1)[0]),
+        scratch_shapes=[
+            pltpu.SMEM((1, 16), jnp.int32),
+            pltpu.SMEM((1, 16), jnp.int32),
+            pltpu.VMEM((1, block), jnp.int32),
+            pltpu.VMEM((block, 8 * head), bf16),
+            pltpu.VMEM((block, 2 * head), bf16),
+            pltpu.VMEM((block, 8 * head), bf16),
+            pltpu.VMEM((128, send_rows, head), bf16),
+            pltpu.SemaphoreType.DMA((6 + 128 // group,)),
+        ],
+        compiler_params=pltpu.CompilerParams(vmem_limit_bytes=58 * mib),
         name="pack",
     )(doc_lengths, other_lengths, place, queries, keys_values, grad_out)
-    got = exchange(sent)
+    mine, info, qg = pl.pallas_call(
+        split_kernel,
+        out_shape=(
+            jax.ShapeDtypeStruct((kv_rows, block, head), bf16),
+            jax.ShapeDtypeStruct((block, head), bf16),
+            jax.ShapeDtypeStruct((2048, head), bf16),
+        ),
+        in_specs=vmem(1),
+        out_specs=tuple(vmem(3)),
+        compiler_params=params(24),
+        name="split",
+    )(exchange(sent))
     dmine, dother, out, dq = pl.pallas_call(
         attention_kernel,
         out_shape=(
@@ -368,11 +434,10 @@
             jax.ShapeDtypeStruct((1024, head), bf16),
             jax.ShapeDtypeStruct((1024, head), bf16),
         ),
-        in_specs=[smem()] * 2 + vmem(3),
+        in_specs=[smem()] * 2 + vmem(5),
         out_specs=tuple(vmem(4)),
         scratch_shapes=[
             pltpu.VMEM((2, entries * block, head), bf16),
-            pltpu.VMEM((2048, head), bf16),
             pltpu.VMEM((pairs // step, 256 * step, 512), f32),
             pltpu.VMEM((pairs // step, 256 * step, 512), bf16),
             pltpu.VMEM((8, 512), f32),
@@ -384,9 +449,9 @@
             pltpu.VMEM((block, block), f32),
             pltpu.VMEM((8, block), f32),
         ],
-        compiler_params=params(48),
+        compiler_params=params(32),
         name="attention",
-    )(doc_lengths, other_lengths, plan, got, swap(got))
+    )(doc_lengths, other_lengths, plan, mine, swap(mine), info, qg)
     back = pl.pallas_call(
         join_kernel,
         out_shape=jax.ShapeDtypeStruct((128, send_rows, head), bf16),
@@ -404,7 +469,13 @@
             jax.ShapeDtypeStruct((block, 2 * head), bf16),
         ),
         in_specs=vmem(3),
-        out_specs=tuple(vmem(3)),
+        out_specs=tuple([pl.BlockSpec(memory_space=pl.ANY)] * 3),
+        scratch_shapes=[
+            pltpu.VMEM((block, 8 * head), bf16),
+            pltpu.VMEM((block, 8 * head), bf16),
+            pltpu.VMEM((block, 2 * head), bf16),
+            pltpu.SemaphoreType.DMA((3,)),
+        ],
         compiler_params=params(24),
         name="unpack",
     )(place, plan, returned)

time: 106 us -> 101 us (0.953)
  local copies, waits for them, and re-layouts: 5.31 us -> 0.53 us
    unnamed x16 -> x10, local copies, waits for them, and re-layouts: 5.31 us -> 0.53 us
    pallas_call x1, Pallas kernels: 17 us -> 15.3 us  [on_device(): pl.pallas_call(attention_kernel, out_shape=(jax.ShapeDtypeStruct((kv_rows...]
    pallas_call x1, Pallas kernels: 2.56 us -> 3.97 us  [on_device(): pl.pallas_call(pack_kernel, out_shape=(jax.ShapeDtypeStruct((128, send_ro...]
where the time goes in v4:
time: 101 us
  blocking collectives  67.6 us (67%)
  Pallas kernels  22.9 us (23%)
  waiting for transfers between devices  5.9 us (6%)
  starting transfers between devices  3.04 us (3%)
    all_to_all x2, blocking collectives, exchange(): lax.all_to_all(x, ('dp', 'ctx'), split_axis=0, concat_axis=0, tiled=True)  67.6 us
    pallas_call x1, Pallas kernels, on_device(): pl.pallas_call(attention_kernel, out_shape=(jax.ShapeDtypeStruct((kv_rows...  15.3 us
    ppermute x3, waiting for transfers between devices, swap(): return lax.ppermute(x, 'dp', [(0, 1), (1, 0)])  5.9 us
    pallas_call x1, Pallas kernels, on_device(): pl.pallas_call(pack_kernel, out_shape=(jax.ShapeDtypeStruct((128, send_ro...  3.97 us
    ppermute x3, starting transfers between devices, swap(): return lax.ppermute(x, 'dp', [(0, 1), (1, 0)])  3.04 us
    pallas_call x1, Pallas kernels, on_device(): pl.pallas_call(unpack_kernel, out_shape=(jax.ShapeDtypeStruct((block, 8 *...  2.44 us
  transfers between devices with their start and end apart: 3, of which 3 were waited for; matrix products, arithmetic and copies ran while one was open for 0% of the time, Pallas kernels for 0%

profile of v4, /device:TPU:1, one launch (start us, length us, event | category | flops | bytes accessed | tf_op | source)
XLA Modules:
  0.0 100.6 jit_solution(645285852417210303)
XLA Ops:
  0.6 1.5 %collective-permute-start = (s32[1,16]{1,0:T(1,128)}, s32[1,16]{1,0:T(1,128)S(1)}, u32[]{:S(2)}, u32[]{:S(2)}) collective-permute-start(s32[1,16]{1,0:T(1,128)} %mine_len.1), channel_id=1, source_target_pairs={{0,64},{64,0},{1,65},{65,1},{2,66},{66,2},{3,67},{67,3},{4,68},{68... | collective-permute-start | bytes 200 | tf_op jit(solution)/shard_map/ppermute | solution.py:385
  2.1 1.0 collective-permute-done.other_hbm.other_len
  3.1 0.0 copy-start.3
  3.1 0.5 copy-done.3
  3.6 4.0 %pack.1 = (bf16[128,56,128]{2,1,0:T(8,128)(2,1)}, f32[8,128]{1,0:T(8,128)}) custom-call(s32[1,16]{1,0:T(1,128)} %mine_len.1, s32[1,16]{1,0:T(1,128)} %copy-done.3, s32[1,128]{1,0:T(1,128)} %bitcast.1, bf16[128,1024]{1,0:T(8,128)(2,1)} %q_hbm.1, bf16[128,256]{1,0:T(8,128)(2,1)} %kv_hbm.1, bf16[128,1024]{1,0:T(8,128)(2,1)} %g_hbm.1), custom_call_target="tpu_custom_call" | custom-call | tf_op jit(solution)/shard_map/pack/pallas_call | solution.py:396
  7.6 37.3 %all_to_all.10.got_ref = bf16[128,56,128]{2,1,0:T(8,128)(2,1)S(1)} all-to-all(bf16[128,56,128]{2,1,0:T(8,128)(2,1)} %get-tuple-element.13), channel_id=1, replica_groups=mesh['dp'=2,'ctx'=64] {'dp','ctx'}, dimensions={0} | all-to-all | bytes 3670016 | tf_op jit(solution)/shard_map/all_to_all | solution.py:389
  44.9 0.0 copy-start
  44.9 0.0 copy-start.1
  44.9 0.0 copy-start.4
  44.9 0.5 split.1
  45.4 1.1 %collective-permute-start.1 = (bf16[36,128,128]{2,1,0:T(8,128)(2,1)S(1)}, bf16[36,128,128]{2,1,0:T(8,128)(2,1)S(1)}, u32[]{:S(2)}, u32[]{:S(2)}) collective-permute-start(bf16[36,128,128]{2,1,0:T(8,128)(2,1)S(1)} %get-tuple-element.14.mine_ref), channel_id=1, source_target_pairs={{0,64},{64,0},{1,65},{65,1},{2,66},{66,2},{3,67},{67,3},{4,68},{68... | collective-permute-start | bytes 3538952 | tf_op jit(solution)/shard_map/ppermute | solution.py:385
  46.4 2.5 %collective-permute-done.1.other_ref = bf16[36,128,128]{2,1,0:T(8,128)(2,1)S(1)} collective-permute-done((bf16[36,128,128]{2,1,0:T(8,128)(2,1)S(1)}, bf16[36,128,128]{2,1,0:T(8,128)(2,1)S(1)}, u32[]{:S(2)}, u32[]{:S(2)}) %collective-permute-start.1) | collective-permute-done | bytes 1179680 | tf_op jit(solution)/shard_map/ppermute | solution.py:385
  48.9 0.0 copy-done
  48.9 0.0 copy-done.1
  48.9 0.0 copy-done.4
  48.9 15.3 %attention.1 = (bf16[36,128,128]{2,1,0:T(8,128)(2,1)S(1)}, bf16[36,128,128]{2,1,0:T(8,128)(2,1)S(1)}, bf16[1024,128]{1,0:T(8,128)(2,1)S(1)}, bf16[1024,128]{1,0:T(8,128)(2,1)S(1)}) custom-call(s32[1,16]{1,0:T(1,128)S(1)} %copy-done.1, s32[1,16]{1,0:T(1,128)S(1)} %copy-done.4, f32[8,128]{1,0:T(8,128)S(1)} %copy-done, ...), custom_call_target="tpu_custom_call" | custom-call | tf_op jit(solution)/shard_map/attention/pallas_call | solution.py:429
  64.2 0.5 collective-permute-start.2
  64.6 2.5 %collective-permute-done.2.other_ref = bf16[36,128,128]{2,1,0:T(8,128)(2,1)S(1)} collective-permute-done((bf16[36,128,128]{2,1,0:T(8,128)(2,1)S(1)}, bf16[36,128,128]{2,1,0:T(8,128)(2,1)S(1)}, u32[]{:S(2)}, u32[]{:S(2)}) %collective-permute-start.2) | collective-permute-done | bytes 1179680 | tf_op jit(solution)/shard_map/ppermute | solution.py:385
  67.1 0.7 join.1
  67.8 0.0 copy-start.2
  67.8 30.3 %all_to_all.11.got_ref = bf16[128,56,128]{2,1,0:T(8,128)(2,1)S(1)} all-to-all(bf16[128,56,128]{2,1,0:T(8,128)(2,1)S(1)} %join.1), channel_id=1, replica_groups=mesh['dp'=2,'ctx'=64] {'dp','ctx'}, dimensions={0} | all-to-all | bytes 3670016 | tf_op jit(solution)/shard_map/all_to_all | solution.py:389
  98.2 0.0 copy-done.2
  98.2 2.4 %unpack.1 = (bf16[128,1024]{1,0:T(8,128)(2,1)}, bf16[128,1024]{1,0:T(8,128)(2,1)}, bf16[128,256]{1,0:T(8,128)(2,1)}) custom-call(s32[1,128]{1,0:T(1,128)S(1)} %bitcast.2, f32[8,128]{1,0:T(8,128)S(1)} %copy-done, bf16[128,56,128]{2,1,0:T(8,128)(2,1)S(1)} %all_to_all.11.got_ref), custom_call_target="tpu_custom_call" | custom-call | tf_op jit(solution)/shard_map/unpack/pallas_call | solution.py:464
Async XLA Ops:
  0.6 2.5 %collective-permute-start = (s32[1,16]{1,0:T(1,128)}, s32[1,16]{1,0:T(1,128)S(1)}, u32[]{:S(2)}, u32[]{:S(2)}) collective-permute-start(s32[1,16]{1,0:T(1,128)} %mine_len.1), channel_id=1, source_target_pairs={{0,64},{64,0},{1,65},{65,1},{2,66},{66,2},{3,67},{67,3},{4,68},{68... | collective-permute-start | bytes 200 | tf_op jit(solution)/shard_map/ppermute | solution.py:385
  3.1 0.5 copy-start.3
  44.9 4.1 %copy-start = (f32[8,128]{1,0:T(8,128)S(1)}, f32[8,128]{1,0:T(8,128)}, u32[]{:S(2)}) copy-start(f32[8,128]{1,0:T(8,128)} %get-tuple-element.12.plan_ref) | copy-start | bytes 12292
  44.9 4.1 %copy-start.1 = (s32[1,16]{1,0:T(1,128)S(1)}, s32[1,16]{1,0:T(1,128)}, u32[]{:S(2)}) copy-start(s32[1,16]{1,0:T(1,128)} %mine_len.1) | copy-start | bytes 196
  44.9 4.1 %copy-start.4 = (s32[1,16]{1,0:T(1,128)S(1)}, s32[1,16]{1,0:T(1,128)}, u32[]{:S(2)}) copy-start(s32[1,16]{1,0:T(1,128)} %copy-done.3) | copy-start | bytes 196
  45.4 3.6 %collective-permute-start.1 = (bf16[36,128,128]{2,1,0:T(8,128)(2,1)S(1)}, bf16[36,128,128]{2,1,0:T(8,128)(2,1)S(1)}, u32[]{:S(2)}, u32[]{:S(2)}) collective-permute-start(bf16[36,128,128]{2,1,0:T(8,128)(2,1)S(1)} %get-tuple-element.14.mine_ref), channel_id=1, source_target_pairs={{0,64},{64,0},{1,65},{65,1},{2,66},{66,2},{3,67},{67,3},{4,68},{68... | collective-permute-start | bytes 3538952 | tf_op jit(solution)/shard_map/ppermute | solution.py:385
  64.2 2.9 %collective-permute-start.2 = (bf16[36,128,128]{2,1,0:T(8,128)(2,1)S(1)}, bf16[36,128,128]{2,1,0:T(8,128)(2,1)S(1)}, u32[]{:S(2)}, u32[]{:S(2)}) collective-permute-start(bf16[36,128,128]{2,1,0:T(8,128)(2,1)S(1)} %get-tuple-element.18), channel_id=1, source_target_pairs={{0,64},{64,0},{1,65},{65,1},{2,66},{66,2},{3,67},{67,3},{4,68},{68... | collective-permute-start | bytes 3538952 | tf_op jit(solution)/shard_map/ppermute | solution.py:385
  67.8 30.3 %copy-start.2 = (s32[128]{0:T(128)S(1)}, s32[128]{0:T(128)}, u32[]{:S(2)}) copy-start(s32[128]{0:T(128)} %param.8) | copy-start | bytes 1540

commit v5 on v4

--- a/solution.py
+++ b/solution.py
@@ -17,7 +17,6 @@
 nothing = -100000
 masked_score = -1e30
 far = 1e9
-step = 3
 mib = 1024 * 1024
 
 
@@ -79,7 +78,7 @@
         move.wait()
     block_line, count_line = make_plan(lax.axis_index("dp"), mine_ref, other_ref)
     row8 = lax.broadcasted_iota(jnp.int32, (8, block), 0)
-    plan_ref[...] = jnp.where(row8 == 0, block_line, jnp.where(row8 == 1, count_line, 0.0))
+    plan_ref[...] = jnp.where(row8 == 0, block_line, jnp.where(row8 == 1, count_line, 0.0)).astype(jnp.int32)
     block_down = down(block_line).astype(jnp.int32)
     count_down = down(count_line).astype(jnp.int32)
     rows = place_ref[...] >> 7
@@ -154,7 +153,7 @@
         for i, (src, dst) in enumerate([(out_ref, out_hbm), (dq_ref, dq_hbm), (dkv_ref, dkv_hbm)])
     ]
     rows_down = down(place_ref[...] >> 7)
-    plan = plan_ref[...]
+    plan = plan_ref[...].astype(jnp.float32)
     lane = lax.broadcasted_iota(jnp.int32, (8, block), 1)
     lines = [plan[0:1], plan[1:2]]
     lines = lines + [pltpu.roll(plan, 64, 1)[i : i + 1] for i in range(2)]
@@ -232,126 +231,210 @@
             qg_ref[at : at + 8 * block, :] = rows.reshape(8 * block, head)
 
 
-def attention_kernel(
-    mine_len, other_len, plan_ref, mine_ref, other_ref, info_ref, qg,
-    dmine_ref, dother_ref, out_ref, dq_ref,
-    kv, scores, weights, top, total, acc, dot, qs, gs, key_pos, bound,
-):
-    core = lax.axis_index("dp")
-    chip = lax.axis_index("ctx")
+to_exp2 = head ** (-0.5) * 1.4426950408889634
+
+
+def span_of(x, plan_ref, chip):
+    count = plan_ref[1, chip + 64 * x]
+    if x == 0:
+        return 3, 0, jnp.int32(0), count, jnp.int32(0), (count + 5) // 6
+    return 1, 3, entries - count, jnp.int32(entries), (entries - count) // 2, jnp.int32(pairs)
+
+
+def rows_of(x):
+    return slice(x * 512, (x + 1) * 512), slice(1024 + x * 512, 1536 + x * 512)
+
+
+def blocks(ref, half, m, n):
+    return jnp.concatenate([ref[2 * (m * n + u) + half] for u in range(n)], axis=0)
+
+
+def slot(m, n, shift):
+    return pl.ds(m * n + shift, n)
+
+
+def flat(x):
+    return x.reshape(x.shape[0] * block, 512)
+
+
+def find_positions(core, chip, mine_len, other_len, plan_ref, info_ref, key_pos, bound):
     stream = chip // 32
-    scale = head ** (-0.5)
-    to_exp2 = scale * 1.4426950408889634
     stream_base = (64 * stream).astype(jnp.float32)
-    block_row = lax.broadcasted_iota(jnp.int32, (block, block), 0).astype(jnp.float32)
-    lane8 = lax.broadcasted_iota(jnp.int32, (8, block), 1)
-    row8 = lax.broadcasted_iota(jnp.int32, (8, block), 0)
-    slots = info_ref[...].astype(jnp.float32)
-    key_pos[...] = slots.T + 128.0 * (block_row - stream_base)
-    for i in range(pairs):
-        for half in range(2):
-            kv[half, 2 * i * block : (2 * i + 1) * block, :] = mine_ref[2 * i + half]
-            kv[half, (2 * i + 1) * block : (2 * i + 2) * block, :] = other_ref[2 * i + half]
-    plan = plan_ref[...]
-    dmine_ref[...] = jnp.zeros(dmine_ref.shape, jnp.bfloat16)
-    dother_ref[...] = jnp.zeros(dother_ref.shape, jnp.bfloat16)
-    span = 256 * step
-
-    def planned(row, x):
-        seat = (row8 == row) & (lane8 == chip + 64 * x)
-        return jnp.sum(jnp.where(seat, plan, 0.0)).astype(jnp.int32)
-
-    def some(half, m):
-        return kv[half, pl.ds(pl.multiple_of(m * span, span), span), :]
-
-    def add(ref, i, x):
-        ref[i] = (ref[i].astype(jnp.float32) + x).astype(jnp.bfloat16)
-
+    block_row = lax.broadcasted_iota(jnp.int32, (block, block), 0)
+    key_pos[...] = info_ref[...].astype(jnp.float32).T + 128.0 * (block_row.astype(jnp.float32) - stream_base)
     for x in range(2):
-        mine_block = planned(0, x)
-        count = planned(1, x)
-        if x == 0:
-            begin, end = jnp.int32(0), (count + 2 * step - 1) // (2 * step)
-            entry_low, entry_high = jnp.int32(0), count
-            base = mine_block - count + 1
-        else:
-            begin, end = (entries - count) // (2 * step), jnp.int32(pairs // step)
-            entry_low, entry_high = entries - count, jnp.int32(entries)
-            base = mine_block - (entries - 1)
-        pos = key_pos[pl.ds(mine_block, 1), :]
+        pos = key_pos[pl.ds(plan_ref[0, chip + 64 * x], 1), :]
         start = jnp.zeros((1, block), jnp.float32)
         doc_end = jnp.int32(0)
         for i in range(16):
             doc_end = doc_end + stream_length(core, mine_len, other_len, stream, i)
             f = doc_end.astype(jnp.float32)
             start = jnp.where(f <= pos, f, start)
-        bound[0:1] = pos
-        bound[1:2] = start
-        top[...] = jnp.full(top.shape, masked_score, jnp.float32)
+        bound[2 * x : 2 * x + 1] = pos
+        bound[2 * x + 1 : 2 * x + 2] = start
+
+
+def score(x, m, n, low, high, parity, plan_ref, chip, kv_ref, qg, key_pos, bound):
+    base = plan_ref[0, chip + 64 * x] - plan_ref[1, chip + 64 * x] + 1 - low
+    bias = []
+    for u in range(n):
+        entry = 2 * (m * n + u) + parity
+        valid = (entry >= low) & (entry < high)
+        kp = key_pos[pl.ds(jnp.where(valid, base + entry, 0), 1), :]
+        kp = jnp.broadcast_to(jnp.where(valid, kp, far), (block, block)).T
+        seen = (kp <= bound[2 * x : 2 * x + 1]) & (kp >= bound[2 * x + 1 : 2 * x + 2])
+        bias.append(jnp.where(seen, 0.0, masked_score))
+    bias = jnp.concatenate(bias, axis=0)
+    bias = jnp.concatenate([bias] * 4, axis=1)
+    return nt(blocks(kv_ref, 0, m, n), qg[rows_of(x)[0], :]) + bias
+
+
+def peak_of(s):
+    return jnp.max(s.reshape(s.shape[0] // 8, 8, 512), axis=0)
+
+
+def sum_of(p):
+    return jnp.sum(p.reshape(p.shape[0] // 8, 8, 512), axis=0)
+
+
+def scores_kernel(
+    mine_len, other_len, plan_ref, mine_ref, info_ref, qg,
+    s_ref, gw_ref, top_ref,
+    key_pos, bound,
+):
+    core = lax.axis_index("dp")
+    chip = lax.axis_index("ctx")
+    find_positions(core, chip, mine_len, other_len, plan_ref, info_ref, key_pos, bound)
+    for x in range(2):
+        n, shift, low, high, begin, end = span_of(x, plan_ref, chip)
+        top_ref[x] = jnp.full((8, 512), masked_score, jnp.float32)
+
+        @pl.loop(begin, end)
+        def _(m):
+            s = score(x, m, n, low, high, core, plan_ref, chip, mine_ref, qg, key_pos, bound)
+            gw = nt(blocks(mine_ref, 1, m, n), qg[rows_of(x)[1], :])
+            s_ref[slot(m, n, shift)] = s.reshape(n, block, 512)
+            top_ref[x] = jnp.maximum(top_ref[x], peak_of(s))
+            gw_ref[slot(m, n, shift)] = gw.reshape(n, block, 512)
+
+
+def backward(n, at, p_ref, gw_ref, kv_ref, dot, qs, gs, acc, out_ref, first, m):
+    p = flat(p_ref[at])
+    ds = (p.astype(jnp.float32) * (flat(gw_ref[at]) - dot)).astype(jnp.bfloat16)
+    dk = nn(ds, qs)
+    acc[...] = acc[...] + tn(blocks(kv_ref, 0, m, n), ds)
+    dv = nn(p, gs)
+    for u in range(n):
+        for half, value in enumerate((dk, dv)):
+            value = value[u * block : (u + 1) * block]
+            i = 2 * (m * n + u) + half
+            if not first:
+                value = value + out_ref[i].astype(jnp.float32)
+            out_ref[i] = value.astype(jnp.bfloat16)
+
+
+def clear_rest(out_ref, end):
+    @pl.loop(6 * end, kv_rows)
+    def _(i):
+        out_ref[i] = jnp.zeros((block, head), jnp.bfloat16)
+
+
+def turned(x):
+    row = lax.broadcasted_iota(jnp.int32, (block, block), 0)
+    eye = one_hot(row == lax.broadcasted_iota(jnp.int32, (block, block), 1))
+    return jnp.concatenate([nt(eye, x[:, h * block : (h + 1) * block]) for h in range(4)], axis=0)
+
+
+def weights_kernel(
+    mine_len, other_len, plan_ref, mine_ref, other_ref, info_ref, qg, s_ref, found_ref,
+    dother_ref, out_ref, p_ref, dot_ref, qs_ref, gs_ref, acc_ref, inv_ref,
+    scores, gws, ps, top, total, acc, key_pos, bound,
+):
+    core = lax.axis_index("dp")
+    chip = lax.axis_index("ctx")
+    scale = head ** (-0.5)
+    ones = jnp.full((16, block), 1.0, jnp.bfloat16)
+    row16 = lax.broadcasted_iota(jnp.int32, (16, 512), 0)
+    find_positions(core, chip, mine_len, other_len, plan_ref, info_ref, key_pos, bound)
+    for x in range(2):
+        n, shift, low, high, begin, end = span_of(x, plan_ref, chip)
+        q_rows, g_rows = rows_of(x)
+        if x == 0:
+            clear_rest(dother_ref, end)
+        top[...] = found_ref[x]
+
+        @pl.loop(begin, end)
+        def _(m):
+            s = score(x, m, n, low, high, 1 - core, plan_ref, chip, other_ref, qg, key_pos, bound)
+            scores[slot(m, n, shift)] = s.reshape(n, block, 512)
+            top[...] = jnp.maximum(top[...], peak_of(s))
+
+        top[...] = jnp.broadcast_to(jnp.max(top[...], axis=0, keepdims=True) * to_exp2, (8, 512))
         total[...] = jnp.zeros(total.shape, jnp.float32)
         acc[...] = jnp.zeros(acc.shape, jnp.float32)
-        q_at, g_at = x * 512, 1024 + x * 512
 
         @pl.loop(begin, end)
         def _(m):
-            keys = some(0, m)
-            bias = []
-            for u, par in [(u, par) for u in range(step) for par in (core, 1 - core)]:
-                entry = 2 * (m * step + u) + par
-                valid = (entry >= entry_low) & (entry < entry_high)
-                kp = key_pos[pl.ds(jnp.where(valid, base + entry, 0), 1), :]
-                kp = jnp.broadcast_to(jnp.where(valid, kp, far), (block, block)).T
-                bias.append(jnp.where((kp <= bound[0:1]) & (kp >= bound[1:2]), 0.0, masked_score))
-            bias = jnp.concatenate(bias, axis=0)
-            bias = jnp.concatenate([bias] * 4, axis=1)
-            s = nt(keys, qg[q_at : q_at + 512, :]) + bias
-            scores[m] = s
-            top[...] = jnp.maximum(top[...], jnp.max(s.reshape(span // 8, 8, 512), axis=0))
-
-        top[...] = jnp.broadcast_to(jnp.max(top[...], axis=0, keepdims=True) * to_exp2, top.shape)
+            at = slot(m, n, shift)
+            gws[at] = nt(blocks(other_ref, 1, m, n), qg[g_rows, :]).reshape(n, block, 512)
+            p = jnp.exp2(flat(s_ref[at]) * to_exp2 - top[0:1])
+            p_other = jnp.exp2(flat(scores[at]) * to_exp2 - top[0:1])
+            total[...] = total[...] + (sum_of(p) + sum_of(p_other))
+            p, p_other = p.astype(jnp.bfloat16), p_other.astype(jnp.bfloat16)
+            p_ref[at] = p.reshape(n, block, 512)
+            ps[at] = p_other.reshape(n, block, 512)
+            values = jnp.concatenate([blocks(mine_ref, 1, m, n), blocks(other_ref, 1, m, n)], axis=0)
+            acc[...] = acc[...] + tn(values, jnp.concatenate([p, p_other], axis=0))
+
+        inv = 1.0 / jnp.sum(total[...], axis=0, keepdims=True)
+        part = inv.astype(jnp.bfloat16).astype(jnp.float32)
+        rest = inv - part
+        middle = rest.astype(jnp.bfloat16).astype(jnp.float32)
+        parts = jnp.where(row16 == 0, part, jnp.where(row16 == 1, middle, jnp.where(row16 == 2, rest - middle, 0.0)))
+        inv_down = tn(parts.astype(jnp.bfloat16), ones)
+        o = turned((acc[...] * inv).astype(jnp.bfloat16))
+        out_ref[q_rows, :] = o.astype(jnp.bfloat16)
+        g = qg[g_rows, :].astype(jnp.float32)
+        terms = g * o
+        part = terms.astype(jnp.bfloat16)
+        d = nt(ones, part) + nt(ones, (terms - part.astype(jnp.float32)).astype(jnp.bfloat16))
+        dot_ref[x] = d[:8]
+        gs_ref[q_rows, :] = (g * inv_down).astype(jnp.bfloat16)
+        qs_ref[q_rows, :] = (qg[q_rows, :].astype(jnp.float32) * (inv_down * scale)).astype(jnp.bfloat16)
+        inv_ref[x] = jnp.broadcast_to(inv * scale, (8, 512))
+        acc[...] = jnp.zeros(acc.shape, jnp.float32)
 
         @pl.loop(begin, end)
         def _(m):
-            p = jnp.exp2(scores[m] * to_exp2 - top[0:1])
-            total[...] = total[...] + jnp.sum(p.reshape(span // 8, 8, 512), axis=0)
-            half = p.astype(jnp.bfloat16)
-            weights[m] = half
-            acc[...] = acc[...] + tn(some(1, m), half)
-
-        inv = 1.0 / jnp.sum(total[...], axis=0, keepdims=True)
-        for h in range(4):
-            at = slice(h * block, (h + 1) * block)
-            q_rows = slice(q_at + h * block, q_at + (h + 1) * block)
-            inv_down = jnp.broadcast_to(inv[:, at], (block, block)).T
-            o = (acc[:, at].T * inv_down).astype(jnp.bfloat16)
-            out_ref[q_rows, :] = o
-            g = qg[g_at + h * block : g_at + (h + 1) * block, :].astype(jnp.float32)
-            q = qg[q_rows, :].astype(jnp.float32)
-            d = jnp.sum(g * o.astype(jnp.float32), axis=1, keepdims=True)
-            dot[:, at] = jnp.broadcast_to(d, (block, block)).T[:8]
-            gs[at] = (g * inv_down).astype(jnp.bfloat16)
-            qs[at] = (q * (inv_down * scale)).astype(jnp.bfloat16)
-        total[...] = jnp.broadcast_to(inv * scale, total.shape)
-        acc[...] = jnp.zeros(acc.shape, jnp.float32)
+            backward(
+                n, slot(m, n, shift), ps, gws, other_ref, dot_ref[x][0:1], qs_ref[q_rows, :], gs_ref[q_rows, :],
+                acc, dother_ref, x == 0, m,
+            )
+
+        acc_ref[x] = acc[...]
+
+
+def grads_kernel(
+    plan_ref, mine_ref, gw_ref, p_ref, dot_ref, qs_ref, gs_ref, acc_ref, inv_ref,
+    dmine_ref, dq_ref,
+    acc,
+):
+    chip = lax.axis_index("ctx")
+    for x in range(2):
+        n, shift, _, _, begin, end = span_of(x, plan_ref, chip)
+        q_rows = rows_of(x)[0]
+        if x == 0:
+            clear_rest(dmine_ref, end)
+        acc[...] = acc_ref[x]
 
         @pl.loop(begin, end)
         def _(m):
-            gw = nt(some(1, m), qg[g_at : g_at + 512, :])
-            p = weights[m]
-            ds = (p.astype(jnp.float32) * (gw - dot[0:1])).astype(jnp.bfloat16)
-            acc[...] = acc[...] + tn(some(0, m), ds)
-            dk = nn(ds, qs[...])
-            dv = nn(p, gs[...])
-            for u in range(step):
-                i = 2 * (m * step + u)
-                add(dmine_ref, i, dk[u * 256 : u * 256 + block])
-                add(dmine_ref, i + 1, dv[u * 256 : u * 256 + block])
-                add(dother_ref, i, dk[u * 256 + block : (u + 1) * 256])
-                add(dother_ref, i + 1, dv[u * 256 + block : (u + 1) * 256])
-
-        for h in range(4):
-            at = slice(h * block, (h + 1) * block)
-            dq_ref[q_at + h * block : q_at + (h + 1) * block, :] = (acc[:, at] * total[0:1, at]).T.astype(jnp.bfloat16)
+            backward(
+                n, slot(m, n, shift), p_ref, gw_ref, mine_ref, dot_ref[x][0:1], qs_ref[q_rows, :], gs_ref[q_rows, :],
+                acc, dmine_ref, x == 0, m,
+            )
+
+        dq_ref[q_rows, :] = turned((acc[...] * inv_ref[x][0:1]).astype(jnp.bfloat16)).astype(jnp.bfloat16)
 
 
 def join_kernel(mine_ref, other_ref, out_ref, dq_ref, back_ref):
@@ -389,6 +472,42 @@
     return lax.all_to_all(x, ("dp", "ctx"), split_axis=0, concat_axis=0, tiled=True)
 
 
+def kernel(name, body, ins, scalars, outs, scratch, size):
+    return pl.pallas_call(
+        body,
+        out_shape=tuple(jax.ShapeDtypeStruct(shape, dtype) for shape, dtype in outs),
+        in_specs=[smem()] * scalars + vmem(len(ins) - scalars),
+        out_specs=tuple(vmem(len(outs))),
+        scratch_shapes=[pltpu.VMEM(shape, dtype) for shape, dtype in scratch],
+        compiler_params=params(size),
+        name=name,
+    )(*ins)
+
+
+def attention(lengths, other_lengths, plan, mine, other, info, qg):
+    bf16, f32 = jnp.bfloat16, jnp.float32
+    slots = (pairs + 3, block, 512)
+    rows = ((2, 8, 512), f32)
+    acc = ((2, head, 512), f32)
+    heads = ((1024, head), bf16)
+    places = [((block, block), f32), ((8, block), f32)]
+    s, gw, top = kernel(
+        "scores", scores_kernel, (lengths, other_lengths, plan, mine, info, qg), 3,
+        [(slots, f32), (slots, f32), rows], places, 12,
+    )
+    dother, out, p, dot, qs, gs, partial, inv = kernel(
+        "weights", weights_kernel, (lengths, other_lengths, plan, mine, other, info, qg, s, top), 3,
+        [((kv_rows, block, head), bf16), heads, (slots, bf16), rows, heads, heads, acc, rows],
+        [(slots, f32), (slots, f32), (slots, bf16), ((8, 512), f32), ((8, 512), f32), ((head, 512), f32)] + places, 24,
+    )
+    other_terms = swap(dother)
+    dmine, dq = kernel(
+        "grads", grads_kernel, (plan, mine, gw, p, dot, qs, gs, partial, inv), 1,
+        [((kv_rows, block, head), bf16), heads], [((head, 512), f32)], 12,
+    )
+    return dmine, other_terms, out, dq
+
+
 def on_device(queries, keys_values, grad_out, placement, doc_lengths):
     bf16, f32 = jnp.bfloat16, jnp.float32
     place = placement.reshape(1, block)
@@ -397,7 +516,7 @@
         pack_kernel,
         out_shape=(
             jax.ShapeDtypeStruct((128, send_rows, head), bf16),
-            jax.ShapeDtypeStruct((8, block), f32),
+            jax.ShapeDtypeStruct((8, block), jnp.int32),
         ),
         in_specs=[pl.BlockSpec(memory_space=pl.ANY)] * 6,
         out_specs=(pl.BlockSpec(memory_space=pl.ANY), vmem(1)[0]),
@@ -426,32 +545,7 @@
         compiler_params=params(24),
         name="split",
     )(exchange(sent))
-    dmine, dother, out, dq = pl.pallas_call(
-        attention_kernel,
-        out_shape=(
-            jax.ShapeDtypeStruct((kv_rows, block, head), bf16),
-            jax.ShapeDtypeStruct((kv_rows, block, head), bf16),
-            jax.ShapeDtypeStruct((1024, head), bf16),
-            jax.ShapeDtypeStruct((1024, head), bf16),
-        ),
-        in_specs=[smem()] * 2 + vmem(5),
-        out_specs=tuple(vmem(4)),
-        scratch_shapes=[
-            pltpu.VMEM((2, entries * block, head), bf16),
-            pltpu.VMEM((pairs // step, 256 * step, 512), f32),
-            pltpu.VMEM((pairs // step, 256 * step, 512), bf16),
-            pltpu.VMEM((8, 512), f32),
-            pltpu.VMEM((8, 512), f32),
-            pltpu.VMEM((head, 512), f32),
-            pltpu.VMEM((8, 512), f32),
-            pltpu.VMEM((512, head), bf16),
-            pltpu.VMEM((512, head), bf16),
-            pltpu.VMEM((block, block), f32),
-            pltpu.VMEM((8, block), f32),
-        ],
-        compiler_params=params(32),
-        name="attention",
-    )(doc_lengths, other_lengths, plan, mine, swap(mine), info, qg)
+    dmine, dother, out, dq = attention(doc_lengths, other_lengths, plan, mine, swap(mine), info, qg)
     back = pl.pallas_call(
         join_kernel,
         out_shape=jax.ShapeDtypeStruct((128, send_rows, head), bf16),
@@ -459,7 +553,7 @@
         out_specs=vmem(1)[0],
         compiler_params=params(24),
         name="join",
-    )(dmine, swap(dother), out, dq)
+    )(dmine, dother, out, dq)
     returned = exchange(back)
     return pl.pallas_call(
         unpack_kernel,

time: 101 us -> 97.6 us (0.966)
  waiting for transfers between devices: 5.9 us -> 0.96 us
  Pallas kernels: 22.9 us -> 24.7 us
    ppermute x3, waiting for transfers between devices: 5.9 us -> 0.96 us  [swap(): return lax.ppermute(x, 'dp', [(0, 1), (1, 0)])]
    pallas_call x1 -> x3, Pallas kernels: 15.3 us -> 17.1 us  [kernel(): pl.pallas_call(body, out_shape=tuple((jax.ShapeDtypeStruct(shape, dtype)...]
  transfers between devices with their start and end apart: 3 -> 3, of which waited for: 3 -> 1; matrix products, arithmetic and copies ran while one was open for 0% -> 0% of each run, Pallas kernels for 0% -> 8%
where the time goes in v5:
time: 97.6 us; the launch traced here: 97.3 us
  blocking collectives  67.6 us (69%)
  Pallas kernels  24.7 us (25%)
  starting transfers between devices  2.74 us (3%)
    all_to_all x2, blocking collectives, exchange(): lax.all_to_all(x, ('dp', 'ctx'), split_axis=0, concat_axis=0, tiled=True)  67.6 us
    pallas_call x3, Pallas kernels, kernel(): pl.pallas_call(body, out_shape=tuple((jax.ShapeDtypeStruct(shape, dtype)...  17.1 us
    pallas_call x1, Pallas kernels, on_device(): pl.pallas_call(pack_kernel, out_shape=(jax.ShapeDtypeStruct((128, send_ro...  3.98 us
    ppermute x3, starting transfers between devices, swap(): return lax.ppermute(x, 'dp', [(0, 1), (1, 0)])  2.74 us
    pallas_call x1, Pallas kernels, on_device(): pl.pallas_call(unpack_kernel, out_shape=(jax.ShapeDtypeStruct((block, 8 *...  2.42 us
  transfers between devices with their start and end apart: 3, of which 1 were waited for; matrix products, arithmetic and copies ran while one was open for 0% of the time, Pallas kernels for 8%

profile of v5, /device:TPU:1, one launch (start us, length us, event | category | flops | bytes accessed | tf_op | source)
XLA Modules:
  0.0 97.3 jit_solution(1002280480088017061)
XLA Ops:
  0.6 1.5 %collective-permute-start = (s32[1,16]{1,0:T(1,128)}, s32[1,16]{1,0:T(1,128)S(1)}, u32[]{:S(2)}, u32[]{:S(2)}) collective-permute-start(s32[1,16]{1,0:T(1,128)} %mine_len.3), channel_id=1, source_target_pairs={{0,64},{64,0},{1,65},{65,1},{2,66},{66,2},{3,67},{67,3},{4,68},{68... | collective-permute-start | bytes 200 | tf_op jit(solution)/shard_map/ppermute | solution.py:468
  2.1 1.0 collective-permute-done.other_hbm.other_len
  3.1 0.0 copy-start.2
  3.1 0.5 copy-done.2
  3.6 4.0 %pack.1 = (bf16[128,56,128]{2,1,0:T(8,128)(2,1)}, s32[8,128]{1,0:T(8,128)}) custom-call(s32[1,16]{1,0:T(1,128)} %mine_len.3, s32[1,16]{1,0:T(1,128)} %copy-done.2, s32[1,128]{1,0:T(1,128)} %bitcast.1, bf16[128,1024]{1,0:T(8,128)(2,1)} %q_hbm.1, bf16[128,256]{1,0:T(8,128)(2,1)} %kv_hbm.1, bf16[128,1024]{1,0:T(8,128)(2,1)} %g_hbm.1), custom_call_target="tpu_custom_call" | custom-call | tf_op jit(solution)/shard_map/pack/pallas_call | solution.py:515
  7.6 37.3 %all_to_all.10.got_ref = bf16[128,56,128]{2,1,0:T(8,128)(2,1)S(1)} all-to-all(bf16[128,56,128]{2,1,0:T(8,128)(2,1)} %get-tuple-element.22), channel_id=1, replica_groups=mesh['dp'=2,'ctx'=64] {'dp','ctx'}, dimensions={0} | all-to-all | bytes 3670016 | tf_op jit(solution)/shard_map/all_to_all | solution.py:472
  44.9 0.0 copy-start
  44.9 0.0 copy-start.1
  44.9 0.5 split.1
  45.4 1.1 %collective-permute-start.1 = (bf16[36,128,128]{2,1,0:T(8,128)(2,1)S(1)}, bf16[36,128,128]{2,1,0:T(8,128)(2,1)S(1)}, u32[]{:S(2)}, u32[]{:S(2)}) collective-permute-start(bf16[36,128,128]{2,1,0:T(8,128)(2,1)S(1)} %get-tuple-element.23.mine_ref), channel_id=1, source_target_pairs={{0,64},{64,0},{1,65},{65,1},{2,66},{66,2},{3,67},{67,3},{4,68},{68... | collective-permute-start | bytes 3538952 | tf_op jit(solution)/shard_map/ppermute | solution.py:468
  46.5 0.0 copy-done
  46.5 0.0 copy-done.1
  46.5 0.0 copy-done.3
  46.5 3.2 %scores.1 = (f32[21,128,512]{2,1,0:T(8,128)S(1)}, f32[21,128,512]{2,1,0:T(8,128)S(1)}, f32[2,8,512]{2,1,0:T(8,128)S(1)}) custom-call(s32[1,16]{1,0:T(1,128)S(1)} %copy-done.1, s32[1,16]{1,0:T(1,128)S(1)} %copy-done.3, s32[8,128]{1,0:T(8,128)S(1)} %copy-done, bf16[36,128,128]{2,1,0:T(8,128)(2,1)S(1)} %get-tuple-element.23.mine_ref, ...), custom_call_target="tpu_custom_call" | custom-call | tf_op jit(solution)/shard_map/scores/pallas_call | solution.py:476
  49.7 0.0 collective-permute-done.1.other_ref
  49.7 9.8 %weights.1 = (bf16[36,128,128]{2,1,0:T(8,128)(2,1)S(1)}, bf16[1024,128]{1,0:T(8,128)(2,1)S(1)}, bf16[21,128,512]{2,1,0:T(8,128)(2,1)S(1)}, f32[2,8,512]{2,1,0:T(...) custom-call(s32[1,16]{1,0:T(1,128)S(1)} %copy-done.1, ...), custom_call_target="tpu_custom_call" | custom-call | tf_op jit(solution)/shard_map/weights/pallas_call | solution.py:476
  59.5 0.2 collective-permute-start.2
  59.7 4.1 %grads.1 = (bf16[36,128,128]{2,1,0:T(8,128)(2,1)S(1)}, bf16[1024,128]{1,0:T(8,128)(2,1)S(1)}) custom-call(s32[8,128]{1,0:T(8,128)S(1)} %copy-done, bf16[36,128,128]{2,1,0:T(8,128)(2,1)S(1)} %get-tuple-element.23.mine_ref, f32[21,128,512]{2,1,0:T(8,128)S(1)} %get-tuple-element.26.gw_ref, bf16[21,128,512]{2,1,0:T(8,128)(2,1)S(1)} %get-tuple-element.29.p_ref, ...), custom_call_target="tpu_custom_call" | custom-call | tf_op jit(solution)/shard_map/grads/pallas_call | solution.py:476
  63.8 0.0 collective-permute-done.2.other_ref
  63.8 0.7 join.1
  64.5 0.0 copy-start.4
  64.5 30.3 %all_to_all.11.got_ref = bf16[128,56,128]{2,1,0:T(8,128)(2,1)S(1)} all-to-all(bf16[128,56,128]{2,1,0:T(8,128)(2,1)S(1)} %join.1), channel_id=1, replica_groups=mesh['dp'=2,'ctx'=64] {'dp','ctx'}, dimensions={0} | all-to-all | bytes 3670016 | tf_op jit(solution)/shard_map/all_to_all | solution.py:472
  94.9 0.0 copy-done.4
  94.9 2.4 %unpack.1 = (bf16[128,1024]{1,0:T(8,128)(2,1)}, bf16[128,1024]{1,0:T(8,128)(2,1)}, bf16[128,256]{1,0:T(8,128)(2,1)}) custom-call(s32[1,128]{1,0:T(1,128)S(1)} %bitcast.2, s32[8,128]{1,0:T(8,128)S(1)} %copy-done, bf16[128,56,128]{2,1,0:T(8,128)(2,1)S(1)} %all_to_all.11.got_ref), custom_call_target="tpu_custom_call" | custom-call | tf_op jit(solution)/shard_map/unpack/pallas_call | solution.py:558
  (1 shorter events, 0.0 us)
Async XLA Ops:
  0.6 2.5 %collective-permute-start = (s32[1,16]{1,0:T(1,128)}, s32[1,16]{1,0:T(1,128)S(1)}, u32[]{:S(2)}, u32[]{:S(2)}) collective-permute-start(s32[1,16]{1,0:T(1,128)} %mine_len.3), channel_id=1, source_target_pairs={{0,64},{64,0},{1,65},{65,1},{2,66},{66,2},{3,67},{67,3},{4,68},{68... | collective-permute-start | bytes 200 | tf_op jit(solution)/shard_map/ppermute | solution.py:468
  3.1 0.5 copy-start.2
  44.9 1.6 %copy-start = (s32[8,128]{1,0:T(8,128)S(1)}, s32[8,128]{1,0:T(8,128)}, u32[]{:S(2)}) copy-start(s32[8,128]{1,0:T(8,128)} %get-tuple-element.21.plan_ref) | copy-start | bytes 12292
  44.9 1.6 %copy-start.1 = (s32[1,16]{1,0:T(1,128)S(1)}, s32[1,16]{1,0:T(1,128)}, u32[]{:S(2)}) copy-start(s32[1,16]{1,0:T(1,128)} %mine_len.3) | copy-start | bytes 196
  44.9 1.6 %copy-start.3 = (s32[1,16]{1,0:T(1,128)S(1)}, s32[1,16]{1,0:T(1,128)}, u32[]{:S(2)}) copy-start(s32[1,16]{1,0:T(1,128)} %copy-done.2) | copy-start | bytes 196
  45.4 4.3 %collective-permute-start.1 = (bf16[36,128,128]{2,1,0:T(8,128)(2,1)S(1)}, bf16[36,128,128]{2,1,0:T(8,128)(2,1)S(1)}, u32[]{:S(2)}, u32[]{:S(2)}) collective-permute-start(bf16[36,128,128]{2,1,0:T(8,128)(2,1)S(1)} %get-tuple-element.23.mine_ref), channel_id=1, source_target_pairs={{0,64},{64,0},{1,65},{65,1},{2,66},{66,2},{3,67},{67,3},{4,68},{68... | collective-permute-start | bytes 3538952 | tf_op jit(solution)/shard_map/ppermute | solution.py:468
  59.5 4.3 %collective-permute-start.2 = (bf16[36,128,128]{2,1,0:T(8,128)(2,1)S(1)}, bf16[36,128,128]{2,1,0:T(8,128)(2,1)S(1)}, u32[]{:S(2)}, u32[]{:S(2)}) collective-permute-start(bf16[36,128,128]{2,1,0:T(8,128)(2,1)S(1)} %get-tuple-element.36), channel_id=1, source_target_pairs={{0,64},{64,0},{1,65},{65,1},{2,66},{66,2},{3,67},{67,3},{4,68},{68... | collective-permute-start | bytes 3538952 | tf_op jit(solution)/shard_map/ppermute | solution.py:468
  64.5 30.3 %copy-start.4 = (s32[128]{0:T(128)S(1)}, s32[128]{0:T(128)}, u32[]{:S(2)}) copy-start(s32[128]{0:T(128)} %param.8) | copy-start | bytes 1540

commit v6 on v5

--- a/solution.py
+++ b/solution.py
@@ -234,11 +234,16 @@
 to_exp2 = head ** (-0.5) * 1.4426950408889634
 
 
-def span_of(x, plan_ref, chip):
-    count = plan_ref[1, chip + 64 * x]
-    if x == 0:
-        return 3, 0, jnp.int32(0), count, jnp.int32(0), (count + 5) // 6
-    return 1, 3, entries - count, jnp.int32(entries), (entries - count) // 2, jnp.int32(pairs)
+def spans_of(plan_ref, chip):
+    first, second = plan_ref[1, chip], plan_ref[1, chip + 64]
+    begin = entries - second
+    few = second <= 2
+    whole = jnp.int32(entries)
+    return [
+        (0, 6, 0, jnp.int32(0), first, jnp.int32(0), (first + 11) // 12),
+        (1, 1, 6, begin, whole, jnp.where(few, begin // 2, pairs), jnp.int32(pairs)),
+        (1, 3, 6, begin, whole, jnp.where(few, pairs // 3, begin // 6), jnp.int32(pairs // 3)),
+    ]
 
 
 def rows_of(x):
@@ -299,42 +304,47 @@
 
 def scores_kernel(
     mine_len, other_len, plan_ref, mine_ref, info_ref, qg,
-    s_ref, gw_ref, top_ref,
-    key_pos, bound,
+    s_ref, gw_ref, top_ref, key_pos, bound,
 ):
     core = lax.axis_index("dp")
     chip = lax.axis_index("ctx")
     find_positions(core, chip, mine_len, other_len, plan_ref, info_ref, key_pos, bound)
-    for x in range(2):
-        n, shift, low, high, begin, end = span_of(x, plan_ref, chip)
-        top_ref[x] = jnp.full((8, 512), masked_score, jnp.float32)
+    top_ref[...] = jnp.full(top_ref.shape, masked_score, jnp.float32)
+    for x, n, shift, low, high, begin, end in spans_of(plan_ref, chip):
+        cols = slice(x * 512, (x + 1) * 512)
 
         @pl.loop(begin, end)
         def _(m):
             s = score(x, m, n, low, high, core, plan_ref, chip, mine_ref, qg, key_pos, bound)
             gw = nt(blocks(mine_ref, 1, m, n), qg[rows_of(x)[1], :])
             s_ref[slot(m, n, shift)] = s.reshape(n, block, 512)
-            top_ref[x] = jnp.maximum(top_ref[x], peak_of(s))
+            top_ref[:, cols] = jnp.maximum(top_ref[:, cols], peak_of(s))
             gw_ref[slot(m, n, shift)] = gw.reshape(n, block, 512)
 
 
-def backward(n, at, p_ref, gw_ref, kv_ref, dot, qs, gs, acc, out_ref, first, m):
-    p = flat(p_ref[at])
-    ds = (p.astype(jnp.float32) * (flat(gw_ref[at]) - dot)).astype(jnp.bfloat16)
-    dk = nn(ds, qs)
-    acc[...] = acc[...] + tn(blocks(kv_ref, 0, m, n), ds)
-    dv = nn(p, gs)
-    for u in range(n):
-        for half, value in enumerate((dk, dv)):
-            value = value[u * block : (u + 1) * block]
-            i = 2 * (m * n + u) + half
-            if not first:
-                value = value + out_ref[i].astype(jnp.float32)
-            out_ref[i] = value.astype(jnp.bfloat16)
+def backward(span, p_ref, gw_ref, kv_ref, dot_ref, qs_ref, gs_ref, acc, out_ref):
+    x, n, shift, _, _, begin, end = span
+    cols = slice(x * 512, (x + 1) * 512)
+
+    @pl.loop(begin, end)
+    def _(m):
+        at = slot(m, n, shift)
+        p = flat(p_ref[at])
+        ds = (p.astype(jnp.float32) * (flat(gw_ref[at]) - dot_ref[0:1, cols])).astype(jnp.bfloat16)
+        dk = nn(ds, qs_ref[cols, :])
+        acc[:, cols] = acc[:, cols] + tn(blocks(kv_ref, 0, m, n), ds)
+        dv = nn(p, gs_ref[cols, :])
+        for u in range(n):
+            for half, value in enumerate((dk, dv)):
+                value = value[u * block : (u + 1) * block]
+                i = 2 * (m * n + u) + half
+                if x == 1:
+                    value = value + out_ref[i].astype(jnp.float32)
+                out_ref[i] = value.astype(jnp.bfloat16)
 
 
 def clear_rest(out_ref, end):
-    @pl.loop(6 * end, kv_rows)
+    @pl.loop(12 * end, kv_rows)
     def _(i):
         out_ref[i] = jnp.zeros((block, head), jnp.bfloat16)
 
@@ -342,99 +352,83 @@
 def turned(x):
     row = lax.broadcasted_iota(jnp.int32, (block, block), 0)
     eye = one_hot(row == lax.broadcasted_iota(jnp.int32, (block, block), 1))
-    return jnp.concatenate([nt(eye, x[:, h * block : (h + 1) * block]) for h in range(4)], axis=0)
+    return jnp.concatenate([nt(eye, x[:, h * block : (h + 1) * block]) for h in range(8)], axis=0)
 
 
 def weights_kernel(
-    mine_len, other_len, plan_ref, mine_ref, other_ref, info_ref, qg, s_ref, found_ref,
+    plan_ref, mine_ref, other_ref, qg, s_ref, found_ref, key_pos, bound,
     dother_ref, out_ref, p_ref, dot_ref, qs_ref, gs_ref, acc_ref, inv_ref,
-    scores, gws, ps, top, total, acc, key_pos, bound,
+    scores, gws, ps, top, total, acc,
 ):
     core = lax.axis_index("dp")
     chip = lax.axis_index("ctx")
     scale = head ** (-0.5)
     ones = jnp.full((16, block), 1.0, jnp.bfloat16)
-    row16 = lax.broadcasted_iota(jnp.int32, (16, 512), 0)
-    find_positions(core, chip, mine_len, other_len, plan_ref, info_ref, key_pos, bound)
-    for x in range(2):
-        n, shift, low, high, begin, end = span_of(x, plan_ref, chip)
-        q_rows, g_rows = rows_of(x)
-        if x == 0:
-            clear_rest(dother_ref, end)
-        top[...] = found_ref[x]
+    row16 = lax.broadcasted_iota(jnp.int32, (16, 1024), 0)
+    spans = spans_of(plan_ref, chip)
+    clear_rest(dother_ref, spans[0][-1])
+    top[...] = found_ref[...]
+    total[...] = jnp.zeros(total.shape, jnp.float32)
+    acc[...] = jnp.zeros(acc.shape, jnp.float32)
+    for x, n, shift, low, high, begin, end in spans:
+        cols = slice(x * 512, (x + 1) * 512)
 
         @pl.loop(begin, end)
         def _(m):
             s = score(x, m, n, low, high, 1 - core, plan_ref, chip, other_ref, qg, key_pos, bound)
             scores[slot(m, n, shift)] = s.reshape(n, block, 512)
-            top[...] = jnp.maximum(top[...], peak_of(s))
-
-        top[...] = jnp.broadcast_to(jnp.max(top[...], axis=0, keepdims=True) * to_exp2, (8, 512))
-        total[...] = jnp.zeros(total.shape, jnp.float32)
-        acc[...] = jnp.zeros(acc.shape, jnp.float32)
+            top[:, cols] = jnp.maximum(top[:, cols], peak_of(s))
+
+    top[...] = jnp.broadcast_to(jnp.max(top[...], axis=0, keepdims=True) * to_exp2, top.shape)
+    for x, n, shift, low, high, begin, end in spans:
+        cols = slice(x * 512, (x + 1) * 512)
 
         @pl.loop(begin, end)
         def _(m):
             at = slot(m, n, shift)
-            gws[at] = nt(blocks(other_ref, 1, m, n), qg[g_rows, :]).reshape(n, block, 512)
-            p = jnp.exp2(flat(s_ref[at]) * to_exp2 - top[0:1])
-            p_other = jnp.exp2(flat(scores[at]) * to_exp2 - top[0:1])
-            total[...] = total[...] + (sum_of(p) + sum_of(p_other))
+            gws[at] = nt(blocks(other_ref, 1, m, n), qg[rows_of(x)[1], :]).reshape(n, block, 512)
+            p = jnp.exp2(flat(s_ref[at]) * to_exp2 - top[0:1, cols])
+            p_other = jnp.exp2(flat(scores[at]) * to_exp2 - top[0:1, cols])
+            total[:, cols] = total[:, cols] + (sum_of(p) + sum_of(p_other))
             p, p_other = p.astype(jnp.bfloat16), p_other.astype(jnp.bfloat16)
             p_ref[at] = p.reshape(n, block, 512)
             ps[at] = p_other.reshape(n, block, 512)
             values = jnp.concatenate([blocks(mine_ref, 1, m, n), blocks(other_ref, 1, m, n)], axis=0)
-            acc[...] = acc[...] + tn(values, jnp.concatenate([p, p_other], axis=0))
-
-        inv = 1.0 / jnp.sum(total[...], axis=0, keepdims=True)
-        part = inv.astype(jnp.bfloat16).astype(jnp.float32)
-        rest = inv - part
-        middle = rest.astype(jnp.bfloat16).astype(jnp.float32)
-        parts = jnp.where(row16 == 0, part, jnp.where(row16 == 1, middle, jnp.where(row16 == 2, rest - middle, 0.0)))
-        inv_down = tn(parts.astype(jnp.bfloat16), ones)
-        o = turned((acc[...] * inv).astype(jnp.bfloat16))
-        out_ref[q_rows, :] = o.astype(jnp.bfloat16)
-        g = qg[g_rows, :].astype(jnp.float32)
-        terms = g * o
-        part = terms.astype(jnp.bfloat16)
-        d = nt(ones, part) + nt(ones, (terms - part.astype(jnp.float32)).astype(jnp.bfloat16))
-        dot_ref[x] = d[:8]
-        gs_ref[q_rows, :] = (g * inv_down).astype(jnp.bfloat16)
-        qs_ref[q_rows, :] = (qg[q_rows, :].astype(jnp.float32) * (inv_down * scale)).astype(jnp.bfloat16)
-        inv_ref[x] = jnp.broadcast_to(inv * scale, (8, 512))
-        acc[...] = jnp.zeros(acc.shape, jnp.float32)
-
-        @pl.loop(begin, end)
-        def _(m):
-            backward(
-                n, slot(m, n, shift), ps, gws, other_ref, dot_ref[x][0:1], qs_ref[q_rows, :], gs_ref[q_rows, :],
-                acc, dother_ref, x == 0, m,
-            )
-
-        acc_ref[x] = acc[...]
+            acc[:, cols] = acc[:, cols] + tn(values, jnp.concatenate([p, p_other], axis=0))
+
+    inv = 1.0 / jnp.sum(total[...], axis=0, keepdims=True)
+    part = inv.astype(jnp.bfloat16).astype(jnp.float32)
+    rest = inv - part
+    middle = rest.astype(jnp.bfloat16).astype(jnp.float32)
+    parts = jnp.where(row16 == 0, part, jnp.where(row16 == 1, middle, jnp.where(row16 == 2, rest - middle, 0.0)))
+    inv_down = tn(parts.astype(jnp.bfloat16), ones)
+    o = turned((acc[...] * inv).astype(jnp.bfloat16))
+    out_ref[...] = o.astype(jnp.bfloat16)
+    g = qg[1024:, :].astype(jnp.float32)
+    terms = g * o
+    part = terms.astype(jnp.bfloat16)
+    d = nt(ones, part) + nt(ones, (terms - part.astype(jnp.float32)).astype(jnp.bfloat16))
+    dot_ref[...] = d[:8]
+    gs_ref[...] = (g * inv_down).astype(jnp.bfloat16)
+    qs_ref[...] = (qg[:1024, :].astype(jnp.float32) * (inv_down * scale)).astype(jnp.bfloat16)
+    inv_ref[...] = jnp.broadcast_to(inv * scale, inv_ref.shape)
+    acc_ref[...] = jnp.zeros(acc_ref.shape, jnp.float32)
+    for span in spans:
+        backward(span, ps, gws, other_ref, dot_ref, qs_ref, gs_ref, acc_ref, dother_ref)
 
 
 def grads_kernel(
-    plan_ref, mine_ref, gw_ref, p_ref, dot_ref, qs_ref, gs_ref, acc_ref, inv_ref,
+    plan_ref, mine_ref, gw_ref, p_ref, dot_ref, qs_ref, gs_ref, part_ref, inv_ref,
     dmine_ref, dq_ref,
     acc,
 ):
     chip = lax.axis_index("ctx")
-    for x in range(2):
-        n, shift, _, _, begin, end = span_of(x, plan_ref, chip)
-        q_rows = rows_of(x)[0]
-        if x == 0:
-            clear_rest(dmine_ref, end)
-        acc[...] = acc_ref[x]
-
-        @pl.loop(begin, end)
-        def _(m):
-            backward(
-                n, slot(m, n, shift), p_ref, gw_ref, mine_ref, dot_ref[x][0:1], qs_ref[q_rows, :], gs_ref[q_rows, :],
-                acc, dmine_ref, x == 0, m,
-            )
-
-        dq_ref[q_rows, :] = turned((acc[...] * inv_ref[x][0:1]).astype(jnp.bfloat16)).astype(jnp.bfloat16)
+    spans = spans_of(plan_ref, chip)
+    clear_rest(dmine_ref, spans[0][-1])
+    acc[...] = part_ref[...]
+    for span in spans:
+        backward(span, p_ref, gw_ref, mine_ref, dot_ref, qs_ref, gs_ref, acc, dmine_ref)
+    dq_ref[...] = turned((acc[...] * inv_ref[0:1]).astype(jnp.bfloat16)).astype(jnp.bfloat16)
 
 
 def join_kernel(mine_ref, other_ref, out_ref, dq_ref, back_ref):
@@ -486,24 +480,24 @@
 
 def attention(lengths, other_lengths, plan, mine, other, info, qg):
     bf16, f32 = jnp.bfloat16, jnp.float32
-    slots = (pairs + 3, block, 512)
-    rows = ((2, 8, 512), f32)
-    acc = ((2, head, 512), f32)
+    slots = (pairs + 6, block, 512)
+    rows = ((8, 1024), f32)
+    acc = ((head, 1024), f32)
     heads = ((1024, head), bf16)
     places = [((block, block), f32), ((8, block), f32)]
-    s, gw, top = kernel(
+    s, gw, top, key_pos, bound = kernel(
         "scores", scores_kernel, (lengths, other_lengths, plan, mine, info, qg), 3,
-        [(slots, f32), (slots, f32), rows], places, 12,
+        [(slots, f32), (slots, f32), ((8, 1024), f32)] + places, [], 12,
     )
     dother, out, p, dot, qs, gs, partial, inv = kernel(
-        "weights", weights_kernel, (lengths, other_lengths, plan, mine, other, info, qg, s, top), 3,
+        "weights", weights_kernel, (plan, mine, other, qg, s, top, key_pos, bound), 1,
         [((kv_rows, block, head), bf16), heads, (slots, bf16), rows, heads, heads, acc, rows],
-        [(slots, f32), (slots, f32), (slots, bf16), ((8, 512), f32), ((8, 512), f32), ((head, 512), f32)] + places, 24,
+        [(slots, f32), (slots, f32), (slots, bf16), rows, rows, acc], 24,
     )
     other_terms = swap(dother)
     dmine, dq = kernel(
         "grads", grads_kernel, (plan, mine, gw, p, dot, qs, gs, partial, inv), 1,
-        [((kv_rows, block, head), bf16), heads], [((head, 512), f32)], 12,
+        [((kv_rows, block, head), bf16), heads], [acc], 12,
     )
     return dmine, other_terms, out, dq
 

time: 97.6 us -> 94.8 us (0.971)
  Pallas kernels: 24.7 us -> 21.7 us
    pallas_call x3, Pallas kernels: 17.1 us -> 14.1 us  [kernel(): pl.pallas_call(body, out_shape=tuple((jax.ShapeDtypeStruct(shape, dtype)...]
  transfers between devices with their start and end apart: 3 -> 3, of which waited for: 1 -> 1; matrix products, arithmetic and copies ran while one was open for 0% -> 0% of each run, Pallas kernels for 8% -> 6%
where the time goes in v6:
time: 94.8 us; the launch traced here: 94.6 us
  blocking collectives  67.9 us (72%)
  Pallas kernels  21.7 us (23%)
  starting transfers between devices  2.76 us (3%)
  waiting for transfers between devices  0.96 us (1%)
    all_to_all x2, blocking collectives, exchange(): lax.all_to_all(x, ('dp', 'ctx'), split_axis=0, concat_axis=0, tiled=True)  67.9 us
    pallas_call x3, Pallas kernels, kernel(): pl.pallas_call(body, out_shape=tuple((jax.ShapeDtypeStruct(shape, dtype)...  14.1 us
    pallas_call x1, Pallas kernels, on_device(): pl.pallas_call(pack_kernel, out_shape=(jax.ShapeDtypeStruct((128, send_ro...  3.98 us
    ppermute x3, starting transfers between devices, swap(): return lax.ppermute(x, 'dp', [(0, 1), (1, 0)])  2.76 us
    pallas_call x1, Pallas kernels, on_device(): pl.pallas_call(unpack_kernel, out_shape=(jax.ShapeDtypeStruct((block, 8 *...  2.43 us
  transfers between devices with their start and end apart: 3, of which 1 were waited for; matrix products, arithmetic and copies ran while one was open for 0% of the time, Pallas kernels for 6%

profile of v6, /device:TPU:1, one launch (start us, length us, event | category | flops | bytes accessed | tf_op | source)
XLA Modules:
  0.0 94.6 jit_solution(5485401869265476135)
XLA Ops:
  0.6 1.5 %collective-permute-start = (s32[1,16]{1,0:T(1,128)}, s32[1,16]{1,0:T(1,128)S(1)}, u32[]{:S(2)}, u32[]{:S(2)}) collective-permute-start(s32[1,16]{1,0:T(1,128)} %mine_len.1), channel_id=1, source_target_pairs={{0,64},{64,0},{1,65},{65,1},{2,66},{66,2},{3,67},{67,3},{4,68},{68... | collective-permute-start | bytes 200 | tf_op jit(solution)/shard_map/ppermute | solution.py:462
  2.1 1.0 %collective-permute-done.other_hbm.other_len = s32[1,16]{1,0:T(1,128)S(1)} collective-permute-done((s32[1,16]{1,0:T(1,128)}, s32[1,16]{1,0:T(1,128)S(1)}, u32[]{:S(2)}, u32[]{:S(2)}) %collective-permute-start) | collective-permute-done | bytes 96 | tf_op jit(solution)/shard_map/ppermute | solution.py:462
  3.1 0.0 copy-start.2
  3.1 0.5 copy-done.2
  3.6 4.0 %pack.1 = (bf16[128,56,128]{2,1,0:T(8,128)(2,1)}, s32[8,128]{1,0:T(8,128)}) custom-call(s32[1,16]{1,0:T(1,128)} %mine_len.1, s32[1,16]{1,0:T(1,128)} %copy-done.2, s32[1,128]{1,0:T(1,128)} %bitcast.1, bf16[128,1024]{1,0:T(8,128)(2,1)} %q_hbm.1, bf16[128,256]{1,0:T(8,128)(2,1)} %kv_hbm.1, bf16[128,1024]{1,0:T(8,128)(2,1)} %g_hbm.1), custom_call_target="tpu_custom_call" | custom-call | tf_op jit(solution)/shard_map/pack/pallas_call | solution.py:509
  7.6 37.3 %all_to_all.10.got_ref = bf16[128,56,128]{2,1,0:T(8,128)(2,1)S(1)} all-to-all(bf16[128,56,128]{2,1,0:T(8,128)(2,1)} %get-tuple-element.24), channel_id=1, replica_groups=mesh['dp'=2,'ctx'=64] {'dp','ctx'}, dimensions={0} | all-to-all | bytes 3670016 | tf_op jit(solution)/shard_map/all_to_all | solution.py:466
  44.9 0.0 copy-start
  44.9 0.0 copy-start.1
  44.9 0.5 split.1
  45.4 1.1 %collective-permute-start.1 = (bf16[36,128,128]{2,1,0:T(8,128)(2,1)S(1)}, bf16[36,128,128]{2,1,0:T(8,128)(2,1)S(1)}, u32[]{:S(2)}, u32[]{:S(2)}) collective-permute-start(bf16[36,128,128]{2,1,0:T(8,128)(2,1)S(1)} %get-tuple-element.25.mine_ref), channel_id=1, source_target_pairs={{0,64},{64,0},{1,65},{65,1},{2,66},{66,2},{3,67},{67,3},{4,68},{68... | collective-permute-start | bytes 3538952 | tf_op jit(solution)/shard_map/ppermute | solution.py:462
  46.5 0.0 copy-done
  46.5 0.0 copy-done.1
  46.5 0.0 copy-done.3
  46.5 2.7 %scores.1 = (f32[24,128,512]{2,1,0:T(8,128)S(1)}, f32[24,128,512]{2,1,0:T(8,128)S(1)}, f32[8,1024]{1,0:T(8,128)S(1)}, f32[128,128]{1,0:T(8,128)S(1)}, f32[8,128]{1,0:T(8,128)S(1)}) custom-call(s32[1,16]{1,0:T(1,128)S(1)} %copy-done.1, s32[1,16]{1,0:T(1,128)S(1)} %copy-done.3, s32[8,128]{1,0:T(8,128)S(1)} %copy-done, ...), custom_call_target="tpu_custom_call" | custom-call | tf_op jit(solution)/shard_map/scores/pallas_call | solution.py:470
  49.2 0.0 collective-permute-done.1.other_ref
  49.2 8.0 %weights.1 = (bf16[36,128,128]{2,1,0:T(8,128)(2,1)S(1)}, bf16[1024,128]{1,0:T(8,128)(2,1)S(1)}, bf16[24,128,512]{2,1,0:T(8,128)(2,1)S(1)}, f32[8,1024]{1,0:T(8,1...) custom-call(s32[8,128]{1,0:T(8,128)S(1)} %copy-done, ...), custom_call_target="tpu_custom_call" | custom-call | tf_op jit(solution)/shard_map/weights/pallas_call | solution.py:470
  57.2 0.2 collective-permute-start.2
  57.4 3.4 %grads.1 = (bf16[36,128,128]{2,1,0:T(8,128)(2,1)S(1)}, bf16[1024,128]{1,0:T(8,128)(2,1)S(1)}) custom-call(s32[8,128]{1,0:T(8,128)S(1)} %copy-done, bf16[36,128,128]{2,1,0:T(8,128)(2,1)S(1)} %get-tuple-element.25.mine_ref, f32[24,128,512]{2,1,0:T(8,128)S(1)} %get-tuple-element.28.gw_ref, bf16[24,128,512]{2,1,0:T(8,128)(2,1)S(1)} %get-tuple-element.33.p_ref, ...), custom_call_target="tpu_custom_call" | custom-call | tf_op jit(solution)/shard_map/grads/pallas_call | solution.py:470
  60.8 0.0 collective-permute-done.2.other_ref
  60.8 0.7 join.1
  61.5 0.0 copy-start.4
  61.5 30.6 %all_to_all.11.got_ref = bf16[128,56,128]{2,1,0:T(8,128)(2,1)S(1)} all-to-all(bf16[128,56,128]{2,1,0:T(8,128)(2,1)S(1)} %join.1), channel_id=1, replica_groups=mesh['dp'=2,'ctx'=64] {'dp','ctx'}, dimensions={0} | all-to-all | bytes 3670016 | tf_op jit(solution)/shard_map/all_to_all | solution.py:466
  92.1 0.0 copy-done.4
  92.1 2.4 %unpack.1 = (bf16[128,1024]{1,0:T(8,128)(2,1)}, bf16[128,1024]{1,0:T(8,128)(2,1)}, bf16[128,256]{1,0:T(8,128)(2,1)}) custom-call(s32[1,128]{1,0:T(1,128)S(1)} %bitcast.2, s32[8,128]{1,0:T(8,128)S(1)} %copy-done, bf16[128,56,128]{2,1,0:T(8,128)(2,1)S(1)} %all_to_all.11.got_ref), custom_call_target="tpu_custom_call" | custom-call | tf_op jit(solution)/shard_map/unpack/pallas_call | solution.py:552
  (1 shorter events, 0.0 us)
Async XLA Ops:
  0.6 2.5 %collective-permute-start = (s32[1,16]{1,0:T(1,128)}, s32[1,16]{1,0:T(1,128)S(1)}, u32[]{:S(2)}, u32[]{:S(2)}) collective-permute-start(s32[1,16]{1,0:T(1,128)} %mine_len.1), channel_id=1, source_target_pairs={{0,64},{64,0},{1,65},{65,1},{2,66},{66,2},{3,67},{67,3},{4,68},{68... | collective-permute-start | bytes 200 | tf_op jit(solution)/shard_map/ppermute | solution.py:462
  3.1 0.5 copy-start.2
  44.9 1.6 %copy-start = (s32[8,128]{1,0:T(8,128)S(1)}, s32[8,128]{1,0:T(8,128)}, u32[]{:S(2)}) copy-start(s32[8,128]{1,0:T(8,128)} %get-tuple-element.23.plan_ref) | copy-start | bytes 12292
  44.9 1.6 %copy-start.1 = (s32[1,16]{1,0:T(1,128)S(1)}, s32[1,16]{1,0:T(1,128)}, u32[]{:S(2)}) copy-start(s32[1,16]{1,0:T(1,128)} %mine_len.1) | copy-start | bytes 196
  44.9 1.6 %copy-start.3 = (s32[1,16]{1,0:T(1,128)S(1)}, s32[1,16]{1,0:T(1,128)}, u32[]{:S(2)}) copy-start(s32[1,16]{1,0:T(1,128)} %copy-done.2) | copy-start | bytes 196
  45.4 3.8 %collective-permute-start.1 = (bf16[36,128,128]{2,1,0:T(8,128)(2,1)S(1)}, bf16[36,128,128]{2,1,0:T(8,128)(2,1)S(1)}, u32[]{:S(2)}, u32[]{:S(2)}) collective-permute-start(bf16[36,128,128]{2,1,0:T(8,128)(2,1)S(1)} %get-tuple-element.25.mine_ref), channel_id=1, source_target_pairs={{0,64},{64,0},{1,65},{65,1},{2,66},{66,2},{3,67},{67,3},{4,68},{68... | collective-permute-start | bytes 3538952 | tf_op jit(solution)/shard_map/ppermute | solution.py:462
  57.2 3.6 %collective-permute-start.2 = (bf16[36,128,128]{2,1,0:T(8,128)(2,1)S(1)}, bf16[36,128,128]{2,1,0:T(8,128)(2,1)S(1)}, u32[]{:S(2)}, u32[]{:S(2)}) collective-permute-start(bf16[36,128,128]{2,1,0:T(8,128)(2,1)S(1)} %get-tuple-element.40), channel_id=1, source_target_pairs={{0,64},{64,0},{1,65},{65,1},{2,66},{66,2},{3,67},{67,3},{4,68},{68... | collective-permute-start | bytes 3538952 | tf_op jit(solution)/shard_map/ppermute | solution.py:462
  61.5 30.6 %copy-start.4 = (s32[128]{0:T(128)S(1)}, s32[128]{0:T(128)}, u32[]{:S(2)}) copy-start(s32[128]{0:T(128)} %param.8) | copy-start | bytes 1540

commit v7 on v6

--- a/solution.py
+++ b/solution.py
@@ -55,44 +55,26 @@
     return block_line, count_line
 
 
-def pack_kernel(
-    mine_hbm, other_hbm, place_hbm, q_hbm, kv_hbm, g_hbm, out_hbm, plan_ref,
-    mine_ref, other_ref, place_ref, q_ref, kv_ref, g_ref, out_ref, sems,
-):
-    moves = [
-        pltpu.make_async_copy(src, dst, sems.at[i])
-        for i, (src, dst) in enumerate(
-            [
-                (mine_hbm, mine_ref),
-                (other_hbm, other_ref),
-                (place_hbm, place_ref),
-                (kv_hbm, kv_ref),
-                (q_hbm, q_ref),
-                (g_hbm, g_ref),
-            ]
-        )
-    ]
-    for move in moves:
-        move.start()
-    for move in moves[:3]:
-        move.wait()
+def slots_kernel(place_ref, line_ref):
+    lane = lax.broadcasted_iota(jnp.int32, (block, block), 1).astype(jnp.float32)
+    slots_down = down(place_ref[...] & (block - 1))
+    line = jnp.sum(jnp.where(down(place_ref[...] >> 7) == lane, slots_down, 0.0), axis=0, keepdims=True)
+    line_ref[...] = jnp.broadcast_to(line, (8, block))
+
+
+def pack_kernel(mine_ref, other_ref, place_ref, line_ref, q_ref, kv_ref, g_ref, out_ref, plan_ref):
     block_line, count_line = make_plan(lax.axis_index("dp"), mine_ref, other_ref)
     row8 = lax.broadcasted_iota(jnp.int32, (8, block), 0)
     plan_ref[...] = jnp.where(row8 == 0, block_line, jnp.where(row8 == 1, count_line, 0.0)).astype(jnp.int32)
     block_down = down(block_line).astype(jnp.int32)
     count_down = down(count_line).astype(jnp.int32)
     rows = place_ref[...] >> 7
-    lane = lax.broadcasted_iota(jnp.int32, (block, block), 1)
-    slots_down = down(place_ref[...] & (block - 1))
-    slot_line = jnp.sum(jnp.where(down(rows) == lane.astype(jnp.float32), slots_down, 0.0), axis=0, keepdims=True)
+    slot_line = line_ref[0:1]
     extra = jnp.where(row8 == kv_rows % 8, slot_line, 0.0)
-    moves[3].wait()
     kv = jnp.concatenate([kv_ref[:, :head], kv_ref[:, head:]], axis=0)
     r = lax.broadcasted_iota(jnp.int32, (group, head_rows, block), 1)
     half = (r & 1) * other_half
     j = lax.broadcasted_iota(jnp.int32, (group, 8, block), 1)
-    moves[4].wait()
-    moves[5].wait()
     both = []
     for core in range(2):
         heads = [slice((4 * core + h) * head, (4 * core + h + 1) * head) for h in range(4)]
@@ -101,7 +83,6 @@
     def spread(x, n):
         return jnp.broadcast_to(x[:, None, :], (group, n, block))
 
-    sends = []
     for chip in range(0, 64, group):
         first = block_down[chip : chip + group]
         first_count = count_down[chip : chip + group]
@@ -132,11 +113,6 @@
             got = jnp.dot(heads, both[core], preferred_element_type=jnp.float32).astype(jnp.bfloat16)
             out_ref[t : t + group, head_rows : head_rows + 8, :] = got[:, :head].reshape(group, 8, head)
             out_ref[t : t + group, head_rows + 8 :, :] = got[:, head:].reshape(group, 8, head)
-            at = pl.ds(t, group)
-            sends.append(pltpu.make_async_copy(out_ref.at[at], out_hbm.at[at], sems.at[6 + len(sends)]))
-            sends[-1].start()
-    for send in sends:
-        send.wait()
 
 
 def spread_lanes(plan, width):
@@ -506,27 +482,26 @@
     bf16, f32 = jnp.bfloat16, jnp.float32
     place = placement.reshape(1, block)
     other_lengths = swap(doc_lengths)
+    line = pl.pallas_call(
+        slots_kernel,
+        out_shape=jax.ShapeDtypeStruct((8, block), f32),
+        in_specs=vmem(1),
+        out_specs=vmem(1)[0],
+        compiler_params=params(8),
+        cost_estimate=pl.CostEstimate(flops=4 * 10**9, bytes_accessed=0, transcendentals=0),
+        name="slots",
+    )(place)
     sent, plan = pl.pallas_call(
         pack_kernel,
         out_shape=(
             jax.ShapeDtypeStruct((128, send_rows, head), bf16),
             jax.ShapeDtypeStruct((8, block), jnp.int32),
         ),
-        in_specs=[pl.BlockSpec(memory_space=pl.ANY)] * 6,
-        out_specs=(pl.BlockSpec(memory_space=pl.ANY), vmem(1)[0]),
-        scratch_shapes=[
-            pltpu.SMEM((1, 16), jnp.int32),
-            pltpu.SMEM((1, 16), jnp.int32),
-            pltpu.VMEM((1, block), jnp.int32),
-            pltpu.VMEM((block, 8 * head), bf16),
-            pltpu.VMEM((block, 2 * head), bf16),
-            pltpu.VMEM((block, 8 * head), bf16),
-            pltpu.VMEM((128, send_rows, head), bf16),
-            pltpu.SemaphoreType.DMA((6 + 128 // group,)),
-        ],
-        compiler_params=pltpu.CompilerParams(vmem_limit_bytes=58 * mib),
+        in_specs=[smem()] * 2 + vmem(5),
+        out_specs=tuple(vmem(2)),
+        compiler_params=params(24),
         name="pack",
-    )(doc_lengths, other_lengths, place, queries, keys_values, grad_out)
+    )(doc_lengths, other_lengths, place, line, queries, keys_values, grad_out)
     mine, info, qg = pl.pallas_call(
         split_kernel,
         out_shape=(

time: 94.8 us -> 92.9 us (0.980)
  Pallas kernels: 21.7 us -> 20.1 us
    pallas_call x1, Pallas kernels: 3.98 us -> 2.32 us  [on_device(): pl.pallas_call(pack_kernel, out_shape=(jax.ShapeDtypeStruct((128, send_ro...]
  transfers between devices with their start and end apart: 3 -> 3, of which waited for: 1 -> 1; matrix products, arithmetic and copies ran while one was open for 0% -> 0% of each run, Pallas kernels for 6% -> 7%
where the time goes in v7:
time: 92.9 us; the launch traced here: 92.7 us
  blocking collectives  67.5 us (73%)
  Pallas kernels  20.1 us (22%)
  starting transfers between devices  2.77 us (3%)
  local copies, waits for them, and re-layouts  1.4 us (2%)
    all_to_all x2, blocking collectives, exchange(): lax.all_to_all(x, ('dp', 'ctx'), split_axis=0, concat_axis=0, tiled=True)  67.5 us
    pallas_call x3, Pallas kernels, kernel(): pl.pallas_call(body, out_shape=tuple((jax.ShapeDtypeStruct(shape, dtype)...  14.1 us
    ppermute x3, starting transfers between devices, swap(): return lax.ppermute(x, 'dp', [(0, 1), (1, 0)])  2.77 us
    pallas_call x1, Pallas kernels, on_device(): pl.pallas_call(unpack_kernel, out_shape=(jax.ShapeDtypeStruct((block, 8 *...  2.42 us
    pallas_call x1, Pallas kernels, on_device(): pl.pallas_call(pack_kernel, out_shape=(jax.ShapeDtypeStruct((128, send_ro...  2.32 us
  transfers between devices with their start and end apart: 3, of which 1 were waited for; matrix products, arithmetic and copies ran while one was open for 0% of the time, Pallas kernels for 7%

profile of v7, /device:TPU:1, one launch (start us, length us, event | category | flops | bytes accessed | tf_op | source)
XLA Modules:
  0.0 92.7 jit_solution(8765122690577906606)
XLA Ops:
  0.6 1.5 %collective-permute-start = (s32[1,16]{1,0:T(1,128)}, s32[1,16]{1,0:T(1,128)S(1)}, u32[]{:S(2)}, u32[]{:S(2)}) collective-permute-start(s32[1,16]{1,0:T(1,128)} %mine_len.1), channel_id=1, source_target_pairs={{0,64},{64,0},{1,65},{65,1},{2,66},{66,2},{3,67},{67,3},{4,68},{68... | collective-permute-start | bytes 200 | tf_op jit(solution)/shard_map/ppermute | solution.py:438
  2.1 0.0 copy-start.4
  2.1 0.7 copy-done.4
  2.8 0.1 slots.1.line_ref
  2.9 0.2 collective-permute-done.other_ref.other_len
  3.1 0.7 copy-done
  3.7 0.1 copy-done.1
  3.8 0.0 copy-done.2
  3.8 0.0 copy-done.3
  3.8 2.3 %pack.1 = (bf16[128,56,128]{2,1,0:T(8,128)(2,1)S(1)}, s32[8,128]{1,0:T(8,128)S(1)}) custom-call(s32[1,16]{1,0:T(1,128)S(1)} %copy-done.3, s32[1,16]{1,0:T(1,128)S(1)} %collective-permute-done.other_ref.other_len, s32[1,128]{1,0:T(1,128)S(1)} %bitcast.2, f32[8,128]{1,0:T(8,128)S(1)} %slots.1.line_ref, bf16[128,1024]{1,0:T(8,128)(2,1)S(1)} %copy-done, ...), custom_call_target="tpu_custom_call" | custom-call | tf_op jit(solution)/shard_map/pack/pallas_call | solution.py:494
  6.2 36.9 %all_to_all.10.got_ref = bf16[128,56,128]{2,1,0:T(8,128)(2,1)S(1)} all-to-all(bf16[128,56,128]{2,1,0:T(8,128)(2,1)S(1)} %get-tuple-element.24), channel_id=1, replica_groups=mesh['dp'=2,'ctx'=64] {'dp','ctx'}, dimensions={0} | all-to-all | bytes 3670016 | tf_op jit(solution)/shard_map/all_to_all | solution.py:442
  43.0 0.5 split.1
  43.5 1.1 %collective-permute-start.1 = (bf16[36,128,128]{2,1,0:T(8,128)(2,1)S(1)}, bf16[36,128,128]{2,1,0:T(8,128)(2,1)S(1)}, u32[]{:S(2)}, u32[]{:S(2)}) collective-permute-start(bf16[36,128,128]{2,1,0:T(8,128)(2,1)S(1)} %get-tuple-element.25.mine_ref), channel_id=1, source_target_pairs={{0,64},{64,0},{1,65},{65,1},{2,66},{66,2},{3,67},{67,3},{4,68},{68... | collective-permute-start | bytes 3538952 | tf_op jit(solution)/shard_map/ppermute | solution.py:438
  44.6 2.7 %scores.1 = (f32[24,128,512]{2,1,0:T(8,128)S(1)}, f32[24,128,512]{2,1,0:T(8,128)S(1)}, f32[8,1024]{1,0:T(8,128)S(1)}, f32[128,128]{1,0:T(8,128)S(1)}, f32[8,128]{1,0:T(8,128)S(1)}) custom-call(s32[1,16]{1,0:T(1,128)S(1)} %copy-done.3, s32[1,16]{1,0:T(1,128)S(1)} %collective-permute-done.other_ref.other_len, s32[8,128]{1,0:T(8,128)S(1)} %get-tuple-element.23.plan_ref, ...), custom_call_target="tpu_custom_call" | custom-call | tf_op jit(solution)/shard_map/scores/pallas_call | solution.py:446
  47.3 0.0 collective-permute-done.1.other_ref
  47.3 8.0 %weights.1 = (bf16[36,128,128]{2,1,0:T(8,128)(2,1)S(1)}, bf16[1024,128]{1,0:T(8,128)(2,1)S(1)}, bf16[24,128,512]{2,1,0:T(8,128)(2,1)S(1)}, f32[8,1024]{1,0:T(8,1...) custom-call(s32[8,128]{1,0:T(8,128)S(1)} %get-tuple-element.23.plan_, ...), custom_call_target="tpu_custom_call" | custom-call | tf_op jit(solution)/shard_map/weights/pallas_call | solution.py:446
  55.3 0.2 collective-permute-start.2
  55.5 3.4 %grads.1 = (bf16[36,128,128]{2,1,0:T(8,128)(2,1)S(1)}, bf16[1024,128]{1,0:T(8,128)(2,1)S(1)}) custom-call(s32[8,128]{1,0:T(8,128)S(1)} %get-tuple-element.23.plan_ref, bf16[36,128,128]{2,1,0:T(8,128)(2,1)S(1)} %get-tuple-element.25.mine_ref, f32[24,128,512]{2,1,0:T(8,128)S(1)} %get-tuple-element.28.gw_ref, ...), custom_call_target="tpu_custom_call" | custom-call | tf_op jit(solution)/shard_map/grads/pallas_call | solution.py:446
  58.9 0.0 collective-permute-done.2.other_ref
  58.9 0.7 join.1
  59.7 0.0 copy-start.5
  59.7 30.6 %all_to_all.11.got_ref = bf16[128,56,128]{2,1,0:T(8,128)(2,1)S(1)} all-to-all(bf16[128,56,128]{2,1,0:T(8,128)(2,1)S(1)} %join.1), channel_id=1, replica_groups=mesh['dp'=2,'ctx'=64] {'dp','ctx'}, dimensions={0} | all-to-all | bytes 3670016 | tf_op jit(solution)/shard_map/all_to_all | solution.py:442
  90.3 0.0 copy-done.5
  90.3 2.4 %unpack.1 = (bf16[128,1024]{1,0:T(8,128)(2,1)}, bf16[128,1024]{1,0:T(8,128)(2,1)}, bf16[128,256]{1,0:T(8,128)(2,1)}) custom-call(s32[1,128]{1,0:T(1,128)S(1)} %bitcast.3, s32[8,128]{1,0:T(8,128)S(1)} %get-tuple-element.23.plan_ref, bf16[128,56,128]{2,1,0:T(8,128)(2,1)S(1)} %all_to_all.11.got_ref), custom_call_target="tpu_custom_call" | custom-call | tf_op jit(solution)/shard_map/unpack/pallas_call | solution.py:527
  (4 shorter events, 0.0 us)
Async XLA Ops:
  0.6 2.5 %collective-permute-start = (s32[1,16]{1,0:T(1,128)}, s32[1,16]{1,0:T(1,128)S(1)}, u32[]{:S(2)}, u32[]{:S(2)}) collective-permute-start(s32[1,16]{1,0:T(1,128)} %mine_len.1), channel_id=1, source_target_pairs={{0,64},{64,0},{1,65},{65,1},{2,66},{66,2},{3,67},{67,3},{4,68},{68... | collective-permute-start | bytes 200 | tf_op jit(solution)/shard_map/ppermute | solution.py:438
  2.1 0.7 copy-start.4
  2.8 0.9 %copy-start = (bf16[128,1024]{1,0:T(8,128)(2,1)S(1)}, bf16[128,1024]{1,0:T(8,128)(2,1)}, u32[]{:S(2)}) copy-start(bf16[128,1024]{1,0:T(8,128)(2,1)} %q_ref.1) | copy-start | bytes 786436
  2.8 1.0 %copy-start.1 = (bf16[128,1024]{1,0:T(8,128)(2,1)S(1)}, bf16[128,1024]{1,0:T(8,128)(2,1)}, u32[]{:S(2)}) copy-start(bf16[128,1024]{1,0:T(8,128)(2,1)} %g_ref.1) | copy-start | bytes 786436
  2.8 1.0 %copy-start.2 = (bf16[128,256]{1,0:T(8,128)(2,1)S(1)}, bf16[128,256]{1,0:T(8,128)(2,1)}, u32[]{:S(2)}) copy-start(bf16[128,256]{1,0:T(8,128)(2,1)} %kv_ref.1) | copy-start | bytes 196612
  2.8 1.0 %copy-start.3 = (s32[1,16]{1,0:T(1,128)S(1)}, s32[1,16]{1,0:T(1,128)}, u32[]{:S(2)}) copy-start(s32[1,16]{1,0:T(1,128)} %mine_len.1) | copy-start | bytes 196
  43.5 3.8 %collective-permute-start.1 = (bf16[36,128,128]{2,1,0:T(8,128)(2,1)S(1)}, bf16[36,128,128]{2,1,0:T(8,128)(2,1)S(1)}, u32[]{:S(2)}, u32[]{:S(2)}) collective-permute-start(bf16[36,128,128]{2,1,0:T(8,128)(2,1)S(1)} %get-tuple-element.25.mine_ref), channel_id=1, source_target_pairs={{0,64},{64,0},{1,65},{65,1},{2,66},{66,2},{3,67},{67,3},{4,68},{68... | collective-permute-start | bytes 3538952 | tf_op jit(solution)/shard_map/ppermute | solution.py:438
  55.3 3.6 %collective-permute-start.2 = (bf16[36,128,128]{2,1,0:T(8,128)(2,1)S(1)}, bf16[36,128,128]{2,1,0:T(8,128)(2,1)S(1)}, u32[]{:S(2)}, u32[]{:S(2)}) collective-permute-start(bf16[36,128,128]{2,1,0:T(8,128)(2,1)S(1)} %get-tuple-element.40), channel_id=1, source_target_pairs={{0,64},{64,0},{1,65},{65,1},{2,66},{66,2},{3,67},{67,3},{4,68},{68... | collective-permute-start | bytes 3538952 | tf_op jit(solution)/shard_map/ppermute | solution.py:438
  59.7 30.6 %copy-start.5 = (s32[128]{0:T(128)S(1)}, s32[128]{0:T(128)}, u32[]{:S(2)}) copy-start(s32[128]{0:T(128)} %param.8) | copy-start | bytes 1540

commit v8 on v7

--- a/solution.py
+++ b/solution.py
@@ -7,11 +7,12 @@
 
 block = 128
 head = 128
-entries = 36
-pairs = entries // 2
-kv_rows = 2 * pairs
-head_rows = 40
-send_rows = 56
+entries = 35
+pairs = 18
+tiles = 2 * pairs
+kv_rows = 4 * pairs
+out_rows = kv_rows + 16
+send_rows = kv_rows + 32
 group = 16
 other_half = 1000
 nothing = -100000
@@ -70,54 +71,55 @@
     count_down = down(count_line).astype(jnp.int32)
     rows = place_ref[...] >> 7
     slot_line = line_ref[0:1]
-    extra = jnp.where(row8 == kv_rows % 8, slot_line, 0.0)
+    extra = jnp.where(row8 == 7, slot_line, 0.0)
     kv = jnp.concatenate([kv_ref[:, :head], kv_ref[:, head:]], axis=0)
-    r = lax.broadcasted_iota(jnp.int32, (group, head_rows, block), 1)
-    half = (r & 1) * other_half
+    r = lax.broadcasted_iota(jnp.int32, (group, kv_rows, block), 1)
+    entry = ((r >> 2) << 1) + (r & 1)
+    half = ((r >> 1) & 1) * other_half
     j = lax.broadcasted_iota(jnp.int32, (group, 8, block), 1)
     both = []
-    for core in range(2):
-        heads = [slice((4 * core + h) * head, (4 * core + h + 1) * head) for h in range(4)]
+    for part in range(2):
+        heads = [slice((4 * part + h) * head, (4 * part + h + 1) * head) for h in range(4)]
         both.append(jnp.concatenate([jnp.concatenate([q_ref[:, at], g_ref[:, at]], axis=1) for at in heads], axis=0))
 
     def spread(x, n):
         return jnp.broadcast_to(x[:, None, :], (group, n, block))
 
     for chip in range(0, 64, group):
-        first = block_down[chip : chip + group]
-        first_count = count_down[chip : chip + group]
+        at = slice(chip, chip + group)
+        first = block_down[at]
+        first_count = count_down[at]
         second = block_down[64 + chip : 64 + chip + group]
         second_count = count_down[64 + chip : 64 + chip + group]
+        code = jnp.where(
+            entry < spread(first_count, kv_rows),
+            entry + spread(first - first_count + 1, kv_rows),
+            jnp.where(
+                (entry >= spread(entries - second_count, kv_rows)) & (entry < entries),
+                entry + spread(second - (entries - 1), kv_rows),
+                nothing,
+            ),
+        )
+        code = (code + half).reshape(group * kv_rows, block)
+        pick = jnp.concatenate([one_hot(code == rows), one_hot(code == rows + other_half)], axis=1)
+        got = jnp.dot(pick, kv, preferred_element_type=jnp.float32).reshape(group, kv_rows, head)
+        tail = got[:, kv_rows - 8 :, :] + extra[None]
+        got = jnp.concatenate([got[:, : kv_rows - 8, :], tail], axis=1)
+        out_ref[at, :kv_rows, :] = got.astype(jnp.bfloat16)
         wanted = jnp.where(j < 4, spread(first, 8), spread(second, 8)) == rows[None]
         heads = jnp.concatenate(
             [one_hot(wanted & ((j & 3) == h)).reshape(group * 8, block) for h in range(4)], axis=1
         )
-        for core in range(2):
-            t = core * 64 + chip
-            entry = (r & -2) + core
-            code = jnp.where(
-                entry < spread(first_count, head_rows),
-                entry + spread(first - first_count + 1, head_rows),
-                jnp.where(
-                    entry >= spread(entries - second_count, head_rows),
-                    entry + spread(second - (entries - 1), head_rows),
-                    nothing,
-                ),
-            )
-            code = (jnp.where(r < kv_rows, code, nothing) + half).reshape(group * head_rows, block)
-            pick = jnp.concatenate([one_hot(code == rows), one_hot(code == rows + other_half)], axis=1)
-            got = jnp.dot(pick, kv, preferred_element_type=jnp.float32).reshape(group, head_rows, head)
-            tail = got[:, head_rows - 8 :, :] + extra[None]
-            got = jnp.concatenate([got[:, : head_rows - 8, :], tail], axis=1)
-            out_ref[t : t + group, :head_rows, :] = got.astype(jnp.bfloat16)
-            got = jnp.dot(heads, both[core], preferred_element_type=jnp.float32).astype(jnp.bfloat16)
-            out_ref[t : t + group, head_rows : head_rows + 8, :] = got[:, :head].reshape(group, 8, head)
-            out_ref[t : t + group, head_rows + 8 :, :] = got[:, head:].reshape(group, 8, head)
+        for part in range(2):
+            got = jnp.dot(heads, both[part], preferred_element_type=jnp.float32).astype(jnp.bfloat16)
+            to = kv_rows + 8 * part
+            out_ref[at, to : to + 8, :] = got[:, :head].reshape(group, 8, head)
+            out_ref[at, to + 16 : to + 24, :] = got[:, head:].reshape(group, 8, head)
 
 
 def spread_lanes(plan, width):
-    chip = lax.broadcasted_iota(jnp.int32, (block, 64 * width), 0) * width
-    lane = lax.broadcasted_iota(jnp.int32, (block, 64 * width), 1)
+    chip = lax.broadcasted_iota(jnp.int32, (64, 64 * width), 0) * width
+    lane = lax.broadcasted_iota(jnp.int32, (64, 64 * width), 1)
     return jnp.dot(plan, one_hot((lane >= chip) & (lane < chip + width)), preferred_element_type=jnp.float32)
 
 
@@ -138,44 +140,42 @@
     row = lax.broadcasted_iota(jnp.int32, (16, block), 0)
     for i, line in enumerate(lines):
         stacked = jnp.where((row == i) & (lane[0:1] < 64), line, stacked)
-    stacked = stacked.astype(jnp.bfloat16)
+    stacked = stacked.astype(jnp.bfloat16)[:, :64]
     wide = spread_lanes(stacked, 8)
     j = lax.broadcasted_iota(jnp.int32, (1, 512), 1) & 7
     code = jnp.where(j < 4, wide[0:1], wide[2:3])
     rows_wide = jnp.concatenate([rows_down] * 4, axis=1)
     picks = [one_hot(jnp.where((j & 3) == h, code, float(nothing)) == rows_wide) for h in range(4)]
-    for core in range(2):
+    for part in range(2):
+        to = kv_rows + 8 * part
         both = jnp.concatenate(
-            [
-                got_ref[core * 64 : core * 64 + 64, head_rows : head_rows + 8, :].reshape(512, head),
-                got_ref[core * 64 : core * 64 + 64, head_rows + 8 :, :].reshape(512, head),
-            ],
+            [got_ref[:, to : to + 8, :].reshape(512, head), got_ref[:, to + 16 : to + 24, :].reshape(512, head)],
             axis=1,
         )
         for h in range(4):
             got = jnp.dot(picks[h], both, preferred_element_type=jnp.float32).astype(jnp.bfloat16)
-            at = (4 * core + h) * head
+            at = (4 * part + h) * head
             out_ref[:, at : at + head] = got[:, :head]
             dq_ref[:, at : at + head] = got[:, head:]
     moves[0].start()
     moves[1].start()
-    wide = spread_lanes(stacked, head_rows)
+    wide = spread_lanes(stacked, kv_rows)
     first, first_count, second, second_count, chip = [wide[i : i + 1] for i in range(5)]
-    r = lax.broadcasted_iota(jnp.int32, (1, 64 * head_rows), 1) - head_rows * chip.astype(jnp.int32)
-    sums = [jnp.zeros((block, head), jnp.float32), jnp.zeros((block, head), jnp.float32)]
-    rows_wide = jnp.concatenate([rows_down] * (64 * head_rows // block), axis=1)
-    for core in range(2):
-        entry = ((r & -2) + core).astype(jnp.float32)
-        code = jnp.where(
-            entry < first_count,
-            entry + (first - first_count + 1),
-            jnp.where(entry >= entries - second_count, entry + (second - (entries - 1)), float(nothing)),
-        )
-        code = jnp.where(r < kv_rows, code, float(nothing))
-        terms = got_ref[core * 64 : core * 64 + 64, :head_rows, :].reshape(64 * head_rows, head)
-        for half in range(2):
-            pick = one_hot(jnp.where((r & 1) == half, code, float(nothing)) == rows_wide)
-            sums[half] = sums[half] + jnp.dot(pick, terms, preferred_element_type=jnp.float32)
+    r = lax.broadcasted_iota(jnp.int32, (1, 64 * kv_rows), 1) - kv_rows * chip.astype(jnp.int32)
+    rows_wide = jnp.concatenate([rows_down] * (64 * kv_rows // block), axis=1)
+    entry = (((r >> 2) << 1) + (r & 1)).astype(jnp.float32)
+    code = jnp.where(
+        entry < first_count,
+        entry + (first - first_count + 1),
+        jnp.where(
+            (entry >= entries - second_count) & (entry < entries), entry + (second - (entries - 1)), float(nothing)
+        ),
+    )
+    terms = got_ref[:, :kv_rows, :].reshape(64 * kv_rows, head)
+    sums = []
+    for half in range(2):
+        pick = one_hot(jnp.where(((r >> 1) & 1) == half, code, float(nothing)) == rows_wide)
+        sums.append(jnp.dot(pick, terms, preferred_element_type=jnp.float32))
     dkv_ref[...] = jnp.concatenate(sums, axis=1).astype(jnp.bfloat16)
     moves[2].start()
     for move in moves:
@@ -194,17 +194,16 @@
     return jnp.dot(a, b, preferred_element_type=jnp.float32)
 
 
-def split_kernel(got_ref, kv_ref, info_ref, qg_ref):
-    for r in range(0, send_rows, 8):
-        rows = jnp.transpose(got_ref[:, r : r + 8, :], (1, 0, 2))
-        if r < kv_rows:
-            n = min(8, kv_rows - r)
-            kv_ref[r : r + n] = rows[:n]
-            if n < 8:
-                info_ref[...] = rows[n]
+def split_kernel(got_ref, kv_ref, qg_ref):
+    for i in range(send_rows // 8):
+        rows = jnp.transpose(got_ref[:, 8 * i : 8 * i + 8, :], (1, 0, 2))
+        if i < tiles // 4:
+            kv_ref[4 * i : 4 * i + 4] = rows.reshape(4, block, head)
         else:
-            at = (r - head_rows) * block
-            qg_ref[at : at + 8 * block, :] = rows.reshape(8 * block, head)
+            kind, part = divmod(i - tiles // 4, 2)
+            for x in range(2):
+                at = 1024 * kind + 512 * x + 256 * part
+                qg_ref[at : at + 256, :] = rows[4 * x : 4 * x + 4].reshape(256, head)
 
 
 to_exp2 = head ** (-0.5) * 1.4426950408889634
@@ -213,11 +212,11 @@
 def spans_of(plan_ref, chip):
     first, second = plan_ref[1, chip], plan_ref[1, chip + 64]
     begin = entries - second
-    few = second <= 2
+    few = second <= 3
     whole = jnp.int32(entries)
     return [
         (0, 6, 0, jnp.int32(0), first, jnp.int32(0), (first + 11) // 12),
-        (1, 1, 6, begin, whole, jnp.where(few, begin // 2, pairs), jnp.int32(pairs)),
+        (1, 2, 6, begin, whole, jnp.where(few, begin // 4, pairs // 2), jnp.int32(pairs // 2)),
         (1, 3, 6, begin, whole, jnp.where(few, pairs // 3, begin // 6), jnp.int32(pairs // 3)),
     ]
 
@@ -238,31 +237,38 @@
     return x.reshape(x.shape[0] * block, 512)
 
 
-def find_positions(core, chip, mine_len, other_len, plan_ref, info_ref, key_pos, bound):
-    stream = chip // 32
-    stream_base = (64 * stream).astype(jnp.float32)
+def find_positions(chip, kv_ref, key_pos):
+    stream_base = (64 * (chip // 32)).astype(jnp.float32)
     block_row = lax.broadcasted_iota(jnp.int32, (block, block), 0)
-    key_pos[...] = info_ref[...].astype(jnp.float32).T + 128.0 * (block_row.astype(jnp.float32) - stream_base)
+    slots = kv_ref[tiles - 1][block // 2 :, :].astype(jnp.float32)
+    key_pos[...] = jnp.concatenate([slots, slots], axis=0).T + 128.0 * (block_row.astype(jnp.float32) - stream_base)
+
+
+def find_bounds(core, chip, mine_len, other_len, plan_ref, key_pos, bound):
     for x in range(2):
         pos = key_pos[pl.ds(plan_ref[0, chip + 64 * x], 1), :]
         start = jnp.zeros((1, block), jnp.float32)
         doc_end = jnp.int32(0)
         for i in range(16):
-            doc_end = doc_end + stream_length(core, mine_len, other_len, stream, i)
+            doc_end = doc_end + stream_length(core, mine_len, other_len, chip // 32, i)
             f = doc_end.astype(jnp.float32)
             start = jnp.where(f <= pos, f, start)
         bound[2 * x : 2 * x + 1] = pos
         bound[2 * x + 1 : 2 * x + 2] = start
 
 
-def score(x, m, n, low, high, parity, plan_ref, chip, kv_ref, qg, key_pos, bound):
+def score(x, m, n, low, high, plan_ref, chip, kv_ref, qg, key_pos, bound):
     base = plan_ref[0, chip + 64 * x] - plan_ref[1, chip + 64 * x] + 1 - low
+    lane = lax.broadcasted_iota(jnp.int32, (1, block), 1)
     bias = []
     for u in range(n):
-        entry = 2 * (m * n + u) + parity
-        valid = (entry >= low) & (entry < high)
-        kp = key_pos[pl.ds(jnp.where(valid, base + entry, 0), 1), :]
-        kp = jnp.broadcast_to(jnp.where(valid, kp, far), (block, block)).T
+        found = []
+        for i in range(2):
+            entry = 2 * (m * n + u) + i
+            valid = (entry >= low) & (entry < high)
+            kp = key_pos[pl.ds(jnp.where(valid, base + entry, 0), 1), :]
+            found.append(jnp.where(valid, kp, far))
+        kp = jnp.broadcast_to(jnp.where(lane < block // 2, found[0], found[1]), (block, block)).T
         seen = (kp <= bound[2 * x : 2 * x + 1]) & (kp >= bound[2 * x + 1 : 2 * x + 2])
         bias.append(jnp.where(seen, 0.0, masked_score))
     bias = jnp.concatenate(bias, axis=0)
@@ -279,19 +285,20 @@
 
 
 def scores_kernel(
-    mine_len, other_len, plan_ref, mine_ref, info_ref, qg,
+    mine_len, other_len, plan_ref, mine_ref, qg,
     s_ref, gw_ref, top_ref, key_pos, bound,
 ):
     core = lax.axis_index("dp")
     chip = lax.axis_index("ctx")
-    find_positions(core, chip, mine_len, other_len, plan_ref, info_ref, key_pos, bound)
+    find_positions(chip, mine_ref, key_pos)
+    find_bounds(core, chip, mine_len, other_len, plan_ref, key_pos, bound)
     top_ref[...] = jnp.full(top_ref.shape, masked_score, jnp.float32)
     for x, n, shift, low, high, begin, end in spans_of(plan_ref, chip):
         cols = slice(x * 512, (x + 1) * 512)
 
         @pl.loop(begin, end)
         def _(m):
-            s = score(x, m, n, low, high, core, plan_ref, chip, mine_ref, qg, key_pos, bound)
+            s = score(x, m, n, low, high, plan_ref, chip, mine_ref, qg, key_pos, bound)
             gw = nt(blocks(mine_ref, 1, m, n), qg[rows_of(x)[1], :])
             s_ref[slot(m, n, shift)] = s.reshape(n, block, 512)
             top_ref[:, cols] = jnp.maximum(top_ref[:, cols], peak_of(s))
@@ -320,7 +327,7 @@
 
 
 def clear_rest(out_ref, end):
-    @pl.loop(12 * end, kv_rows)
+    @pl.loop(12 * end, tiles)
     def _(i):
         out_ref[i] = jnp.zeros((block, head), jnp.bfloat16)
 
@@ -332,12 +339,12 @@
 
 
 def weights_kernel(
-    plan_ref, mine_ref, other_ref, qg, s_ref, found_ref, key_pos, bound,
+    plan_ref, mine_ref, other_ref, qg, s_ref, found_ref, bound,
     dother_ref, out_ref, p_ref, dot_ref, qs_ref, gs_ref, acc_ref, inv_ref,
-    scores, gws, ps, top, total, acc,
+    scores, gws, ps, top, total, acc, key_pos,
 ):
-    core = lax.axis_index("dp")
     chip = lax.axis_index("ctx")
+    find_positions(chip, other_ref, key_pos)
     scale = head ** (-0.5)
     ones = jnp.full((16, block), 1.0, jnp.bfloat16)
     row16 = lax.broadcasted_iota(jnp.int32, (16, 1024), 0)
@@ -351,7 +358,7 @@
 
         @pl.loop(begin, end)
         def _(m):
-            s = score(x, m, n, low, high, 1 - core, plan_ref, chip, other_ref, qg, key_pos, bound)
+            s = score(x, m, n, low, high, plan_ref, chip, other_ref, qg, key_pos, bound)
             scores[slot(m, n, shift)] = s.reshape(n, block, 512)
             top[:, cols] = jnp.maximum(top[:, cols], peak_of(s))
 
@@ -408,18 +415,18 @@
 
 
 def join_kernel(mine_ref, other_ref, out_ref, dq_ref, back_ref):
-    def put(r, rows):
-        back_ref[:, r : r + 8, :] = jnp.transpose(rows, (1, 0, 2))
-
-    for r in range(0, head_rows, 8):
-        n = min(8, kv_rows - r)
-        rows = mine_ref[r : r + n].astype(jnp.float32) + other_ref[r : r + n].astype(jnp.float32)
-        rows = rows.astype(jnp.bfloat16)
-        if n < 8:
-            rows = jnp.concatenate([rows, jnp.zeros((8 - n, block, head), jnp.bfloat16)], axis=0)
-        put(r, rows)
-    put(head_rows, out_ref[...].reshape(8, block, head))
-    put(head_rows + 8, dq_ref[...].reshape(8, block, head))
+    def put(i, rows):
+        back_ref[:, 8 * i : 8 * i + 8, :] = jnp.transpose(rows, (1, 0, 2))
+
+    for i in range(tiles // 4):
+        at = slice(4 * i, 4 * i + 4)
+        rows = mine_ref[at].astype(jnp.float32) + other_ref[at].astype(jnp.float32)
+        put(i, rows.astype(jnp.bfloat16).reshape(8, block // 2, head))
+    for kind, ref in enumerate((out_ref, dq_ref)):
+        for part in range(2):
+            at = [512 * x + 256 * part for x in range(2)]
+            rows = jnp.concatenate([ref[i : i + 256, :].reshape(4, block // 2, head) for i in at], axis=0)
+            put(tiles // 4 + 2 * kind + part, rows)
 
 
 def vmem(n):
@@ -439,7 +446,7 @@
 
 
 def exchange(x):
-    return lax.all_to_all(x, ("dp", "ctx"), split_axis=0, concat_axis=0, tiled=True)
+    return lax.all_to_all(x, "ctx", split_axis=0, concat_axis=0, tiled=True)
 
 
 def kernel(name, body, ins, scalars, outs, scratch, size):
@@ -454,26 +461,26 @@
     )(*ins)
 
 
-def attention(lengths, other_lengths, plan, mine, other, info, qg):
+def attention(lengths, other_lengths, plan, mine, other, qg):
     bf16, f32 = jnp.bfloat16, jnp.float32
     slots = (pairs + 6, block, 512)
     rows = ((8, 1024), f32)
     acc = ((head, 1024), f32)
     heads = ((1024, head), bf16)
     places = [((block, block), f32), ((8, block), f32)]
-    s, gw, top, key_pos, bound = kernel(
-        "scores", scores_kernel, (lengths, other_lengths, plan, mine, info, qg), 3,
+    s, gw, top, _, bound = kernel(
+        "scores", scores_kernel, (lengths, other_lengths, plan, mine, qg), 3,
         [(slots, f32), (slots, f32), ((8, 1024), f32)] + places, [], 12,
     )
     dother, out, p, dot, qs, gs, partial, inv = kernel(
-        "weights", weights_kernel, (plan, mine, other, qg, s, top, key_pos, bound), 1,
-        [((kv_rows, block, head), bf16), heads, (slots, bf16), rows, heads, heads, acc, rows],
-        [(slots, f32), (slots, f32), (slots, bf16), rows, rows, acc], 24,
+        "weights", weights_kernel, (plan, mine, other, qg, s, top, bound), 1,
+        [((tiles, block, head), bf16), heads, (slots, bf16), rows, heads, heads, acc, rows],
+        [(slots, f32), (slots, f32), (slots, bf16), rows, rows, acc, places[0]], 24,
     )
     other_terms = swap(dother)
     dmine, dq = kernel(
         "grads", grads_kernel, (plan, mine, gw, p, dot, qs, gs, partial, inv), 1,
-        [((kv_rows, block, head), bf16), heads], [acc], 12,
+        [((tiles, block, head), bf16), heads], [acc], 12,
     )
     return dmine, other_terms, out, dq
 
@@ -494,7 +501,7 @@
     sent, plan = pl.pallas_call(
         pack_kernel,
         out_shape=(
-            jax.ShapeDtypeStruct((128, send_rows, head), bf16),
+            jax.ShapeDtypeStruct((64, send_rows, head), bf16),
             jax.ShapeDtypeStruct((8, block), jnp.int32),
         ),
         in_specs=[smem()] * 2 + vmem(5),
@@ -502,22 +509,21 @@
         compiler_params=params(24),
         name="pack",
     )(doc_lengths, other_lengths, place, line, queries, keys_values, grad_out)
-    mine, info, qg = pl.pallas_call(
+    mine, qg = pl.pallas_call(
         split_kernel,
         out_shape=(
-            jax.ShapeDtypeStruct((kv_rows, block, head), bf16),
-            jax.ShapeDtypeStruct((block, head), bf16),
+            jax.ShapeDtypeStruct((tiles, block, head), bf16),
             jax.ShapeDtypeStruct((2048, head), bf16),
         ),
         in_specs=vmem(1),
-        out_specs=tuple(vmem(3)),
+        out_specs=tuple(vmem(2)),
         compiler_params=params(24),
         name="split",
     )(exchange(sent))
-    dmine, dother, out, dq = attention(doc_lengths, other_lengths, plan, mine, swap(mine), info, qg)
+    dmine, dother, out, dq = attention(doc_lengths, other_lengths, plan, mine, swap(mine), qg)
     back = pl.pallas_call(
         join_kernel,
-        out_shape=jax.ShapeDtypeStruct((128, send_rows, head), bf16),
+        out_shape=jax.ShapeDtypeStruct((64, send_rows, head), bf16),
         in_specs=vmem(4),
         out_specs=vmem(1)[0],
         compiler_params=params(24),

time: 92.9 us -> 92.9 us (level)
  blocking collectives: 67.5 us -> 65.9 us
    all_to_all x2, blocking collectives: 67.5 us -> 65.9 us  [exchange(): return lax.all_to_all(x, 'ctx', split_axis=0, concat_axis=0, tiled=True)]
    pallas_call x3, Pallas kernels: 14.1 us -> 15.1 us  [kernel(): pl.pallas_call(body, out_shape=tuple((jax.ShapeDtypeStruct(shape, dtype)...]
  transfers between devices with their start and end apart: 3 -> 3, of which waited for: 1 -> 1; matrix products, arithmetic and copies ran while one was open for 0% -> 0% of each run, Pallas kernels for 7% -> 8%
where the time goes in v8:
time: 92.9 us; the launch traced here: 92.3 us
  blocking collectives  65.9 us (71%)
  Pallas kernels  20.9 us (22%)
  starting transfers between devices  3.17 us (3%)
  local copies, waits for them, and re-layouts  1.4 us (2%)
    all_to_all x2, blocking collectives, exchange(): return lax.all_to_all(x, 'ctx', split_axis=0, concat_axis=0, tiled=True)  65.9 us
    pallas_call x3, Pallas kernels, kernel(): pl.pallas_call(body, out_shape=tuple((jax.ShapeDtypeStruct(shape, dtype)...  15.1 us
    ppermute x3, starting transfers between devices, swap(): return lax.ppermute(x, 'dp', [(0, 1), (1, 0)])  3.17 us
    pallas_call x1, Pallas kernels, on_device(): pl.pallas_call(unpack_kernel, out_shape=(jax.ShapeDtypeStruct((block, 8 *...  2.33 us
    pallas_call x1, Pallas kernels, on_device(): pl.pallas_call(pack_kernel, out_shape=(jax.ShapeDtypeStruct((64, send_row...  2.25 us
  transfers between devices with their start and end apart: 3, of which 1 were waited for; matrix products, arithmetic and copies ran while one was open for 0% of the time, Pallas kernels for 8%

profile of v8, /device:TPU:1, one launch (start us, length us, event | category | flops | bytes accessed | tf_op | source)
XLA Modules:
  0.0 92.3 jit_solution(5975086026871048421)
XLA Ops:
  0.6 1.5 %collective-permute-start = (s32[1,16]{1,0:T(1,128)}, s32[1,16]{1,0:T(1,128)S(1)}, u32[]{:S(2)}, u32[]{:S(2)}) collective-permute-start(s32[1,16]{1,0:T(1,128)} %mine_len.1), channel_id=1, source_target_pairs={{0,64},{64,0},{1,65},{65,1},{2,66},{66,2},{3,67},{67,3},{4,68},{68... | collective-permute-start | bytes 200 | tf_op jit(solution)/shard_map/ppermute | solution.py:445
  2.1 0.0 copy-start.3
  2.1 0.7 copy-done.3
  2.8 0.0 copy-start.5
  2.8 0.1 slots.1.line_ref
  2.9 0.2 collective-permute-done.other_ref.other_len
  3.1 0.7 copy-done
  3.7 0.1 copy-done.1
  3.8 0.0 copy-done.2
  3.8 0.0 copy-done.4
  3.8 0.0 copy-done.5
  3.8 2.2 %pack.1 = (bf16[64,104,128]{2,1,0:T(8,128)(2,1)S(1)}, s32[8,128]{1,0:T(8,128)S(1)}) custom-call(s32[1,16]{1,0:T(1,128)S(1)} %copy-done.5, s32[1,16]{1,0:T(1,128)S(1)} %collective-permute-done.other_ref.other_len, s32[1,128]{1,0:T(1,128)S(1)} %bitcast.2, f32[8,128]{1,0:T(8,128)S(1)} %slots.1.line_ref, bf16[128,1024]{1,0:T(8,128)(2,1)S(1)} %copy-done, ...), custom_call_target="tpu_custom_call" | custom-call | tf_op jit(solution)/shard_map/pack/pallas_call | solution.py:501
  6.1 36.8 %all_to_all.10.got_ref = bf16[64,104,128]{2,1,0:T(8,128)(2,1)S(1)} all-to-all(bf16[64,104,128]{2,1,0:T(8,128)(2,1)S(1)} %get-tuple-element.22), channel_id=1, replica_groups=mesh['dp'=2,'ctx'=64] {'ctx'}, dimensions={0} | all-to-all | bytes 3407872 | tf_op jit(solution)/shard_map/all_to_all | solution.py:449
  42.9 0.5 split.1
  43.4 1.6 %collective-permute-start.1 = (bf16[36,128,128]{2,1,0:T(8,128)(2,1)S(1)}, bf16[36,128,128]{2,1,0:T(8,128)(2,1)S(1)}, u32[]{:S(2)}, u32[]{:S(2)}) collective-permute-start(bf16[36,128,128]{2,1,0:T(8,128)(2,1)S(1)} %get-tuple-element.23.mine_ref), channel_id=1, source_target_pairs={{0,64},{64,0},{1,65},{65,1},{2,66},{66,2},{3,67},{67,3},{4,68},{68... | collective-permute-start | bytes 3538952 | tf_op jit(solution)/shard_map/ppermute | solution.py:445
  44.9 3.4 %scores.1 = (f32[24,128,512]{2,1,0:T(8,128)S(1)}, f32[24,128,512]{2,1,0:T(8,128)S(1)}, f32[8,1024]{1,0:T(8,128)S(1)}, f32[128,128]{1,0:T(8,128)}, f32[8,128]{1,0:T(8,128)S(1)}) custom-call(s32[1,16]{1,0:T(1,128)S(1)} %copy-done.5, s32[1,16]{1,0:T(1,128)S(1)} %collective-permute-done.other_ref.other_len, s32[8,128]{1,0:T(8,128)S(1)} %get-tuple-element.21.plan_ref, ...), custom_call_target="tpu_custom_call" | custom-call | tf_op jit(solution)/shard_map/scores/pallas_call | solution.py:453
  48.3 0.0 collective-permute-done.1.other_ref
  48.3 8.3 %weights.1 = (bf16[36,128,128]{2,1,0:T(8,128)(2,1)S(1)}, bf16[1024,128]{1,0:T(8,128)(2,1)S(1)}, bf16[24,128,512]{2,1,0:T(8,128)(2,1)S(1)}, f32[8,1024]{1,0:T(8,1...) custom-call(s32[8,128]{1,0:T(8,128)S(1)} %get-tuple-element.21.plan_, ...), custom_call_target="tpu_custom_call" | custom-call | tf_op jit(solution)/shard_map/weights/pallas_call | solution.py:453
  56.6 0.1 collective-permute-start.2
  56.7 3.4 %grads.1 = (bf16[36,128,128]{2,1,0:T(8,128)(2,1)S(1)}, bf16[1024,128]{1,0:T(8,128)(2,1)S(1)}) custom-call(s32[8,128]{1,0:T(8,128)S(1)} %get-tuple-element.21.plan_ref, bf16[36,128,128]{2,1,0:T(8,128)(2,1)S(1)} %get-tuple-element.23.mine_ref, f32[24,128,512]{2,1,0:T(8,128)S(1)} %get-tuple-element.25.gw_ref, ...), custom_call_target="tpu_custom_call" | custom-call | tf_op jit(solution)/shard_map/grads/pallas_call | solution.py:453
  60.1 0.0 collective-permute-done.2.other_ref
  60.2 0.7 join.1
  60.9 29.1 %all_to_all.11.got_ref = bf16[64,104,128]{2,1,0:T(8,128)(2,1)S(1)} all-to-all(bf16[64,104,128]{2,1,0:T(8,128)(2,1)S(1)} %join.1), channel_id=1, replica_groups=mesh['dp'=2,'ctx'=64] {'ctx'}, dimensions={0} | all-to-all | bytes 3407872 | tf_op jit(solution)/shard_map/all_to_all | solution.py:449
  90.0 2.3 %unpack.1 = (bf16[128,1024]{1,0:T(8,128)(2,1)}, bf16[128,1024]{1,0:T(8,128)(2,1)}, bf16[128,256]{1,0:T(8,128)(2,1)}) custom-call(s32[1,128]{1,0:T(1,128)S(1)} %bitcast.3, s32[8,128]{1,0:T(8,128)S(1)} %get-tuple-element.21.plan_ref, bf16[64,104,128]{2,1,0:T(8,128)(2,1)S(1)} %all_to_all.11.got_ref), custom_call_target="tpu_custom_call" | custom-call | tf_op jit(solution)/shard_map/unpack/pallas_call | solution.py:533
  (4 shorter events, 0.0 us)
Async XLA Ops:
  0.6 2.5 %collective-permute-start = (s32[1,16]{1,0:T(1,128)}, s32[1,16]{1,0:T(1,128)S(1)}, u32[]{:S(2)}, u32[]{:S(2)}) collective-permute-start(s32[1,16]{1,0:T(1,128)} %mine_len.1), channel_id=1, source_target_pairs={{0,64},{64,0},{1,65},{65,1},{2,66},{66,2},{3,67},{67,3},{4,68},{68... | collective-permute-start | bytes 200 | tf_op jit(solution)/shard_map/ppermute | solution.py:445
  2.1 0.7 copy-start.3
  2.8 0.9 %copy-start = (bf16[128,1024]{1,0:T(8,128)(2,1)S(1)}, bf16[128,1024]{1,0:T(8,128)(2,1)}, u32[]{:S(2)}) copy-start(bf16[128,1024]{1,0:T(8,128)(2,1)} %q_ref.1) | copy-start | bytes 786436
  2.8 1.0 %copy-start.1 = (bf16[128,1024]{1,0:T(8,128)(2,1)S(1)}, bf16[128,1024]{1,0:T(8,128)(2,1)}, u32[]{:S(2)}) copy-start(bf16[128,1024]{1,0:T(8,128)(2,1)} %g_ref.1) | copy-start | bytes 786436
  2.8 1.0 %copy-start.2 = (bf16[128,256]{1,0:T(8,128)(2,1)S(1)}, bf16[128,256]{1,0:T(8,128)(2,1)}, u32[]{:S(2)}) copy-start(bf16[128,256]{1,0:T(8,128)(2,1)} %kv_ref.1) | copy-start | bytes 196612
  2.8 1.0 %copy-start.4 = (s32[128]{0:T(128)S(1)}, s32[128]{0:T(128)}, u32[]{:S(2)}) copy-start(s32[128]{0:T(128)} %param.8) | copy-start | bytes 1540
  2.8 1.0 %copy-start.5 = (s32[1,16]{1,0:T(1,128)S(1)}, s32[1,16]{1,0:T(1,128)}, u32[]{:S(2)}) copy-start(s32[1,16]{1,0:T(1,128)} %mine_len.1) | copy-start | bytes 196
  43.4 5.0 %collective-permute-start.1 = (bf16[36,128,128]{2,1,0:T(8,128)(2,1)S(1)}, bf16[36,128,128]{2,1,0:T(8,128)(2,1)S(1)}, u32[]{:S(2)}, u32[]{:S(2)}) collective-permute-start(bf16[36,128,128]{2,1,0:T(8,128)(2,1)S(1)} %get-tuple-element.23.mine_ref), channel_id=1, source_target_pairs={{0,64},{64,0},{1,65},{65,1},{2,66},{66,2},{3,67},{67,3},{4,68},{68... | collective-permute-start | bytes 3538952 | tf_op jit(solution)/shard_map/ppermute | solution.py:445
  56.6 3.5 %collective-permute-start.2 = (bf16[36,128,128]{2,1,0:T(8,128)(2,1)S(1)}, bf16[36,128,128]{2,1,0:T(8,128)(2,1)S(1)}, u32[]{:S(2)}, u32[]{:S(2)}) collective-permute-start(bf16[36,128,128]{2,1,0:T(8,128)(2,1)S(1)} %get-tuple-element.36), channel_id=1, source_target_pairs={{0,64},{64,0},{1,65},{65,1},{2,66},{66,2},{3,67},{67,3},{4,68},{68... | collective-permute-start | bytes 3538952 | tf_op jit(solution)/shard_map/ppermute | solution.py:445

commit v9 on v8

--- a/solution.py
+++ b/solution.py
@@ -7,7 +7,6 @@
 
 block = 128
 head = 128
-entries = 35
 pairs = 18
 tiles = 2 * pairs
 kv_rows = 4 * pairs
@@ -19,6 +18,14 @@
 masked_score = -1e30
 far = 1e9
 mib = 1024 * 1024
+
+
+def second_place(count):
+    return 2 * pairs - count - count % 2
+
+
+def slots_place(count):
+    return 2 * pairs - 1 - jnp.where(count % 2 == 0, count, 0)
 
 
 def one_hot(mask):
@@ -71,11 +78,11 @@
     count_down = down(count_line).astype(jnp.int32)
     rows = place_ref[...] >> 7
     slot_line = line_ref[0:1]
-    extra = jnp.where(row8 == 7, slot_line, 0.0)
     kv = jnp.concatenate([kv_ref[:, :head], kv_ref[:, head:]], axis=0)
     r = lax.broadcasted_iota(jnp.int32, (group, kv_rows, block), 1)
     entry = ((r >> 2) << 1) + (r & 1)
     half = ((r >> 1) & 1) * other_half
+    odd_values = jnp.where((r & 3) == 3, entry, nothing)
     j = lax.broadcasted_iota(jnp.int32, (group, 8, block), 1)
     both = []
     for part in range(2):
@@ -91,20 +98,20 @@
         first_count = count_down[at]
         second = block_down[64 + chip : 64 + chip + group]
         second_count = count_down[64 + chip : 64 + chip + group]
+        place = second_place(second_count)
         code = jnp.where(
             entry < spread(first_count, kv_rows),
             entry + spread(first - first_count + 1, kv_rows),
             jnp.where(
-                (entry >= spread(entries - second_count, kv_rows)) & (entry < entries),
-                entry + spread(second - (entries - 1), kv_rows),
+                (entry >= spread(place, kv_rows)) & (entry < spread(place + second_count, kv_rows)),
+                entry + spread(second - second_count + 1 - place, kv_rows),
                 nothing,
             ),
         )
         code = (code + half).reshape(group * kv_rows, block)
         pick = jnp.concatenate([one_hot(code == rows), one_hot(code == rows + other_half)], axis=1)
         got = jnp.dot(pick, kv, preferred_element_type=jnp.float32).reshape(group, kv_rows, head)
-        tail = got[:, kv_rows - 8 :, :] + extra[None]
-        got = jnp.concatenate([got[:, : kv_rows - 8, :], tail], axis=1)
+        got = jnp.where(odd_values == spread(slots_place(second_count), kv_rows), slot_line[None], got)
         out_ref[at, :kv_rows, :] = got.astype(jnp.bfloat16)
         wanted = jnp.where(j < 4, spread(first, 8), spread(second, 8)) == rows[None]
         heads = jnp.concatenate(
@@ -164,11 +171,14 @@
     r = lax.broadcasted_iota(jnp.int32, (1, 64 * kv_rows), 1) - kv_rows * chip.astype(jnp.int32)
     rows_wide = jnp.concatenate([rows_down] * (64 * kv_rows // block), axis=1)
     entry = (((r >> 2) << 1) + (r & 1)).astype(jnp.float32)
+    place = second_place(second_count.astype(jnp.int32)).astype(jnp.float32)
     code = jnp.where(
         entry < first_count,
         entry + (first - first_count + 1),
         jnp.where(
-            (entry >= entries - second_count) & (entry < entries), entry + (second - (entries - 1)), float(nothing)
+            (entry >= place) & (entry < place + second_count),
+            entry + (second - second_count + 1 - place),
+            float(nothing),
         ),
     )
     terms = got_ref[:, :kv_rows, :].reshape(64 * kv_rows, head)
@@ -211,13 +221,12 @@
 
 def spans_of(plan_ref, chip):
     first, second = plan_ref[1, chip], plan_ref[1, chip + 64]
-    begin = entries - second
-    few = second <= 3
-    whole = jnp.int32(entries)
+    begin = second_place(second)
+    few = second <= 2
     return [
         (0, 6, 0, jnp.int32(0), first, jnp.int32(0), (first + 11) // 12),
-        (1, 2, 6, begin, whole, jnp.where(few, begin // 4, pairs // 2), jnp.int32(pairs // 2)),
-        (1, 3, 6, begin, whole, jnp.where(few, pairs // 3, begin // 6), jnp.int32(pairs // 3)),
+        (1, 1, 6, begin, begin + second, jnp.where(few, begin // 2, pairs), jnp.int32(pairs)),
+        (1, 3, 6, begin, begin + second, jnp.where(few, pairs // 3, begin // 6), jnp.int32(pairs // 3)),
     ]
 
 
@@ -237,10 +246,10 @@
     return x.reshape(x.shape[0] * block, 512)
 
 
-def find_positions(chip, kv_ref, key_pos):
+def find_positions(chip, plan_ref, kv_ref, key_pos):
     stream_base = (64 * (chip // 32)).astype(jnp.float32)
     block_row = lax.broadcasted_iota(jnp.int32, (block, block), 0)
-    slots = kv_ref[tiles - 1][block // 2 :, :].astype(jnp.float32)
+    slots = kv_ref[slots_place(plan_ref[1, chip + 64])][block // 2 :, :].astype(jnp.float32)
     key_pos[...] = jnp.concatenate([slots, slots], axis=0).T + 128.0 * (block_row.astype(jnp.float32) - stream_base)
 
 
@@ -286,11 +295,12 @@
 
 def scores_kernel(
     mine_len, other_len, plan_ref, mine_ref, qg,
-    s_ref, gw_ref, top_ref, key_pos, bound,
+    s_ref, gw_ref, top_ref, bound,
+    key_pos,
 ):
     core = lax.axis_index("dp")
     chip = lax.axis_index("ctx")
-    find_positions(chip, mine_ref, key_pos)
+    find_positions(chip, plan_ref, mine_ref, key_pos)
     find_bounds(core, chip, mine_len, other_len, plan_ref, key_pos, bound)
     top_ref[...] = jnp.full(top_ref.shape, masked_score, jnp.float32)
     for x, n, shift, low, high, begin, end in spans_of(plan_ref, chip):
@@ -344,7 +354,7 @@
     scores, gws, ps, top, total, acc, key_pos,
 ):
     chip = lax.axis_index("ctx")
-    find_positions(chip, other_ref, key_pos)
+    find_positions(chip, plan_ref, other_ref, key_pos)
     scale = head ** (-0.5)
     ones = jnp.full((16, block), 1.0, jnp.bfloat16)
     row16 = lax.broadcasted_iota(jnp.int32, (16, 1024), 0)
@@ -467,15 +477,15 @@
     rows = ((8, 1024), f32)
     acc = ((head, 1024), f32)
     heads = ((1024, head), bf16)
-    places = [((block, block), f32), ((8, block), f32)]
-    s, gw, top, _, bound = kernel(
+    table = ((block, block), f32)
+    s, gw, top, bound = kernel(
         "scores", scores_kernel, (lengths, other_lengths, plan, mine, qg), 3,
-        [(slots, f32), (slots, f32), ((8, 1024), f32)] + places, [], 12,
+        [(slots, f32), (slots, f32), rows, ((8, block), f32)], [table], 12,
     )
     dother, out, p, dot, qs, gs, partial, inv = kernel(
         "weights", weights_kernel, (plan, mine, other, qg, s, top, bound), 1,
         [((tiles, block, head), bf16), heads, (slots, bf16), rows, heads, heads, acc, rows],
-        [(slots, f32), (slots, f32), (slots, bf16), rows, rows, acc, places[0]], 24,
+        [(slots, f32), (slots, f32), (slots, bf16), rows, rows, acc, table], 24,
     )
     other_terms = swap(dother)
     dmine, dq = kernel(

time: 92.9 us -> 92.4 us (level)
  transfers between devices with their start and end apart: 3 -> 3, of which waited for: 1 -> 1; matrix products, arithmetic and copies ran while one was open for 0% -> 0% of each run, Pallas kernels for 8% -> 7%
where the time goes in v9:
time: 92.4 us; the launch traced here: 91.8 us
  blocking collectives  66 us (71%)
  Pallas kernels  20.3 us (22%)
  starting transfers between devices  3.22 us (3%)
  local copies, waits for them, and re-layouts  1.4 us (2%)
    all_to_all x2, blocking collectives, exchange(): return lax.all_to_all(x, 'ctx', split_axis=0, concat_axis=0, tiled=True)  66 us
    pallas_call x3, Pallas kernels, kernel(): pl.pallas_call(body, out_shape=tuple((jax.ShapeDtypeStruct(shape, dtype)...  14.2 us
    ppermute x3, starting transfers between devices, swap(): return lax.ppermute(x, 'dp', [(0, 1), (1, 0)])  3.22 us
    pallas_call x1, Pallas kernels, on_device(): pl.pallas_call(unpack_kernel, out_shape=(jax.ShapeDtypeStruct((block, 8 *...  2.46 us
    pallas_call x1, Pallas kernels, on_device(): pl.pallas_call(pack_kernel, out_shape=(jax.ShapeDtypeStruct((64, send_row...  2.37 us
  transfers between devices with their start and end apart: 3, of which 1 were waited for; matrix products, arithmetic and copies ran while one was open for 0% of the time, Pallas kernels for 7%

profile of v9, /device:TPU:1, one launch (start us, length us, event | category | flops | bytes accessed | tf_op | source)
XLA Modules:
  0.0 91.8 jit_solution(13408691143566650521)
XLA Ops:
  0.6 1.5 %collective-permute-start = (s32[1,16]{1,0:T(1,128)}, s32[1,16]{1,0:T(1,128)S(1)}, u32[]{:S(2)}, u32[]{:S(2)}) collective-permute-start(s32[1,16]{1,0:T(1,128)} %mine_len.1), channel_id=1, source_target_pairs={{0,64},{64,0},{1,65},{65,1},{2,66},{66,2},{3,67},{67,3},{4,68},{68... | collective-permute-start | bytes 200 | tf_op jit(solution)/shard_map/ppermute | solution.py:455
  2.1 0.0 copy-start.3
  2.1 0.7 copy-done.3
  2.8 0.0 copy-start.5
  2.8 0.1 slots.1.line_ref
  2.9 0.2 collective-permute-done.other_ref.other_len
  3.1 0.7 copy-done
  3.7 0.1 copy-done.1
  3.8 0.0 copy-done.2
  3.8 0.0 copy-done.4
  3.8 0.0 copy-done.5
  3.8 2.4 %pack.1 = (bf16[64,104,128]{2,1,0:T(8,128)(2,1)S(1)}, s32[8,128]{1,0:T(8,128)S(1)}) custom-call(s32[1,16]{1,0:T(1,128)S(1)} %copy-done.5, s32[1,16]{1,0:T(1,128)S(1)} %collective-permute-done.other_ref.other_len, s32[1,128]{1,0:T(1,128)S(1)} %bitcast.2, f32[8,128]{1,0:T(8,128)S(1)} %slots.1.line_ref, bf16[128,1024]{1,0:T(8,128)(2,1)S(1)} %copy-done, ...), custom_call_target="tpu_custom_call" | custom-call | tf_op jit(solution)/shard_map/pack/pallas_call | solution.py:511
  6.2 36.8 %all_to_all.10.got_ref = bf16[64,104,128]{2,1,0:T(8,128)(2,1)S(1)} all-to-all(bf16[64,104,128]{2,1,0:T(8,128)(2,1)S(1)} %get-tuple-element.22), channel_id=1, replica_groups=mesh['dp'=2,'ctx'=64] {'ctx'}, dimensions={0} | all-to-all | bytes 3407872 | tf_op jit(solution)/shard_map/all_to_all | solution.py:459
  43.0 0.5 split.1
  43.5 1.6 %collective-permute-start.1 = (bf16[36,128,128]{2,1,0:T(8,128)(2,1)S(1)}, bf16[36,128,128]{2,1,0:T(8,128)(2,1)S(1)}, u32[]{:S(2)}, u32[]{:S(2)}) collective-permute-start(bf16[36,128,128]{2,1,0:T(8,128)(2,1)S(1)} %get-tuple-element.23.mine_ref), channel_id=1, source_target_pairs={{0,64},{64,0},{1,65},{65,1},{2,66},{66,2},{3,67},{67,3},{4,68},{68... | collective-permute-start | bytes 3538952 | tf_op jit(solution)/shard_map/ppermute | solution.py:455
  45.0 2.7 %scores.1 = (f32[24,128,512]{2,1,0:T(8,128)S(1)}, f32[24,128,512]{2,1,0:T(8,128)S(1)}, f32[8,1024]{1,0:T(8,128)S(1)}, f32[8,128]{1,0:T(8,128)S(1)}) custom-call(s32[1,16]{1,0:T(1,128)S(1)} %copy-done.5, s32[1,16]{1,0:T(1,128)S(1)} %collective-permute-done.other_ref.other_len, s32[8,128]{1,0:T(8,128)S(1)} %get-tuple-element.21.plan_ref, ...), custom_call_target="tpu_custom_call" | custom-call | tf_op jit(solution)/shard_map/scores/pallas_call | solution.py:463
  47.8 0.0 collective-permute-done.1.other_ref
  47.8 8.1 %weights.1 = (bf16[36,128,128]{2,1,0:T(8,128)(2,1)S(1)}, bf16[1024,128]{1,0:T(8,128)(2,1)S(1)}, bf16[24,128,512]{2,1,0:T(8,128)(2,1)S(1)}, f32[8,1024]{1,0:T(8,1...) custom-call(s32[8,128]{1,0:T(8,128)S(1)} %get-tuple-element.21.plan_, ...), custom_call_target="tpu_custom_call" | custom-call | tf_op jit(solution)/shard_map/weights/pallas_call | solution.py:463
  55.9 0.2 collective-permute-start.2
  56.1 3.4 %grads.1 = (bf16[36,128,128]{2,1,0:T(8,128)(2,1)S(1)}, bf16[1024,128]{1,0:T(8,128)(2,1)S(1)}) custom-call(s32[8,128]{1,0:T(8,128)S(1)} %get-tuple-element.21.plan_ref, bf16[36,128,128]{2,1,0:T(8,128)(2,1)S(1)} %get-tuple-element.23.mine_ref, f32[24,128,512]{2,1,0:T(8,128)S(1)} %get-tuple-element.25.gw_ref, ...), custom_call_target="tpu_custom_call" | custom-call | tf_op jit(solution)/shard_map/grads/pallas_call | solution.py:463
  59.4 0.0 collective-permute-done.2.other_ref
  59.5 0.7 join.1
  60.2 29.2 %all_to_all.11.got_ref = bf16[64,104,128]{2,1,0:T(8,128)(2,1)S(1)} all-to-all(bf16[64,104,128]{2,1,0:T(8,128)(2,1)S(1)} %join.1), channel_id=1, replica_groups=mesh['dp'=2,'ctx'=64] {'ctx'}, dimensions={0} | all-to-all | bytes 3407872 | tf_op jit(solution)/shard_map/all_to_all | solution.py:459
  89.3 2.5 %unpack.1 = (bf16[128,1024]{1,0:T(8,128)(2,1)}, bf16[128,1024]{1,0:T(8,128)(2,1)}, bf16[128,256]{1,0:T(8,128)(2,1)}) custom-call(s32[1,128]{1,0:T(1,128)S(1)} %bitcast.3, s32[8,128]{1,0:T(8,128)S(1)} %get-tuple-element.21.plan_ref, bf16[64,104,128]{2,1,0:T(8,128)(2,1)S(1)} %all_to_all.11.got_ref), custom_call_target="tpu_custom_call" | custom-call | tf_op jit(solution)/shard_map/unpack/pallas_call | solution.py:543
  (4 shorter events, 0.0 us)
Async XLA Ops:
  0.6 2.5 %collective-permute-start = (s32[1,16]{1,0:T(1,128)}, s32[1,16]{1,0:T(1,128)S(1)}, u32[]{:S(2)}, u32[]{:S(2)}) collective-permute-start(s32[1,16]{1,0:T(1,128)} %mine_len.1), channel_id=1, source_target_pairs={{0,64},{64,0},{1,65},{65,1},{2,66},{66,2},{3,67},{67,3},{4,68},{68... | collective-permute-start | bytes 200 | tf_op jit(solution)/shard_map/ppermute | solution.py:455
  2.1 0.7 copy-start.3
  2.8 0.9 %copy-start = (bf16[128,1024]{1,0:T(8,128)(2,1)S(1)}, bf16[128,1024]{1,0:T(8,128)(2,1)}, u32[]{:S(2)}) copy-start(bf16[128,1024]{1,0:T(8,128)(2,1)} %q_ref.1) | copy-start | bytes 786436
  2.8 1.0 %copy-start.1 = (bf16[128,1024]{1,0:T(8,128)(2,1)S(1)}, bf16[128,1024]{1,0:T(8,128)(2,1)}, u32[]{:S(2)}) copy-start(bf16[128,1024]{1,0:T(8,128)(2,1)} %g_ref.1) | copy-start | bytes 786436
  2.8 1.0 %copy-start.2 = (bf16[128,256]{1,0:T(8,128)(2,1)S(1)}, bf16[128,256]{1,0:T(8,128)(2,1)}, u32[]{:S(2)}) copy-start(bf16[128,256]{1,0:T(8,128)(2,1)} %kv_ref.1) | copy-start | bytes 196612
  2.8 1.0 %copy-start.4 = (s32[128]{0:T(128)S(1)}, s32[128]{0:T(128)}, u32[]{:S(2)}) copy-start(s32[128]{0:T(128)} %param.8) | copy-start | bytes 1540
  2.8 1.0 %copy-start.5 = (s32[1,16]{1,0:T(1,128)S(1)}, s32[1,16]{1,0:T(1,128)}, u32[]{:S(2)}) copy-start(s32[1,16]{1,0:T(1,128)} %mine_len.1) | copy-start | bytes 196
  43.5 4.3 %collective-permute-start.1 = (bf16[36,128,128]{2,1,0:T(8,128)(2,1)S(1)}, bf16[36,128,128]{2,1,0:T(8,128)(2,1)S(1)}, u32[]{:S(2)}, u32[]{:S(2)}) collective-permute-start(bf16[36,128,128]{2,1,0:T(8,128)(2,1)S(1)} %get-tuple-element.23.mine_ref), channel_id=1, source_target_pairs={{0,64},{64,0},{1,65},{65,1},{2,66},{66,2},{3,67},{67,3},{4,68},{68... | collective-permute-start | bytes 3538952 | tf_op jit(solution)/shard_map/ppermute | solution.py:455
  55.9 3.6 %collective-permute-start.2 = (bf16[36,128,128]{2,1,0:T(8,128)(2,1)S(1)}, bf16[36,128,128]{2,1,0:T(8,128)(2,1)S(1)}, u32[]{:S(2)}, u32[]{:S(2)}) collective-permute-start(bf16[36,128,128]{2,1,0:T(8,128)(2,1)S(1)} %get-tuple-element.36), channel_id=1, source_target_pairs={{0,64},{64,0},{1,65},{65,1},{2,66},{66,2},{3,67},{67,3},{4,68},{68... | collective-permute-start | bytes 3538952 | tf_op jit(solution)/shard_map/ppermute | solution.py:455

commit v10 on v7

--- a/solution.py
+++ b/solution.py
@@ -214,9 +214,11 @@
     first, second = plan_ref[1, chip], plan_ref[1, chip + 64]
     begin = entries - second
     few = second <= 2
+    long = first > 24
     whole = jnp.int32(entries)
     return [
-        (0, 6, 0, jnp.int32(0), first, jnp.int32(0), (first + 11) // 12),
+        (0, 9, 0, jnp.int32(0), first, jnp.int32(0), jnp.where(long, 2, 0)),
+        (0, 6, 0, jnp.int32(0), first, jnp.int32(0), jnp.where(long, 0, (first + 11) // 12)),
         (1, 1, 6, begin, whole, jnp.where(few, begin // 2, pairs), jnp.int32(pairs)),
         (1, 3, 6, begin, whole, jnp.where(few, pairs // 3, begin // 6), jnp.int32(pairs // 3)),
     ]
@@ -319,8 +321,10 @@
                 out_ref[i] = value.astype(jnp.bfloat16)
 
 
-def clear_rest(out_ref, end):
-    @pl.loop(12 * end, kv_rows)
+def clear_rest(out_ref, spans):
+    long, short = spans[0], spans[1]
+
+    @pl.loop(2 * (long[1] * long[-1] + short[1] * short[-1]), kv_rows)
     def _(i):
         out_ref[i] = jnp.zeros((block, head), jnp.bfloat16)
 
@@ -342,7 +346,7 @@
     ones = jnp.full((16, block), 1.0, jnp.bfloat16)
     row16 = lax.broadcasted_iota(jnp.int32, (16, 1024), 0)
     spans = spans_of(plan_ref, chip)
-    clear_rest(dother_ref, spans[0][-1])
+    clear_rest(dother_ref, spans)
     top[...] = found_ref[...]
     total[...] = jnp.zeros(total.shape, jnp.float32)
     acc[...] = jnp.zeros(acc.shape, jnp.float32)
@@ -400,7 +404,7 @@
 ):
     chip = lax.axis_index("ctx")
     spans = spans_of(plan_ref, chip)
-    clear_rest(dmine_ref, spans[0][-1])
+    clear_rest(dmine_ref, spans)
     acc[...] = part_ref[...]
     for span in spans:
         backward(span, p_ref, gw_ref, mine_ref, dot_ref, qs_ref, gs_ref, acc, dmine_ref)

time: 92.9 us -> 92.7 us (level)
  no operation moved by 1% of the time
where the time goes in v10:
time: 92.7 us; the launch traced here: 92.5 us
  blocking collectives  67.4 us (73%)
  Pallas kernels  19.7 us (21%)
  starting transfers between devices  2.94 us (3%)
  local copies, waits for them, and re-layouts  1.4 us (2%)
    all_to_all x2, blocking collectives, exchange(): lax.all_to_all(x, ('dp', 'ctx'), split_axis=0, concat_axis=0, tiled=True)  67.4 us
    pallas_call x3, Pallas kernels, kernel(): pl.pallas_call(body, out_shape=tuple((jax.ShapeDtypeStruct(shape, dtype)...  13.6 us
    ppermute x3, starting transfers between devices, swap(): return lax.ppermute(x, 'dp', [(0, 1), (1, 0)])  2.94 us
    pallas_call x1, Pallas kernels, on_device(): pl.pallas_call(unpack_kernel, out_shape=(jax.ShapeDtypeStruct((block, 8 *...  2.43 us
    pallas_call x1, Pallas kernels, on_device(): pl.pallas_call(pack_kernel, out_shape=(jax.ShapeDtypeStruct((128, send_ro...  2.32 us
  transfers between devices with their start and end apart: 3, of which 1 were waited for; matrix products, arithmetic and copies ran while one was open for 0% of the time, Pallas kernels for 7%

profile of v10, /device:TPU:1, one launch (start us, length us, event | category | flops | bytes accessed | tf_op | source)
XLA Modules:
  0.0 92.5 jit_solution(1788713946925973080)
XLA Ops:
  0.6 1.5 %collective-permute-start = (s32[1,16]{1,0:T(1,128)}, s32[1,16]{1,0:T(1,128)S(1)}, u32[]{:S(2)}, u32[]{:S(2)}) collective-permute-start(s32[1,16]{1,0:T(1,128)} %mine_len.1), channel_id=1, source_target_pairs={{0,64},{64,0},{1,65},{65,1},{2,66},{66,2},{3,67},{67,3},{4,68},{68... | collective-permute-start | bytes 200 | tf_op jit(solution)/shard_map/ppermute | solution.py:442
  2.1 0.0 copy-start.4
  2.1 0.7 copy-done.4
  2.8 0.1 slots.1.line_ref
  2.9 0.2 collective-permute-done.other_ref.other_len
  3.1 0.7 copy-done
  3.7 0.1 copy-done.1
  3.8 0.0 copy-done.2
  3.8 0.0 copy-done.3
  3.8 2.3 %pack.1 = (bf16[128,56,128]{2,1,0:T(8,128)(2,1)S(1)}, s32[8,128]{1,0:T(8,128)S(1)}) custom-call(s32[1,16]{1,0:T(1,128)S(1)} %copy-done.3, s32[1,16]{1,0:T(1,128)S(1)} %collective-permute-done.other_ref.other_len, s32[1,128]{1,0:T(1,128)S(1)} %bitcast.2, f32[8,128]{1,0:T(8,128)S(1)} %slots.1.line_ref, bf16[128,1024]{1,0:T(8,128)(2,1)S(1)} %copy-done, ...), custom_call_target="tpu_custom_call" | custom-call | tf_op jit(solution)/shard_map/pack/pallas_call | solution.py:498
  6.2 36.9 %all_to_all.10.got_ref = bf16[128,56,128]{2,1,0:T(8,128)(2,1)S(1)} all-to-all(bf16[128,56,128]{2,1,0:T(8,128)(2,1)S(1)} %get-tuple-element.24), channel_id=1, replica_groups=mesh['dp'=2,'ctx'=64] {'dp','ctx'}, dimensions={0} | all-to-all | bytes 3670016 | tf_op jit(solution)/shard_map/all_to_all | solution.py:446
  43.0 0.5 split.1
  43.5 1.1 %collective-permute-start.1 = (bf16[36,128,128]{2,1,0:T(8,128)(2,1)S(1)}, bf16[36,128,128]{2,1,0:T(8,128)(2,1)S(1)}, u32[]{:S(2)}, u32[]{:S(2)}) collective-permute-start(bf16[36,128,128]{2,1,0:T(8,128)(2,1)S(1)} %get-tuple-element.25.mine_ref), channel_id=1, source_target_pairs={{0,64},{64,0},{1,65},{65,1},{2,66},{66,2},{3,67},{67,3},{4,68},{68... | collective-permute-start | bytes 3538952 | tf_op jit(solution)/shard_map/ppermute | solution.py:442
  44.6 2.5 %scores.1 = (f32[24,128,512]{2,1,0:T(8,128)S(1)}, f32[24,128,512]{2,1,0:T(8,128)S(1)}, f32[8,1024]{1,0:T(8,128)S(1)}, f32[128,128]{1,0:T(8,128)S(1)}, f32[8,128]{1,0:T(8,128)S(1)}) custom-call(s32[1,16]{1,0:T(1,128)S(1)} %copy-done.3, s32[1,16]{1,0:T(1,128)S(1)} %collective-permute-done.other_ref.other_len, s32[8,128]{1,0:T(8,128)S(1)} %get-tuple-element.23.plan_ref, ...), custom_call_target="tpu_custom_call" | custom-call | tf_op jit(solution)/shard_map/scores/pallas_call | solution.py:450
  47.2 0.0 collective-permute-done.1.other_ref
  47.2 7.7 %weights.1 = (bf16[36,128,128]{2,1,0:T(8,128)(2,1)S(1)}, bf16[1024,128]{1,0:T(8,128)(2,1)S(1)}, bf16[24,128,512]{2,1,0:T(8,128)(2,1)S(1)}, f32[8,1024]{1,0:T(8,1...) custom-call(s32[8,128]{1,0:T(8,128)S(1)} %get-tuple-element.23.plan_, ...), custom_call_target="tpu_custom_call" | custom-call | tf_op jit(solution)/shard_map/weights/pallas_call | solution.py:450
  54.8 0.4 collective-permute-start.2
  55.2 3.4 %grads.1 = (bf16[36,128,128]{2,1,0:T(8,128)(2,1)S(1)}, bf16[1024,128]{1,0:T(8,128)(2,1)S(1)}) custom-call(s32[8,128]{1,0:T(8,128)S(1)} %get-tuple-element.23.plan_ref, bf16[36,128,128]{2,1,0:T(8,128)(2,1)S(1)} %get-tuple-element.25.mine_ref, f32[24,128,512]{2,1,0:T(8,128)S(1)} %get-tuple-element.28.gw_ref, ...), custom_call_target="tpu_custom_call" | custom-call | tf_op jit(solution)/shard_map/grads/pallas_call | solution.py:450
  58.6 0.0 collective-permute-done.2.other_ref
  58.7 0.7 join.1
  59.4 0.0 copy-start.5
  59.4 30.5 %all_to_all.11.got_ref = bf16[128,56,128]{2,1,0:T(8,128)(2,1)S(1)} all-to-all(bf16[128,56,128]{2,1,0:T(8,128)(2,1)S(1)} %join.1), channel_id=1, replica_groups=mesh['dp'=2,'ctx'=64] {'dp','ctx'}, dimensions={0} | all-to-all | bytes 3670016 | tf_op jit(solution)/shard_map/all_to_all | solution.py:446
  89.9 0.0 copy-done.5
  89.9 2.4 %unpack.1 = (bf16[128,1024]{1,0:T(8,128)(2,1)}, bf16[128,1024]{1,0:T(8,128)(2,1)}, bf16[128,256]{1,0:T(8,128)(2,1)}) custom-call(s32[1,128]{1,0:T(1,128)S(1)} %bitcast.3, s32[8,128]{1,0:T(8,128)S(1)} %get-tuple-element.23.plan_ref, bf16[128,56,128]{2,1,0:T(8,128)(2,1)S(1)} %all_to_all.11.got_ref), custom_call_target="tpu_custom_call" | custom-call | tf_op jit(solution)/shard_map/unpack/pallas_call | solution.py:531
  (4 shorter events, 0.0 us)
Async XLA Ops:
  0.6 2.5 %collective-permute-start = (s32[1,16]{1,0:T(1,128)}, s32[1,16]{1,0:T(1,128)S(1)}, u32[]{:S(2)}, u32[]{:S(2)}) collective-permute-start(s32[1,16]{1,0:T(1,128)} %mine_len.1), channel_id=1, source_target_pairs={{0,64},{64,0},{1,65},{65,1},{2,66},{66,2},{3,67},{67,3},{4,68},{68... | collective-permute-start | bytes 200 | tf_op jit(solution)/shard_map/ppermute | solution.py:442
  2.1 0.7 copy-start.4
  2.8 0.9 %copy-start = (bf16[128,1024]{1,0:T(8,128)(2,1)S(1)}, bf16[128,1024]{1,0:T(8,128)(2,1)}, u32[]{:S(2)}) copy-start(bf16[128,1024]{1,0:T(8,128)(2,1)} %q_ref.1) | copy-start | bytes 786436
  2.8 1.0 %copy-start.1 = (bf16[128,1024]{1,0:T(8,128)(2,1)S(1)}, bf16[128,1024]{1,0:T(8,128)(2,1)}, u32[]{:S(2)}) copy-start(bf16[128,1024]{1,0:T(8,128)(2,1)} %g_ref.1) | copy-start | bytes 786436
  2.8 1.0 %copy-start.2 = (bf16[128,256]{1,0:T(8,128)(2,1)S(1)}, bf16[128,256]{1,0:T(8,128)(2,1)}, u32[]{:S(2)}) copy-start(bf16[128,256]{1,0:T(8,128)(2,1)} %kv_ref.1) | copy-start | bytes 196612
  2.8 1.0 %copy-start.3 = (s32[1,16]{1,0:T(1,128)S(1)}, s32[1,16]{1,0:T(1,128)}, u32[]{:S(2)}) copy-start(s32[1,16]{1,0:T(1,128)} %mine_len.1) | copy-start | bytes 196
  43.5 3.6 %collective-permute-start.1 = (bf16[36,128,128]{2,1,0:T(8,128)(2,1)S(1)}, bf16[36,128,128]{2,1,0:T(8,128)(2,1)S(1)}, u32[]{:S(2)}, u32[]{:S(2)}) collective-permute-start(bf16[36,128,128]{2,1,0:T(8,128)(2,1)S(1)} %get-tuple-element.25.mine_ref), channel_id=1, source_target_pairs={{0,64},{64,0},{1,65},{65,1},{2,66},{66,2},{3,67},{67,3},{4,68},{68... | collective-permute-start | bytes 3538952 | tf_op jit(solution)/shard_map/ppermute | solution.py:442
  54.8 3.8 %collective-permute-start.2 = (bf16[36,128,128]{2,1,0:T(8,128)(2,1)S(1)}, bf16[36,128,128]{2,1,0:T(8,128)(2,1)S(1)}, u32[]{:S(2)}, u32[]{:S(2)}) collective-permute-start(bf16[36,128,128]{2,1,0:T(8,128)(2,1)S(1)} %get-tuple-element.40), channel_id=1, source_target_pairs={{0,64},{64,0},{1,65},{65,1},{2,66},{66,2},{3,67},{67,3},{4,68},{68... | collective-permute-start | bytes 3538952 | tf_op jit(solution)/shard_map/ppermute | solution.py:442
  59.4 30.5 %copy-start.5 = (s32[128]{0:T(128)S(1)}, s32[128]{0:T(128)}, u32[]{:S(2)}) copy-start(s32[128]{0:T(128)} %param.8) | copy-start | bytes 1540

commit v11 on v10

--- a/solution.py
+++ b/solution.py
@@ -55,21 +55,23 @@
     return block_line, count_line
 
 
-def slots_kernel(place_ref, line_ref):
-    lane = lax.broadcasted_iota(jnp.int32, (block, block), 1).astype(jnp.float32)
-    slots_down = down(place_ref[...] & (block - 1))
-    line = jnp.sum(jnp.where(down(place_ref[...] >> 7) == lane, slots_down, 0.0), axis=0, keepdims=True)
-    line_ref[...] = jnp.broadcast_to(line, (8, block))
-
-
-def pack_kernel(mine_ref, other_ref, place_ref, line_ref, q_ref, kv_ref, g_ref, out_ref, plan_ref):
+def tables_kernel(rows_ref, heads_ref, lane_ref):
+    lane_ref[...] = lax.broadcasted_iota(jnp.int32, (block, block), 1).astype(jnp.float32)
+    for ref, width in ((rows_ref, head_rows), (heads_ref, 8)):
+        chip = lax.broadcasted_iota(jnp.int32, ref.shape, 0) * width
+        lane = lax.broadcasted_iota(jnp.int32, ref.shape, 1)
+        ref[...] = one_hot((lane >= chip) & (lane < chip + width))
+
+
+def pack_kernel(mine_ref, other_ref, place_ref, lane_ref, q_ref, kv_ref, g_ref, out_ref, plan_ref):
     block_line, count_line = make_plan(lax.axis_index("dp"), mine_ref, other_ref)
     row8 = lax.broadcasted_iota(jnp.int32, (8, block), 0)
     plan_ref[...] = jnp.where(row8 == 0, block_line, jnp.where(row8 == 1, count_line, 0.0)).astype(jnp.int32)
     block_down = down(block_line).astype(jnp.int32)
     count_down = down(count_line).astype(jnp.int32)
     rows = place_ref[...] >> 7
-    slot_line = line_ref[0:1]
+    slots_down = down(place_ref[...] & (block - 1))
+    slot_line = jnp.sum(jnp.where(down(rows) == lane_ref[...], slots_down, 0.0), axis=0, keepdims=True)
     extra = jnp.where(row8 == kv_rows % 8, slot_line, 0.0)
     kv = jnp.concatenate([kv_ref[:, :head], kv_ref[:, head:]], axis=0)
     r = lax.broadcasted_iota(jnp.int32, (group, head_rows, block), 1)
@@ -115,14 +117,8 @@
             out_ref[t : t + group, head_rows + 8 :, :] = got[:, head:].reshape(group, 8, head)
 
 
-def spread_lanes(plan, width):
-    chip = lax.broadcasted_iota(jnp.int32, (block, 64 * width), 0) * width
-    lane = lax.broadcasted_iota(jnp.int32, (block, 64 * width), 1)
-    return jnp.dot(plan, one_hot((lane >= chip) & (lane < chip + width)), preferred_element_type=jnp.float32)
-
-
 def unpack_kernel(
-    place_ref, plan_ref, got_ref, out_hbm, dq_hbm, dkv_hbm, out_ref, dq_ref, dkv_ref, sems
+    place_ref, plan_ref, rows_table, heads_table, got_ref, out_hbm, dq_hbm, dkv_hbm, out_ref, dq_ref, dkv_ref, sems
 ):
     moves = [
         pltpu.make_async_copy(src, dst, sems.at[i])
@@ -139,7 +135,7 @@
     for i, line in enumerate(lines):
         stacked = jnp.where((row == i) & (lane[0:1] < 64), line, stacked)
     stacked = stacked.astype(jnp.bfloat16)
-    wide = spread_lanes(stacked, 8)
+    wide = nn(stacked, heads_table[...])
     j = lax.broadcasted_iota(jnp.int32, (1, 512), 1) & 7
     code = jnp.where(j < 4, wide[0:1], wide[2:3])
     rows_wide = jnp.concatenate([rows_down] * 4, axis=1)
@@ -159,7 +155,7 @@
             dq_ref[:, at : at + head] = got[:, head:]
     moves[0].start()
     moves[1].start()
-    wide = spread_lanes(stacked, head_rows)
+    wide = nn(stacked, rows_table[...])
     first, first_count, second, second_count, chip = [wide[i : i + 1] for i in range(5)]
     r = lax.broadcasted_iota(jnp.int32, (1, 64 * head_rows), 1) - head_rows * chip.astype(jnp.int32)
     sums = [jnp.zeros((block, head), jnp.float32), jnp.zeros((block, head), jnp.float32)]
@@ -486,15 +482,19 @@
     bf16, f32 = jnp.bfloat16, jnp.float32
     place = placement.reshape(1, block)
     other_lengths = swap(doc_lengths)
-    line = pl.pallas_call(
-        slots_kernel,
-        out_shape=jax.ShapeDtypeStruct((8, block), f32),
-        in_specs=vmem(1),
-        out_specs=vmem(1)[0],
+    rows_table, heads_table, lanes = pl.pallas_call(
+        tables_kernel,
+        out_shape=(
+            jax.ShapeDtypeStruct((block, 64 * head_rows), bf16),
+            jax.ShapeDtypeStruct((block, 64 * 8), bf16),
+            jax.ShapeDtypeStruct((block, block), f32),
+        ),
+        in_specs=[],
+        out_specs=tuple(vmem(3)),
         compiler_params=params(8),
         cost_estimate=pl.CostEstimate(flops=4 * 10**9, bytes_accessed=0, transcendentals=0),
-        name="slots",
-    )(place)
+        name="tables",
+    )()
     sent, plan = pl.pallas_call(
         pack_kernel,
         out_shape=(
@@ -505,7 +505,7 @@
         out_specs=tuple(vmem(2)),
         compiler_params=params(24),
         name="pack",
-    )(doc_lengths, other_lengths, place, line, queries, keys_values, grad_out)
+    )(doc_lengths, other_lengths, place, lanes, queries, keys_values, grad_out)
     mine, info, qg = pl.pallas_call(
         split_kernel,
         out_shape=(
@@ -535,7 +535,7 @@
             jax.ShapeDtypeStruct((block, 8 * head), bf16),
             jax.ShapeDtypeStruct((block, 2 * head), bf16),
         ),
-        in_specs=vmem(3),
+        in_specs=vmem(5),
         out_specs=tuple([pl.BlockSpec(memory_space=pl.ANY)] * 3),
         scratch_shapes=[
             pltpu.VMEM((block, 8 * head), bf16),
@@ -545,7 +545,7 @@
         ],
         compiler_params=params(24),
         name="unpack",
-    )(place, plan, returned)
+    )(place, plan, rows_table, heads_table, returned)
 
 
 def solution(mesh):

time: 92.7 us -> 91.9 us (level)
  local copies, waits for them, and re-layouts: 1.4 us -> 0.02 us
    unnamed x12 -> x10, local copies, waits for them, and re-layouts: 1.4 us -> 0.02 us
where the time goes in v11:
time: 91.9 us; the launch traced here: 91.8 us
  blocking collectives  67.6 us (74%)
  Pallas kernels  19.4 us (21%)
  starting transfers between devices  3.12 us (3%)
    all_to_all x2, blocking collectives, exchange(): lax.all_to_all(x, ('dp', 'ctx'), split_axis=0, concat_axis=0, tiled=True)  67.6 us
    pallas_call x3, Pallas kernels, kernel(): pl.pallas_call(body, out_shape=tuple((jax.ShapeDtypeStruct(shape, dtype)...  13.4 us
    ppermute x3, starting transfers between devices, swap(): return lax.ppermute(x, 'dp', [(0, 1), (1, 0)])  3.12 us
    pallas_call x1, Pallas kernels, on_device(): pl.pallas_call(pack_kernel, out_shape=(jax.ShapeDtypeStruct((128, send_ro...  2.34 us
    pallas_call x1, Pallas kernels, on_device(): pl.pallas_call(unpack_kernel, out_shape=(jax.ShapeDtypeStruct((block, 8 *...  2.19 us
  transfers between devices with their start and end apart: 3, of which 1 were waited for; matrix products, arithmetic and copies ran while one was open for 0% of the time, Pallas kernels for 7%

profile of v11, /device:TPU:1, one launch (start us, length us, event | category | flops | bytes accessed | tf_op | source)
XLA Modules:
  0.0 91.8 jit_solution(8669471904887633613)
XLA Ops:
  0.6 0.0 copy-start.3
  0.6 0.0 copy-start.4
  0.7 0.0 copy-start.1
  0.7 0.0 copy-start.2
  0.7 0.0 copy-start
  0.7 1.5 %collective-permute-start = (s32[1,16]{1,0:T(1,128)}, s32[1,16]{1,0:T(1,128)S(1)}, u32[]{:S(2)}, u32[]{:S(2)}) collective-permute-start(s32[1,16]{1,0:T(1,128)} %mine_len.1), channel_id=1, source_target_pairs={{0,64},{64,0},{1,65},{65,1},{2,66},{66,2},{3,67},{67,3},{4,68},{68... | collective-permute-start | bytes 200 | tf_op jit(solution)/shard_map/ppermute | solution.py:438
  2.2 0.2 tables.1
  2.4 0.7 collective-permute-done.other_ref.other_len
  3.1 0.0 copy-done.3
  3.1 0.0 copy-done.4
  3.1 0.0 copy-done.1
  3.2 2.3 %pack.1 = (bf16[128,56,128]{2,1,0:T(8,128)(2,1)S(1)}, s32[8,128]{1,0:T(8,128)S(1)}) custom-call(s32[1,16]{1,0:T(1,128)S(1)} %copy-done.3, s32[1,16]{1,0:T(1,128)S(1)} %collective-permute-done.other_ref.other_len, s32[1,128]{1,0:T(1,128)S(1)} %bitcast.1, f32[128,128]{1,0:T(8,128)S(1)} %get-tuple-element.26.lane_ref, bf16[128,1024]{1,0:T(8,128)(2,1)S(1)} %copy-done, ...), custom_call_target="tpu_custom_call" | custom-call | tf_op jit(solution)/shard_map/pack/pallas_call | solution.py:498
  5.5 37.1 %all_to_all.10.got_ref = bf16[128,56,128]{2,1,0:T(8,128)(2,1)S(1)} all-to-all(bf16[128,56,128]{2,1,0:T(8,128)(2,1)S(1)} %get-tuple-element.30), channel_id=1, replica_groups=mesh['dp'=2,'ctx'=64] {'dp','ctx'}, dimensions={0} | all-to-all | bytes 3670016 | tf_op jit(solution)/shard_map/all_to_all | solution.py:442
  42.6 0.5 split.1
  43.1 1.1 %collective-permute-start.1 = (bf16[36,128,128]{2,1,0:T(8,128)(2,1)S(1)}, bf16[36,128,128]{2,1,0:T(8,128)(2,1)S(1)}, u32[]{:S(2)}, u32[]{:S(2)}) collective-permute-start(bf16[36,128,128]{2,1,0:T(8,128)(2,1)S(1)} %get-tuple-element.31.mine_ref), channel_id=1, source_target_pairs={{0,64},{64,0},{1,65},{65,1},{2,66},{66,2},{3,67},{67,3},{4,68},{68... | collective-permute-start | bytes 3538952 | tf_op jit(solution)/shard_map/ppermute | solution.py:438
  44.2 2.5 %scores.1 = (f32[24,128,512]{2,1,0:T(8,128)S(1)}, f32[24,128,512]{2,1,0:T(8,128)S(1)}, f32[8,1024]{1,0:T(8,128)S(1)}, f32[128,128]{1,0:T(8,128)S(1)}, f32[8,128]{1,0:T(8,128)S(1)}) custom-call(s32[1,16]{1,0:T(1,128)S(1)} %copy-done.3, s32[1,16]{1,0:T(1,128)S(1)} %collective-permute-done.other_ref.other_len, s32[8,128]{1,0:T(8,128)S(1)} %get-tuple-element.27.plan_ref, ...), custom_call_target="tpu_custom_call" | custom-call | tf_op jit(solution)/shard_map/scores/pallas_call | solution.py:446
  46.7 0.0 collective-permute-done.1.other_ref
  46.7 7.6 %weights.1 = (bf16[36,128,128]{2,1,0:T(8,128)(2,1)S(1)}, bf16[1024,128]{1,0:T(8,128)(2,1)S(1)}, bf16[24,128,512]{2,1,0:T(8,128)(2,1)S(1)}, f32[8,1024]{1,0:T(8,1...) custom-call(s32[8,128]{1,0:T(8,128)S(1)} %get-tuple-element.27.plan_, ...), custom_call_target="tpu_custom_call" | custom-call | tf_op jit(solution)/shard_map/weights/pallas_call | solution.py:446
  54.4 0.5 collective-permute-start.2
  54.9 3.3 %grads.1 = (bf16[36,128,128]{2,1,0:T(8,128)(2,1)S(1)}, bf16[1024,128]{1,0:T(8,128)(2,1)S(1)}) custom-call(s32[8,128]{1,0:T(8,128)S(1)} %get-tuple-element.27.plan_ref, bf16[36,128,128]{2,1,0:T(8,128)(2,1)S(1)} %get-tuple-element.31.mine_ref, f32[24,128,512]{2,1,0:T(8,128)S(1)} %get-tuple-element.34.gw_ref, ...), custom_call_target="tpu_custom_call" | custom-call | tf_op jit(solution)/shard_map/grads/pallas_call | solution.py:446
  58.2 0.0 collective-permute-done.2.other_ref
  58.2 0.7 join.1
  58.9 30.5 %all_to_all.11.got_ref = bf16[128,56,128]{2,1,0:T(8,128)(2,1)S(1)} all-to-all(bf16[128,56,128]{2,1,0:T(8,128)(2,1)S(1)} %join.1), channel_id=1, replica_groups=mesh['dp'=2,'ctx'=64] {'dp','ctx'}, dimensions={0} | all-to-all | bytes 3670016 | tf_op jit(solution)/shard_map/all_to_all | solution.py:442
  89.4 2.2 %unpack.1 = (bf16[128,1024]{1,0:T(8,128)(2,1)}, bf16[128,1024]{1,0:T(8,128)(2,1)}, bf16[128,256]{1,0:T(8,128)(2,1)}) custom-call(s32[1,128]{1,0:T(1,128)S(1)} %bitcast.2, s32[8,128]{1,0:T(8,128)S(1)} %get-tuple-element.27.plan_ref, bf16[128,2560]{1,0:T(8,128)(2,1)S(1)} %get-tuple-element.28.rows_table, bf16[128,512]{1,0:T(8,128)(2,1)S(1)} %get-tuple-element.29.heads_table, ...), custom_call_target="tpu_custom_call" | custom-call | tf_op jit(solution)/shard_map/unpack/pallas_call | solution.py:531
  (2 shorter events, 0.0 us)
Async XLA Ops:
  0.6 2.5 %copy-start.3 = (s32[1,16]{1,0:T(1,128)S(1)}, s32[1,16]{1,0:T(1,128)}, u32[]{:S(2)}) copy-start(s32[1,16]{1,0:T(1,128)} %mine_len.1) | copy-start | bytes 196
  0.6 2.5 %copy-start.4 = (s32[128]{0:T(128)S(1)}, s32[128]{0:T(128)}, u32[]{:S(2)}) copy-start(s32[128]{0:T(128)} %param.8) | copy-start | bytes 1540
  0.7 2.5 %copy-start.1 = (bf16[128,1024]{1,0:T(8,128)(2,1)S(1)}, bf16[128,1024]{1,0:T(8,128)(2,1)}, u32[]{:S(2)}) copy-start(bf16[128,1024]{1,0:T(8,128)(2,1)} %g_ref.1) | copy-start | bytes 786436
  0.7 2.5 %copy-start.2 = (bf16[128,256]{1,0:T(8,128)(2,1)S(1)}, bf16[128,256]{1,0:T(8,128)(2,1)}, u32[]{:S(2)}) copy-start(bf16[128,256]{1,0:T(8,128)(2,1)} %kv_ref.1) | copy-start | bytes 196612
  0.7 2.5 %copy-start = (bf16[128,1024]{1,0:T(8,128)(2,1)S(1)}, bf16[128,1024]{1,0:T(8,128)(2,1)}, u32[]{:S(2)}) copy-start(bf16[128,1024]{1,0:T(8,128)(2,1)} %q_ref.1) | copy-start | bytes 786436
  0.7 2.5 %collective-permute-start = (s32[1,16]{1,0:T(1,128)}, s32[1,16]{1,0:T(1,128)S(1)}, u32[]{:S(2)}, u32[]{:S(2)}) collective-permute-start(s32[1,16]{1,0:T(1,128)} %mine_len.1), channel_id=1, source_target_pairs={{0,64},{64,0},{1,65},{65,1},{2,66},{66,2},{3,67},{67,3},{4,68},{68... | collective-permute-start | bytes 200 | tf_op jit(solution)/shard_map/ppermute | solution.py:438
  43.1 3.6 %collective-permute-start.1 = (bf16[36,128,128]{2,1,0:T(8,128)(2,1)S(1)}, bf16[36,128,128]{2,1,0:T(8,128)(2,1)S(1)}, u32[]{:S(2)}, u32[]{:S(2)}) collective-permute-start(bf16[36,128,128]{2,1,0:T(8,128)(2,1)S(1)} %get-tuple-element.31.mine_ref), channel_id=1, source_target_pairs={{0,64},{64,0},{1,65},{65,1},{2,66},{66,2},{3,67},{67,3},{4,68},{68... | collective-permute-start | bytes 3538952 | tf_op jit(solution)/shard_map/ppermute | solution.py:438
  54.4 3.8 %collective-permute-start.2 = (bf16[36,128,128]{2,1,0:T(8,128)(2,1)S(1)}, bf16[36,128,128]{2,1,0:T(8,128)(2,1)S(1)}, u32[]{:S(2)}, u32[]{:S(2)}) collective-permute-start(bf16[36,128,128]{2,1,0:T(8,128)(2,1)S(1)} %get-tuple-element.46), channel_id=1, source_target_pairs={{0,64},{64,0},{1,65},{65,1},{2,66},{66,2},{3,67},{67,3},{4,68},{68... | collective-permute-start | bytes 3538952 | tf_op jit(solution)/shard_map/ppermute | solution.py:438

commit v12 on v11

--- a/solution.py
+++ b/solution.py
@@ -158,8 +158,10 @@
     wide = nn(stacked, rows_table[...])
     first, first_count, second, second_count, chip = [wide[i : i + 1] for i in range(5)]
     r = lax.broadcasted_iota(jnp.int32, (1, 64 * head_rows), 1) - head_rows * chip.astype(jnp.int32)
-    sums = [jnp.zeros((block, head), jnp.float32), jnp.zeros((block, head), jnp.float32)]
+    sums = jnp.zeros((block, 2 * head), jnp.float32)
     rows_wide = jnp.concatenate([rows_down] * (64 * head_rows // block), axis=1)
+    row = lax.broadcasted_iota(jnp.int32, (16, head), 0)
+    keys, values = one_hot((row & 1) == 0)[None], one_hot((row & 1) == 1)[None]
     for core in range(2):
         entry = ((r & -2) + core).astype(jnp.float32)
         code = jnp.where(
@@ -168,11 +170,11 @@
             jnp.where(entry >= entries - second_count, entry + (second - (entries - 1)), float(nothing)),
         )
         code = jnp.where(r < kv_rows, code, float(nothing))
-        terms = got_ref[core * 64 : core * 64 + 64, :head_rows, :].reshape(64 * head_rows, head)
-        for half in range(2):
-            pick = one_hot(jnp.where((r & 1) == half, code, float(nothing)) == rows_wide)
-            sums[half] = sums[half] + jnp.dot(pick, terms, preferred_element_type=jnp.float32)
-    dkv_ref[...] = jnp.concatenate(sums, axis=1).astype(jnp.bfloat16)
+        terms = got_ref[core * 64 : core * 64 + 64, :head_rows, :].reshape(4 * head_rows, 16, head)
+        sides = [(terms * side).reshape(64 * head_rows, head) for side in (keys, values)]
+        pick = one_hot(code == rows_wide)
+        sums = sums + jnp.dot(pick, jnp.concatenate(sides, axis=1), preferred_element_type=jnp.float32)
+    dkv_ref[...] = sums.astype(jnp.bfloat16)
     moves[2].start()
     for move in moves:
         move.wait()

time: 91.9 us -> 92 us (level)
  no operation moved by 1% of the time
where the time goes in v12:
time: 92 us; the launch traced here: 91.9 us
  blocking collectives  67.6 us (73%)
  Pallas kernels  19.5 us (21%)
  starting transfers between devices  3.12 us (3%)
    all_to_all x2, blocking collectives, exchange(): lax.all_to_all(x, ('dp', 'ctx'), split_axis=0, concat_axis=0, tiled=True)  67.6 us
    pallas_call x3, Pallas kernels, kernel(): pl.pallas_call(body, out_shape=tuple((jax.ShapeDtypeStruct(shape, dtype)...  13.4 us
    ppermute x3, starting transfers between devices, swap(): return lax.ppermute(x, 'dp', [(0, 1), (1, 0)])  3.12 us
    pallas_call x1, Pallas kernels, on_device(): pl.pallas_call(pack_kernel, out_shape=(jax.ShapeDtypeStruct((128, send_ro...  2.34 us
    pallas_call x1, Pallas kernels, on_device(): pl.pallas_call(unpack_kernel, out_shape=(jax.ShapeDtypeStruct((block, 8 *...  2.28 us
  transfers between devices with their start and end apart: 3, of which 1 were waited for; matrix products, arithmetic and copies ran while one was open for 0% of the time, Pallas kernels for 7%

profile of v12, /device:TPU:1, one launch (start us, length us, event | category | flops | bytes accessed | tf_op | source)
XLA Modules:
  0.0 91.9 jit_solution(7795172065584384482)
XLA Ops:
  0.6 0.0 copy-start.3
  0.6 0.0 copy-start.4
  0.7 0.0 copy-start.1
  0.7 0.0 copy-start.2
  0.7 0.0 copy-start
  0.7 1.5 %collective-permute-start = (s32[1,16]{1,0:T(1,128)}, s32[1,16]{1,0:T(1,128)S(1)}, u32[]{:S(2)}, u32[]{:S(2)}) collective-permute-start(s32[1,16]{1,0:T(1,128)} %mine_len.1), channel_id=1, source_target_pairs={{0,64},{64,0},{1,65},{65,1},{2,66},{66,2},{3,67},{67,3},{4,68},{68... | collective-permute-start | bytes 200 | tf_op jit(solution)/shard_map/ppermute | solution.py:440
  2.2 0.2 tables.1
  2.4 0.7 collective-permute-done.other_ref.other_len
  3.1 0.0 copy-done.3
  3.1 0.0 copy-done.4
  3.1 0.0 copy-done.2
  3.2 2.3 %pack.1 = (bf16[128,56,128]{2,1,0:T(8,128)(2,1)S(1)}, s32[8,128]{1,0:T(8,128)S(1)}) custom-call(s32[1,16]{1,0:T(1,128)S(1)} %copy-done.3, s32[1,16]{1,0:T(1,128)S(1)} %collective-permute-done.other_ref.other_len, s32[1,128]{1,0:T(1,128)S(1)} %bitcast.1, f32[128,128]{1,0:T(8,128)S(1)} %get-tuple-element.26.lane_ref, bf16[128,1024]{1,0:T(8,128)(2,1)S(1)} %copy-done, ...), custom_call_target="tpu_custom_call" | custom-call | tf_op jit(solution)/shard_map/pack/pallas_call | solution.py:500
  5.5 37.1 %all_to_all.10.got_ref = bf16[128,56,128]{2,1,0:T(8,128)(2,1)S(1)} all-to-all(bf16[128,56,128]{2,1,0:T(8,128)(2,1)S(1)} %get-tuple-element.30), channel_id=1, replica_groups=mesh['dp'=2,'ctx'=64] {'dp','ctx'}, dimensions={0} | all-to-all | bytes 3670016 | tf_op jit(solution)/shard_map/all_to_all | solution.py:444
  42.6 0.5 split.1
  43.1 1.1 %collective-permute-start.1 = (bf16[36,128,128]{2,1,0:T(8,128)(2,1)S(1)}, bf16[36,128,128]{2,1,0:T(8,128)(2,1)S(1)}, u32[]{:S(2)}, u32[]{:S(2)}) collective-permute-start(bf16[36,128,128]{2,1,0:T(8,128)(2,1)S(1)} %get-tuple-element.31.mine_ref), channel_id=1, source_target_pairs={{0,64},{64,0},{1,65},{65,1},{2,66},{66,2},{3,67},{67,3},{4,68},{68... | collective-permute-start | bytes 3538952 | tf_op jit(solution)/shard_map/ppermute | solution.py:440
  44.2 2.5 %scores.1 = (f32[24,128,512]{2,1,0:T(8,128)S(1)}, f32[24,128,512]{2,1,0:T(8,128)S(1)}, f32[8,1024]{1,0:T(8,128)S(1)}, f32[128,128]{1,0:T(8,128)S(1)}, f32[8,128]{1,0:T(8,128)S(1)}) custom-call(s32[1,16]{1,0:T(1,128)S(1)} %copy-done.3, s32[1,16]{1,0:T(1,128)S(1)} %collective-permute-done.other_ref.other_len, s32[8,128]{1,0:T(8,128)S(1)} %get-tuple-element.27.plan_ref, ...), custom_call_target="tpu_custom_call" | custom-call | tf_op jit(solution)/shard_map/scores/pallas_call | solution.py:448
  46.7 0.0 collective-permute-done.1.other_ref
  46.7 7.6 %weights.1 = (bf16[36,128,128]{2,1,0:T(8,128)(2,1)S(1)}, bf16[1024,128]{1,0:T(8,128)(2,1)S(1)}, bf16[24,128,512]{2,1,0:T(8,128)(2,1)S(1)}, f32[8,1024]{1,0:T(8,1...) custom-call(s32[8,128]{1,0:T(8,128)S(1)} %get-tuple-element.27.plan_, ...), custom_call_target="tpu_custom_call" | custom-call | tf_op jit(solution)/shard_map/weights/pallas_call | solution.py:448
  54.4 0.5 collective-permute-start.2
  54.9 3.3 %grads.1 = (bf16[36,128,128]{2,1,0:T(8,128)(2,1)S(1)}, bf16[1024,128]{1,0:T(8,128)(2,1)S(1)}) custom-call(s32[8,128]{1,0:T(8,128)S(1)} %get-tuple-element.27.plan_ref, bf16[36,128,128]{2,1,0:T(8,128)(2,1)S(1)} %get-tuple-element.31.mine_ref, f32[24,128,512]{2,1,0:T(8,128)S(1)} %get-tuple-element.34.gw_ref, ...), custom_call_target="tpu_custom_call" | custom-call | tf_op jit(solution)/shard_map/grads/pallas_call | solution.py:448
  58.2 0.0 collective-permute-done.2.other_ref
  58.2 0.7 join.1
  58.9 30.5 %all_to_all.11.got_ref = bf16[128,56,128]{2,1,0:T(8,128)(2,1)S(1)} all-to-all(bf16[128,56,128]{2,1,0:T(8,128)(2,1)S(1)} %join.1), channel_id=1, replica_groups=mesh['dp'=2,'ctx'=64] {'dp','ctx'}, dimensions={0} | all-to-all | bytes 3670016 | tf_op jit(solution)/shard_map/all_to_all | solution.py:444
  89.4 2.3 %unpack.1 = (bf16[128,1024]{1,0:T(8,128)(2,1)}, bf16[128,1024]{1,0:T(8,128)(2,1)}, bf16[128,256]{1,0:T(8,128)(2,1)}) custom-call(s32[1,128]{1,0:T(1,128)S(1)} %bitcast.2, s32[8,128]{1,0:T(8,128)S(1)} %get-tuple-element.27.plan_ref, bf16[128,2560]{1,0:T(8,128)(2,1)S(1)} %get-tuple-element.28.rows_table, bf16[128,512]{1,0:T(8,128)(2,1)S(1)} %get-tuple-element.29.heads_table, ...), custom_call_target="tpu_custom_call" | custom-call | tf_op jit(solution)/shard_map/unpack/pallas_call | solution.py:533
  (2 shorter events, 0.0 us)
Async XLA Ops:
  0.6 2.5 %copy-start.3 = (s32[1,16]{1,0:T(1,128)S(1)}, s32[1,16]{1,0:T(1,128)}, u32[]{:S(2)}) copy-start(s32[1,16]{1,0:T(1,128)} %mine_len.1) | copy-start | bytes 196
  0.6 2.5 %copy-start.4 = (s32[128]{0:T(128)S(1)}, s32[128]{0:T(128)}, u32[]{:S(2)}) copy-start(s32[128]{0:T(128)} %param.8) | copy-start | bytes 1540
  0.7 2.5 %copy-start.1 = (bf16[128,1024]{1,0:T(8,128)(2,1)S(1)}, bf16[128,1024]{1,0:T(8,128)(2,1)}, u32[]{:S(2)}) copy-start(bf16[128,1024]{1,0:T(8,128)(2,1)} %g_ref.1) | copy-start | bytes 786436
  0.7 2.5 %copy-start.2 = (bf16[128,256]{1,0:T(8,128)(2,1)S(1)}, bf16[128,256]{1,0:T(8,128)(2,1)}, u32[]{:S(2)}) copy-start(bf16[128,256]{1,0:T(8,128)(2,1)} %kv_ref.1) | copy-start | bytes 196612
  0.7 2.5 %copy-start = (bf16[128,1024]{1,0:T(8,128)(2,1)S(1)}, bf16[128,1024]{1,0:T(8,128)(2,1)}, u32[]{:S(2)}) copy-start(bf16[128,1024]{1,0:T(8,128)(2,1)} %q_ref.1) | copy-start | bytes 786436
  0.7 2.5 %collective-permute-start = (s32[1,16]{1,0:T(1,128)}, s32[1,16]{1,0:T(1,128)S(1)}, u32[]{:S(2)}, u32[]{:S(2)}) collective-permute-start(s32[1,16]{1,0:T(1,128)} %mine_len.1), channel_id=1, source_target_pairs={{0,64},{64,0},{1,65},{65,1},{2,66},{66,2},{3,67},{67,3},{4,68},{68... | collective-permute-start | bytes 200 | tf_op jit(solution)/shard_map/ppermute | solution.py:440
  43.1 3.6 %collective-permute-start.1 = (bf16[36,128,128]{2,1,0:T(8,128)(2,1)S(1)}, bf16[36,128,128]{2,1,0:T(8,128)(2,1)S(1)}, u32[]{:S(2)}, u32[]{:S(2)}) collective-permute-start(bf16[36,128,128]{2,1,0:T(8,128)(2,1)S(1)} %get-tuple-element.31.mine_ref), channel_id=1, source_target_pairs={{0,64},{64,0},{1,65},{65,1},{2,66},{66,2},{3,67},{67,3},{4,68},{68... | collective-permute-start | bytes 3538952 | tf_op jit(solution)/shard_map/ppermute | solution.py:440
  54.4 3.8 %collective-permute-start.2 = (bf16[36,128,128]{2,1,0:T(8,128)(2,1)S(1)}, bf16[36,128,128]{2,1,0:T(8,128)(2,1)S(1)}, u32[]{:S(2)}, u32[]{:S(2)}) collective-permute-start(bf16[36,128,128]{2,1,0:T(8,128)(2,1)S(1)} %get-tuple-element.46), channel_id=1, source_target_pairs={{0,64},{64,0},{1,65},{65,1},{2,66},{66,2},{3,67},{67,3},{4,68},{68... | collective-permute-start | bytes 3538952 | tf_op jit(solution)/shard_map/ppermute | solution.py:440

commit v13 on v11

--- a/solution.py
+++ b/solution.py
@@ -13,7 +13,6 @@
 head_rows = 40
 send_rows = 56
 group = 16
-other_half = 1000
 nothing = -100000
 masked_score = -1e30
 far = 1e9
@@ -73,9 +72,9 @@
     slots_down = down(place_ref[...] & (block - 1))
     slot_line = jnp.sum(jnp.where(down(rows) == lane_ref[...], slots_down, 0.0), axis=0, keepdims=True)
     extra = jnp.where(row8 == kv_rows % 8, slot_line, 0.0)
-    kv = jnp.concatenate([kv_ref[:, :head], kv_ref[:, head:]], axis=0)
+    kv = kv_ref[...]
     r = lax.broadcasted_iota(jnp.int32, (group, head_rows, block), 1)
-    half = (r & 1) * other_half
+    odd = (r & 1) == 1
     j = lax.broadcasted_iota(jnp.int32, (group, 8, block), 1)
     both = []
     for core in range(2):
@@ -106,9 +105,11 @@
                     nothing,
                 ),
             )
-            code = (jnp.where(r < kv_rows, code, nothing) + half).reshape(group * head_rows, block)
-            pick = jnp.concatenate([one_hot(code == rows), one_hot(code == rows + other_half)], axis=1)
-            got = jnp.dot(pick, kv, preferred_element_type=jnp.float32).reshape(group, head_rows, head)
+            code = jnp.where(r < kv_rows, code, nothing).reshape(group * head_rows, block)
+            pick = one_hot(code == rows)
+            got = jnp.dot(pick, kv, preferred_element_type=jnp.float32)
+            sides = [got[:, at : at + head].reshape(group, head_rows, head) for at in (0, head)]
+            got = jnp.where(odd, sides[1], sides[0])
             tail = got[:, head_rows - 8 :, :] + extra[None]
             got = jnp.concatenate([got[:, : head_rows - 8, :], tail], axis=1)
             out_ref[t : t + group, :head_rows, :] = got.astype(jnp.bfloat16)

time: 91.9 us -> 91.8 us (level)
  no operation moved by 1% of the time
where the time goes in v13:
time: 91.8 us; the launch traced here: 91.7 us
  blocking collectives  67.6 us (74%)
  Pallas kernels  19.5 us (21%)
  starting transfers between devices  2.93 us (3%)
    all_to_all x2, blocking collectives, exchange(): lax.all_to_all(x, ('dp', 'ctx'), split_axis=0, concat_axis=0, tiled=True)  67.6 us
    pallas_call x3, Pallas kernels, kernel(): pl.pallas_call(body, out_shape=tuple((jax.ShapeDtypeStruct(shape, dtype)...  13.6 us
    ppermute x3, starting transfers between devices, swap(): return lax.ppermute(x, 'dp', [(0, 1), (1, 0)])  2.93 us
    pallas_call x1, Pallas kernels, on_device(): pl.pallas_call(pack_kernel, out_shape=(jax.ShapeDtypeStruct((128, send_ro...  2.23 us
    pallas_call x1, Pallas kernels, on_device(): pl.pallas_call(unpack_kernel, out_shape=(jax.ShapeDtypeStruct((block, 8 *...  2.18 us
  transfers between devices with their start and end apart: 3, of which 1 were waited for; matrix products, arithmetic and copies ran while one was open for 0% of the time, Pallas kernels for 7%

profile of v13, /device:TPU:1, one launch (start us, length us, event | category | flops | bytes accessed | tf_op | source)
XLA Modules:
  0.0 91.7 jit_solution(16489143834839947569)
XLA Ops:
  0.6 0.0 copy-start.3
  0.6 0.0 copy-start.4
  0.7 0.0 copy-start.1
  0.7 0.0 copy-start.2
  0.7 0.0 copy-start
  0.7 1.5 %collective-permute-start = (s32[1,16]{1,0:T(1,128)}, s32[1,16]{1,0:T(1,128)S(1)}, u32[]{:S(2)}, u32[]{:S(2)}) collective-permute-start(s32[1,16]{1,0:T(1,128)} %mine_len.1), channel_id=1, source_target_pairs={{0,64},{64,0},{1,65},{65,1},{2,66},{66,2},{3,67},{67,3},{4,68},{68... | collective-permute-start | bytes 200 | tf_op jit(solution)/shard_map/ppermute | solution.py:439
  2.2 0.2 tables.1
  2.4 0.7 collective-permute-done.other_ref.other_len
  3.1 0.0 copy-done.3
  3.1 0.0 copy-done.4
  3.1 0.0 copy-done.1
  3.2 2.2 %pack.1 = (bf16[128,56,128]{2,1,0:T(8,128)(2,1)S(1)}, s32[8,128]{1,0:T(8,128)S(1)}) custom-call(s32[1,16]{1,0:T(1,128)S(1)} %copy-done.3, s32[1,16]{1,0:T(1,128)S(1)} %collective-permute-done.other_ref.other_len, s32[1,128]{1,0:T(1,128)S(1)} %bitcast.1, f32[128,128]{1,0:T(8,128)S(1)} %get-tuple-element.26.lane_ref, bf16[128,1024]{1,0:T(8,128)(2,1)S(1)} %copy-done, ...), custom_call_target="tpu_custom_call" | custom-call | tf_op jit(solution)/shard_map/pack/pallas_call | solution.py:499
  5.4 37.1 %all_to_all.10.got_ref = bf16[128,56,128]{2,1,0:T(8,128)(2,1)S(1)} all-to-all(bf16[128,56,128]{2,1,0:T(8,128)(2,1)S(1)} %get-tuple-element.30), channel_id=1, replica_groups=mesh['dp'=2,'ctx'=64] {'dp','ctx'}, dimensions={0} | all-to-all | bytes 3670016 | tf_op jit(solution)/shard_map/all_to_all | solution.py:443
  42.5 0.5 split.1
  43.0 1.1 %collective-permute-start.1 = (bf16[36,128,128]{2,1,0:T(8,128)(2,1)S(1)}, bf16[36,128,128]{2,1,0:T(8,128)(2,1)S(1)}, u32[]{:S(2)}, u32[]{:S(2)}) collective-permute-start(bf16[36,128,128]{2,1,0:T(8,128)(2,1)S(1)} %get-tuple-element.31.mine_ref), channel_id=1, source_target_pairs={{0,64},{64,0},{1,65},{65,1},{2,66},{66,2},{3,67},{67,3},{4,68},{68... | collective-permute-start | bytes 3538952 | tf_op jit(solution)/shard_map/ppermute | solution.py:439
  44.1 2.5 %scores.1 = (f32[24,128,512]{2,1,0:T(8,128)S(1)}, f32[24,128,512]{2,1,0:T(8,128)S(1)}, f32[8,1024]{1,0:T(8,128)S(1)}, f32[128,128]{1,0:T(8,128)S(1)}, f32[8,128]{1,0:T(8,128)S(1)}) custom-call(s32[1,16]{1,0:T(1,128)S(1)} %copy-done.3, s32[1,16]{1,0:T(1,128)S(1)} %collective-permute-done.other_ref.other_len, s32[8,128]{1,0:T(8,128)S(1)} %get-tuple-element.27.plan_ref, ...), custom_call_target="tpu_custom_call" | custom-call | tf_op jit(solution)/shard_map/scores/pallas_call | solution.py:447
  46.6 0.0 collective-permute-done.1.other_ref
  46.6 7.6 %weights.1 = (bf16[36,128,128]{2,1,0:T(8,128)(2,1)S(1)}, bf16[1024,128]{1,0:T(8,128)(2,1)S(1)}, bf16[24,128,512]{2,1,0:T(8,128)(2,1)S(1)}, f32[8,1024]{1,0:T(8,1...) custom-call(s32[8,128]{1,0:T(8,128)S(1)} %get-tuple-element.27.plan_, ...), custom_call_target="tpu_custom_call" | custom-call | tf_op jit(solution)/shard_map/weights/pallas_call | solution.py:447
  54.3 0.4 collective-permute-start.2
  54.6 3.4 %grads.1 = (bf16[36,128,128]{2,1,0:T(8,128)(2,1)S(1)}, bf16[1024,128]{1,0:T(8,128)(2,1)S(1)}) custom-call(s32[8,128]{1,0:T(8,128)S(1)} %get-tuple-element.27.plan_ref, bf16[36,128,128]{2,1,0:T(8,128)(2,1)S(1)} %get-tuple-element.31.mine_ref, f32[24,128,512]{2,1,0:T(8,128)S(1)} %get-tuple-element.34.gw_ref, ...), custom_call_target="tpu_custom_call" | custom-call | tf_op jit(solution)/shard_map/grads/pallas_call | solution.py:447
  58.1 0.0 collective-permute-done.2.other_ref
  58.1 0.7 join.1
  58.8 30.5 %all_to_all.11.got_ref = bf16[128,56,128]{2,1,0:T(8,128)(2,1)S(1)} all-to-all(bf16[128,56,128]{2,1,0:T(8,128)(2,1)S(1)} %join.1), channel_id=1, replica_groups=mesh['dp'=2,'ctx'=64] {'dp','ctx'}, dimensions={0} | all-to-all | bytes 3670016 | tf_op jit(solution)/shard_map/all_to_all | solution.py:443
  89.3 2.2 %unpack.1 = (bf16[128,1024]{1,0:T(8,128)(2,1)}, bf16[128,1024]{1,0:T(8,128)(2,1)}, bf16[128,256]{1,0:T(8,128)(2,1)}) custom-call(s32[1,128]{1,0:T(1,128)S(1)} %bitcast.2, s32[8,128]{1,0:T(8,128)S(1)} %get-tuple-element.27.plan_ref, bf16[128,2560]{1,0:T(8,128)(2,1)S(1)} %get-tuple-element.28.rows_table, bf16[128,512]{1,0:T(8,128)(2,1)S(1)} %get-tuple-element.29.heads_table, ...), custom_call_target="tpu_custom_call" | custom-call | tf_op jit(solution)/shard_map/unpack/pallas_call | solution.py:532
  (2 shorter events, 0.0 us)
Async XLA Ops:
  0.6 2.5 %copy-start.3 = (s32[1,16]{1,0:T(1,128)S(1)}, s32[1,16]{1,0:T(1,128)}, u32[]{:S(2)}) copy-start(s32[1,16]{1,0:T(1,128)} %mine_len.1) | copy-start | bytes 196
  0.6 2.5 %copy-start.4 = (s32[128]{0:T(128)S(1)}, s32[128]{0:T(128)}, u32[]{:S(2)}) copy-start(s32[128]{0:T(128)} %param.8) | copy-start | bytes 1540
  0.7 2.5 %copy-start.1 = (bf16[128,1024]{1,0:T(8,128)(2,1)S(1)}, bf16[128,1024]{1,0:T(8,128)(2,1)}, u32[]{:S(2)}) copy-start(bf16[128,1024]{1,0:T(8,128)(2,1)} %g_ref.1) | copy-start | bytes 786436
  0.7 2.5 %copy-start.2 = (bf16[128,256]{1,0:T(8,128)(2,1)S(1)}, bf16[128,256]{1,0:T(8,128)(2,1)}, u32[]{:S(2)}) copy-start(bf16[128,256]{1,0:T(8,128)(2,1)} %kv_ref.1) | copy-start | bytes 196612
  0.7 2.5 %copy-start = (bf16[128,1024]{1,0:T(8,128)(2,1)S(1)}, bf16[128,1024]{1,0:T(8,128)(2,1)}, u32[]{:S(2)}) copy-start(bf16[128,1024]{1,0:T(8,128)(2,1)} %q_ref.1) | copy-start | bytes 786436
  0.7 2.5 %collective-permute-start = (s32[1,16]{1,0:T(1,128)}, s32[1,16]{1,0:T(1,128)S(1)}, u32[]{:S(2)}, u32[]{:S(2)}) collective-permute-start(s32[1,16]{1,0:T(1,128)} %mine_len.1), channel_id=1, source_target_pairs={{0,64},{64,0},{1,65},{65,1},{2,66},{66,2},{3,67},{67,3},{4,68},{68... | collective-permute-start | bytes 200 | tf_op jit(solution)/shard_map/ppermute | solution.py:439
  43.0 3.6 %collective-permute-start.1 = (bf16[36,128,128]{2,1,0:T(8,128)(2,1)S(1)}, bf16[36,128,128]{2,1,0:T(8,128)(2,1)S(1)}, u32[]{:S(2)}, u32[]{:S(2)}) collective-permute-start(bf16[36,128,128]{2,1,0:T(8,128)(2,1)S(1)} %get-tuple-element.31.mine_ref), channel_id=1, source_target_pairs={{0,64},{64,0},{1,65},{65,1},{2,66},{66,2},{3,67},{67,3},{4,68},{68... | collective-permute-start | bytes 3538952 | tf_op jit(solution)/shard_map/ppermute | solution.py:439
  54.3 3.8 %collective-permute-start.2 = (bf16[36,128,128]{2,1,0:T(8,128)(2,1)S(1)}, bf16[36,128,128]{2,1,0:T(8,128)(2,1)S(1)}, u32[]{:S(2)}, u32[]{:S(2)}) collective-permute-start(bf16[36,128,128]{2,1,0:T(8,128)(2,1)S(1)} %get-tuple-element.46), channel_id=1, source_target_pairs={{0,64},{64,0},{1,65},{65,1},{2,66},{66,2},{3,67},{67,3},{4,68},{68... | collective-permute-start | bytes 3538952 | tf_op jit(solution)/shard_map/ppermute | solution.py:439

commit v14 on v13

--- a/solution.py
+++ b/solution.py
@@ -75,6 +75,8 @@
     kv = kv_ref[...]
     r = lax.broadcasted_iota(jnp.int32, (group, head_rows, block), 1)
     odd = (r & 1) == 1
+    early = [jnp.where(r < kv_rows, (r & -2) + core, -nothing) for core in range(2)]
+    late = [jnp.where(r < kv_rows, (r & -2) + core, nothing) for core in range(2)]
     j = lax.broadcasted_iota(jnp.int32, (group, 8, block), 1)
     both = []
     for core in range(2):
@@ -95,17 +97,16 @@
         )
         for core in range(2):
             t = core * 64 + chip
-            entry = (r & -2) + core
             code = jnp.where(
-                entry < spread(first_count, head_rows),
-                entry + spread(first - first_count + 1, head_rows),
+                early[core] < spread(first_count, head_rows),
+                early[core] + spread(first - first_count + 1, head_rows),
                 jnp.where(
-                    entry >= spread(entries - second_count, head_rows),
-                    entry + spread(second - (entries - 1), head_rows),
+                    late[core] >= spread(entries - second_count, head_rows),
+                    late[core] + spread(second - (entries - 1), head_rows),
                     nothing,
                 ),
             )
-            code = jnp.where(r < kv_rows, code, nothing).reshape(group * head_rows, block)
+            code = code.reshape(group * head_rows, block)
             pick = one_hot(code == rows)
             got = jnp.dot(pick, kv, preferred_element_type=jnp.float32)
             sides = [got[:, at : at + head].reshape(group, head_rows, head) for at in (0, head)]

time: 91.8 us -> 91.8 us (level)
  no operation moved by 1% of the time
where the time goes in v14:
time: 91.8 us; the launch traced here: 91.6 us
  blocking collectives  67.6 us (74%)
  Pallas kernels  19.4 us (21%)
  starting transfers between devices  2.93 us (3%)
    all_to_all x2, blocking collectives, exchange(): lax.all_to_all(x, ('dp', 'ctx'), split_axis=0, concat_axis=0, tiled=True)  67.6 us
    pallas_call x3, Pallas kernels, kernel(): pl.pallas_call(body, out_shape=tuple((jax.ShapeDtypeStruct(shape, dtype)...  13.6 us
    ppermute x3, starting transfers between devices, swap(): return lax.ppermute(x, 'dp', [(0, 1), (1, 0)])  2.93 us
    pallas_call x1, Pallas kernels, on_device(): pl.pallas_call(pack_kernel, out_shape=(jax.ShapeDtypeStruct((128, send_ro...  2.18 us
    pallas_call x1, Pallas kernels, on_device(): pl.pallas_call(unpack_kernel, out_shape=(jax.ShapeDtypeStruct((block, 8 *...  2.18 us
  transfers between devices with their start and end apart: 3, of which 1 were waited for; matrix products, arithmetic and copies ran while one was open for 0% of the time, Pallas kernels for 7%

profile of v14, /device:TPU:1, one launch (start us, length us, event | category | flops | bytes accessed | tf_op | source)
XLA Modules:
  0.0 91.6 jit_solution(12288653913943983573)
XLA Ops:
  0.6 0.0 copy-start.3
  0.6 0.0 copy-start.4
  0.7 0.0 copy-start.1
  0.7 0.0 copy-start.2
  0.7 0.0 copy-start
  0.7 1.5 %collective-permute-start = (s32[1,16]{1,0:T(1,128)}, s32[1,16]{1,0:T(1,128)S(1)}, u32[]{:S(2)}, u32[]{:S(2)}) collective-permute-start(s32[1,16]{1,0:T(1,128)} %mine_len.1), channel_id=1, source_target_pairs={{0,64},{64,0},{1,65},{65,1},{2,66},{66,2},{3,67},{67,3},{4,68},{68... | collective-permute-start | bytes 200 | tf_op jit(solution)/shard_map/ppermute | solution.py:440
  2.2 0.2 tables.1
  2.4 0.7 collective-permute-done.other_ref.other_len
  3.1 0.0 copy-done.3
  3.1 0.0 copy-done.4
  3.1 0.0 copy-done.1
  3.2 2.2 %pack.1 = (bf16[128,56,128]{2,1,0:T(8,128)(2,1)S(1)}, s32[8,128]{1,0:T(8,128)S(1)}) custom-call(s32[1,16]{1,0:T(1,128)S(1)} %copy-done.3, s32[1,16]{1,0:T(1,128)S(1)} %collective-permute-done.other_ref.other_len, s32[1,128]{1,0:T(1,128)S(1)} %bitcast.1, f32[128,128]{1,0:T(8,128)S(1)} %get-tuple-element.26.lane_ref, bf16[128,1024]{1,0:T(8,128)(2,1)S(1)} %copy-done, ...), custom_call_target="tpu_custom_call" | custom-call | tf_op jit(solution)/shard_map/pack/pallas_call | solution.py:500
  5.4 37.1 %all_to_all.10.got_ref = bf16[128,56,128]{2,1,0:T(8,128)(2,1)S(1)} all-to-all(bf16[128,56,128]{2,1,0:T(8,128)(2,1)S(1)} %get-tuple-element.30), channel_id=1, replica_groups=mesh['dp'=2,'ctx'=64] {'dp','ctx'}, dimensions={0} | all-to-all | bytes 3670016 | tf_op jit(solution)/shard_map/all_to_all | solution.py:444
  42.4 0.5 split.1
  42.9 1.1 %collective-permute-start.1 = (bf16[36,128,128]{2,1,0:T(8,128)(2,1)S(1)}, bf16[36,128,128]{2,1,0:T(8,128)(2,1)S(1)}, u32[]{:S(2)}, u32[]{:S(2)}) collective-permute-start(bf16[36,128,128]{2,1,0:T(8,128)(2,1)S(1)} %get-tuple-element.31.mine_ref), channel_id=1, source_target_pairs={{0,64},{64,0},{1,65},{65,1},{2,66},{66,2},{3,67},{67,3},{4,68},{68... | collective-permute-start | bytes 3538952 | tf_op jit(solution)/shard_map/ppermute | solution.py:440
  44.0 2.5 %scores.1 = (f32[24,128,512]{2,1,0:T(8,128)S(1)}, f32[24,128,512]{2,1,0:T(8,128)S(1)}, f32[8,1024]{1,0:T(8,128)S(1)}, f32[128,128]{1,0:T(8,128)S(1)}, f32[8,128]{1,0:T(8,128)S(1)}) custom-call(s32[1,16]{1,0:T(1,128)S(1)} %copy-done.3, s32[1,16]{1,0:T(1,128)S(1)} %collective-permute-done.other_ref.other_len, s32[8,128]{1,0:T(8,128)S(1)} %get-tuple-element.27.plan_ref, ...), custom_call_target="tpu_custom_call" | custom-call | tf_op jit(solution)/shard_map/scores/pallas_call | solution.py:448
  46.6 0.0 collective-permute-done.1.other_ref
  46.6 7.6 %weights.1 = (bf16[36,128,128]{2,1,0:T(8,128)(2,1)S(1)}, bf16[1024,128]{1,0:T(8,128)(2,1)S(1)}, bf16[24,128,512]{2,1,0:T(8,128)(2,1)S(1)}, f32[8,1024]{1,0:T(8,1...) custom-call(s32[8,128]{1,0:T(8,128)S(1)} %get-tuple-element.27.plan_, ...), custom_call_target="tpu_custom_call" | custom-call | tf_op jit(solution)/shard_map/weights/pallas_call | solution.py:448
  54.2 0.4 collective-permute-start.2
  54.6 3.4 %grads.1 = (bf16[36,128,128]{2,1,0:T(8,128)(2,1)S(1)}, bf16[1024,128]{1,0:T(8,128)(2,1)S(1)}) custom-call(s32[8,128]{1,0:T(8,128)S(1)} %get-tuple-element.27.plan_ref, bf16[36,128,128]{2,1,0:T(8,128)(2,1)S(1)} %get-tuple-element.31.mine_ref, f32[24,128,512]{2,1,0:T(8,128)S(1)} %get-tuple-element.34.gw_ref, ...), custom_call_target="tpu_custom_call" | custom-call | tf_op jit(solution)/shard_map/grads/pallas_call | solution.py:448
  58.0 0.0 collective-permute-done.2.other_ref
  58.0 0.7 join.1
  58.8 30.5 %all_to_all.11.got_ref = bf16[128,56,128]{2,1,0:T(8,128)(2,1)S(1)} all-to-all(bf16[128,56,128]{2,1,0:T(8,128)(2,1)S(1)} %join.1), channel_id=1, replica_groups=mesh['dp'=2,'ctx'=64] {'dp','ctx'}, dimensions={0} | all-to-all | bytes 3670016 | tf_op jit(solution)/shard_map/all_to_all | solution.py:444
  89.3 2.2 %unpack.1 = (bf16[128,1024]{1,0:T(8,128)(2,1)}, bf16[128,1024]{1,0:T(8,128)(2,1)}, bf16[128,256]{1,0:T(8,128)(2,1)}) custom-call(s32[1,128]{1,0:T(1,128)S(1)} %bitcast.2, s32[8,128]{1,0:T(8,128)S(1)} %get-tuple-element.27.plan_ref, bf16[128,2560]{1,0:T(8,128)(2,1)S(1)} %get-tuple-element.28.rows_table, bf16[128,512]{1,0:T(8,128)(2,1)S(1)} %get-tuple-element.29.heads_table, ...), custom_call_target="tpu_custom_call" | custom-call | tf_op jit(solution)/shard_map/unpack/pallas_call | solution.py:533
  (2 shorter events, 0.0 us)
Async XLA Ops:
  0.6 2.5 %copy-start.3 = (s32[1,16]{1,0:T(1,128)S(1)}, s32[1,16]{1,0:T(1,128)}, u32[]{:S(2)}) copy-start(s32[1,16]{1,0:T(1,128)} %mine_len.1) | copy-start | bytes 196
  0.6 2.5 %copy-start.4 = (s32[128]{0:T(128)S(1)}, s32[128]{0:T(128)}, u32[]{:S(2)}) copy-start(s32[128]{0:T(128)} %param.8) | copy-start | bytes 1540
  0.7 2.5 %copy-start.1 = (bf16[128,1024]{1,0:T(8,128)(2,1)S(1)}, bf16[128,1024]{1,0:T(8,128)(2,1)}, u32[]{:S(2)}) copy-start(bf16[128,1024]{1,0:T(8,128)(2,1)} %g_ref.1) | copy-start | bytes 786436
  0.7 2.5 %copy-start.2 = (bf16[128,256]{1,0:T(8,128)(2,1)S(1)}, bf16[128,256]{1,0:T(8,128)(2,1)}, u32[]{:S(2)}) copy-start(bf16[128,256]{1,0:T(8,128)(2,1)} %kv_ref.1) | copy-start | bytes 196612
  0.7 2.5 %copy-start = (bf16[128,1024]{1,0:T(8,128)(2,1)S(1)}, bf16[128,1024]{1,0:T(8,128)(2,1)}, u32[]{:S(2)}) copy-start(bf16[128,1024]{1,0:T(8,128)(2,1)} %q_ref.1) | copy-start | bytes 786436
  0.7 2.5 %collective-permute-start = (s32[1,16]{1,0:T(1,128)}, s32[1,16]{1,0:T(1,128)S(1)}, u32[]{:S(2)}, u32[]{:S(2)}) collective-permute-start(s32[1,16]{1,0:T(1,128)} %mine_len.1), channel_id=1, source_target_pairs={{0,64},{64,0},{1,65},{65,1},{2,66},{66,2},{3,67},{67,3},{4,68},{68... | collective-permute-start | bytes 200 | tf_op jit(solution)/shard_map/ppermute | solution.py:440
  42.9 3.6 %collective-permute-start.1 = (bf16[36,128,128]{2,1,0:T(8,128)(2,1)S(1)}, bf16[36,128,128]{2,1,0:T(8,128)(2,1)S(1)}, u32[]{:S(2)}, u32[]{:S(2)}) collective-permute-start(bf16[36,128,128]{2,1,0:T(8,128)(2,1)S(1)} %get-tuple-element.31.mine_ref), channel_id=1, source_target_pairs={{0,64},{64,0},{1,65},{65,1},{2,66},{66,2},{3,67},{67,3},{4,68},{68... | collective-permute-start | bytes 3538952 | tf_op jit(solution)/shard_map/ppermute | solution.py:440
  54.2 3.8 %collective-permute-start.2 = (bf16[36,128,128]{2,1,0:T(8,128)(2,1)S(1)}, bf16[36,128,128]{2,1,0:T(8,128)(2,1)S(1)}, u32[]{:S(2)}, u32[]{:S(2)}) collective-permute-start(bf16[36,128,128]{2,1,0:T(8,128)(2,1)S(1)} %get-tuple-element.46), channel_id=1, source_target_pairs={{0,64},{64,0},{1,65},{65,1},{2,66},{66,2},{3,67},{67,3},{4,68},{68... | collective-permute-start | bytes 3538952 | tf_op jit(solution)/shard_map/ppermute | solution.py:440
